TPU v7x, 32 devices: a whole 2x2x4 slice. The times are simulated.
32 devices in a mesh: seq: 16 (over z, x, core), head: 2 (over y).
Axes of the slice: x: 2, y: 2, z: 4, core: 2. Of those that a mesh axis runs over, the one named last changes fastest.
Arguments:
- queries: bfloat16 [4096, 8192], P('seq', 'head'), may hold values from -200 to 200
- layer_key_rows: bfloat16 [4096, 1024], P('seq', 'head'), may hold values from -7 to 7
- layer_value_rows: bfloat16 [4096, 1024], P('seq', 'head'), may hold values from -6 to 6
- output_gradient: bfloat16 [4096, 8192], P('seq', 'head'), may hold values from -24 to 24
- output_row_sums: float32 [64, 4096], P('head', 'seq'), may hold values from -72 to 72
- shifted_head_flags: int32 [64], P('head'), may hold values from 0 to 1, as said below
- inputs: bfloat16 [4096, 8192], P('seq', 'head'), may hold values from -6 to 6
- adapter_down_weight: bfloat16 [3, 16, 8192], P(None, None, 'head'), may hold values from -0.0625 to 0.0625
- query_up_weight: bfloat16 [16, 8192], P(None, 'head'), may hold values from -0.75 to 0.75
- key_value_up_weight: bfloat16 [2, 16, 1024], P(None, None, 'head'), may hold values from -0.75 to 0.75
Outputs:
- grad_inputs: bfloat16 [4096, 8192], P('seq', 'head')
- key_value_gradient: bfloat16 [2, 4096, 1024], P(None, 'seq', 'head')
- down_gradient: float32 [3, 16, 8192], P(None, None, 'head')
- grad_up_q: float32 [16, 8192], P(None, 'head')
- grad_up_kv: float32 [2, 16, 1024], P(None, None, 'head')
Inputs may be any that keep to these rules, and one draw needn't show every extreme that they name: `shifted_head_flags`: exactly half of the 64 heads have 1.
All inputs are finite; a program needn't handle non-finite values.
Results may differ from a plain program's by a relative error of at most 0.013.
Values may be sent and summed in bfloat16 or wider, within the bound.
No kernel may reach another device: no remote copies, remote signals or barrier semaphores. Data moves between devices by JAX's collectives and lax.ppermute only.
A program may use at most 128 MiB of HBM per device.

v0:
```python
import functools
import math

import jax
import jax.numpy as jnp
from jax import lax
from jax.experimental import pallas as pl
from jax.experimental.pallas import tpu as pltpu
from jax.sharding import PartitionSpec as P

HEAD_SIZE = 128
GROUP = 1024
SHIFT = 512
CHUNK = 32
SMALL_VMEM = 8 * 1024 * 1024
VMEM_LIMIT = 32 * 1024 * 1024

adapter_scale = 2.0
masked_score = -1e30
score_scale = HEAD_SIZE ** (-0.5)
exp2_scale = score_scale * math.log2(math.e)

NT = (((1,), (1,)), ((), ()))
NN = (((1,), (0,)), ((), ()))


def mm(left, right, dims=NN):
    return lax.dot_general(left, right, dims, preferred_element_type=jnp.float32)


def scores_and_softmax(head, low, diag, keys, values, q_ref, do_ref, term_ref, slot):
    tokens = q_ref.shape[0]
    s_ref, e_ref, ds_ref, inv_ref = slot
    group, column, key_column = head
    query = q_ref[:, column]
    grad = do_ref[:, column]
    term = term_ref[pl.ds(group[0], 1), :]
    top = None
    for block in range(low, len(keys)):
        rows = slice(block * tokens, (block + 1) * tokens)
        scores = mm(keys[block][:, key_column], query, NT)
        if block == diag:
            key_row = lax.broadcasted_iota(jnp.int32, (tokens, tokens), 0)
            query_row = lax.broadcasted_iota(jnp.int32, (tokens, tokens), 1)
            scores = jnp.where(key_row <= query_row, scores, masked_score)
        s_ref[rows, :] = scores
        here = jnp.max(scores.reshape(tokens // 8, 8, tokens), axis=0)
        top = here if top is None else jnp.maximum(top, here)
    top = jnp.max(top, axis=0, keepdims=True)
    total = jnp.zeros((8, tokens), jnp.float32)
    for block in range(low, len(keys)):
        grad_probs = mm(values[block][:, key_column], grad, NT)
        for at in range(0, tokens, CHUNK):
            rows = slice(block * tokens + at, block * tokens + at + CHUNK)
            weights = jnp.exp2((s_ref[rows, :] - top) * exp2_scale)
            total = total + jnp.sum(weights.reshape(CHUNK // 8, 8, tokens), axis=0)
            e_ref[rows, :] = weights.astype(jnp.bfloat16)
            ds_ref[rows, :] = (weights * (grad_probs[at : at + CHUNK, :] - term)).astype(jnp.bfloat16)
    inv_ref[...] = 1.0 / jnp.sum(total, axis=0, keepdims=True)


def add_gradients(head, valid, low, high, rank, q_ref, do_ref, down, up_q, wk, dk_acc, dv_acc, slot):
    tokens = q_ref.shape[0]
    _, e_ref, ds_ref, inv_ref = slot
    (_, group, inner), column, _ = head
    height = wk.shape[1]
    inverse = inv_ref[...] * valid
    inverse_rows = jnp.broadcast_to(inverse, (HEAD_SIZE, tokens)).T
    scaled = inverse_rows * score_scale
    lane = lax.broadcasted_iota(jnp.int32, (tokens, HEAD_SIZE), 1) // rank
    own_columns = jnp.where(lane == inner, down[...].astype(jnp.float32), 0.0)
    grad_n = (do_ref[:, column].astype(jnp.float32) * inverse_rows).astype(jnp.bfloat16)
    query_n = jnp.concatenate(
        [q_ref[:, column].astype(jnp.float32) * scaled, own_columns * scaled], axis=1
    ).astype(jnp.bfloat16)
    rows = pl.ds(pl.multiple_of(group * height + low, tokens), high - low)
    dv_acc[rows, :] += mm(e_ref[low:high, :], grad_n)
    dk_acc[rows, :] += mm(ds_ref[low:high, :], query_n)
    own = pl.ds(pl.multiple_of(group * HEAD_SIZE + inner * rank, rank), rank)
    up_q[...] += mm(wk[own, low:high], ds_ref[low:high, :]) * (inverse * score_scale)


def all_heads(
    with_previous, per_kv, rank, flags, keys, values, q_hbm, do_hbm, term, w_q, down, up_q, dk, dv, scratch
):
    listed, q, do, q_sem, do_sem, wk, *buffers = scratch
    tokens, width = q.shape
    groups = width // (per_kv * HEAD_SIZE)
    loads = []
    for g in range(groups):
        part = slice(g * per_kv * HEAD_SIZE, (g + 1) * per_kv * HEAD_SIZE)
        loads.append(
            [
                pltpu.make_async_copy(q_hbm.at[:, part], q.at[:, part], q_sem.at[g]),
                pltpu.make_async_copy(do_hbm.at[:, part], do.at[:, part], do_sem.at[g]),
            ]
        )
    for load in sum(loads, []):
        load.start()

    def wait(group):
        for load in loads[group]:
            load.wait()

    def wait_between(held, wanted):
        for g in range(1, groups):
            pl.when((g > held) & (g <= wanted))(functools.partial(wait, g))
        return jnp.maximum(held, wanted)

    height = wk.shape[1]
    for g in range(groups):
        stacked = jnp.concatenate(
            [w_q[:, h * HEAD_SIZE : (h + 1) * HEAD_SIZE] for h in range(g * per_kv, (g + 1) * per_kv)], axis=0
        )
        for block, key in enumerate(keys):
            wk[g * HEAD_SIZE : (g + 1) * HEAD_SIZE, block * tokens : (block + 1) * tokens] = mm(
                stacked, key[:, g * HEAD_SIZE : (g + 1) * HEAD_SIZE], NT
            ).astype(jnp.bfloat16)
    dk[...] = jnp.zeros_like(dk)
    dv[...] = jnp.zeros_like(dv)
    slots = (buffers[:4], buffers[4:])
    for _, e_ref, ds_ref, inv_ref in slots:
        e_ref[...] = jnp.zeros_like(e_ref)
        ds_ref[...] = jnp.zeros_like(ds_ref)
        inv_ref[...] = jnp.zeros_like(inv_ref)
    wait(0)
    index = lax.axis_index("seq")
    core = index % 2
    half = index // 2 % 2
    count = jnp.int32(0)
    for h in range(groups * per_kv):
        listed[count] = jnp.int32(h)
        needs = flags[h] != half
        count = count + jnp.where(needs == with_previous, 1, 0).astype(jnp.int32)

    def head_at(i):
        h = listed[jnp.clip(i, 0, count - 1)]
        group = h // per_kv
        return (
            (h, group, h - group * per_kv),
            pl.ds(pl.multiple_of(h * HEAD_SIZE, HEAD_SIZE), HEAD_SIZE),
            pl.ds(pl.multiple_of(group * HEAD_SIZE, HEAD_SIZE), HEAD_SIZE),
        )

    for which in range(2):
        low = 1 - which

        def softmax(i, slot):
            scores_and_softmax(head_at(i), low, 1, keys, values, q, do, term, slot)

        def gradients(i, slot):
            valid = jnp.where((i >= 0) & (i < count), 1.0, 0.0).astype(jnp.float32)
            add_gradients(
                head_at(i), valid, low * tokens, height, rank, q, do, down, up_q, wk, dk, dv, slot
            )

        @pl.when((core == which) & (count > 0))
        def _():
            def two(t, held):
                held = wait_between(held, head_at(2 * t + 1)[0][1])
                softmax(2 * t, slots[0])
                gradients(2 * t - 1, slots[1])
                softmax(2 * t + 1, slots[1])
                gradients(2 * t, slots[0])
                return held

            held = lax.fori_loop(0, (count + 1) // 2, two, jnp.int32(0))
            wait_between(held, jnp.int32(groups - 1))

            @pl.when(count % 2 == 0)
            def _():
                gradients(count - 1, slots[1])

    @pl.when(count == 0)
    def _():
        wait_between(jnp.int32(0), jnp.int32(groups - 1))


def own_kernel(
    per_kv, rank, flags, q, do, term, w_q, down, kv_own, kv_sib, up_q, dk, dv, *scratch
):
    up_q[...] = jnp.zeros_like(up_q)
    keys, values = ([kv.at[c] for kv in (kv_sib, kv_own)] for c in range(2))
    all_heads(False, per_kv, rank, flags, keys, values, q, do, term, w_q, down, up_q, dk, dv, scratch)


def previous_kernel(
    scale, per_kv, rank, flags, q, do, term, w_q, down, kv_own, kv_sib, kv_pc, kv_px,
    up_q_own, dk_own, dv_own, w_kv, down_win,
    keep_own, keep_pc, send, up_q, up_keep, up_send, grad_up,
    dk, dv, grads, *scratch,
):
    tokens = q.shape[0]
    up_q[...] = up_q_own[...]
    keys, values = ([kv.at[c] for kv in (kv_sib, kv_own, kv_pc, kv_px)] for c in range(2))
    all_heads(True, per_kv, rank, flags, keys, values, q, do, term, w_q, down, up_q, dk, dv, scratch)
    up_kv = [jnp.zeros((rank, 4 * tokens), jnp.float32) for _ in range(2)]
    kv_width = kv_own.shape[2]
    for g in range(kv_width // HEAD_SIZE):
        columns = slice(g * HEAD_SIZE, (g + 1) * HEAD_SIZE)
        low_row, own_row = g * 4 * tokens, g * 2 * tokens
        by_head = None
        for block in range(4):
            tail = dk[low_row + block * tokens : low_row + (block + 1) * tokens, HEAD_SIZE:]
            if block < 2:
                tail = tail + dk_own[own_row + block * tokens : own_row + (block + 1) * tokens, HEAD_SIZE:]
            part = mm(tail.T.astype(jnp.bfloat16), keys[block][:, columns])
            by_head = part if by_head is None else by_head + part
        for h in range(per_kv):
            at = (g * per_kv + h) * HEAD_SIZE
            grads[:rank, at : at + HEAD_SIZE] = by_head[h * rank : (h + 1) * rank, :]
        for c, acc, start in ((0, dk, dk_own), (1, dv, dv_own)):
            total = acc[low_row : low_row + 4 * tokens, :HEAD_SIZE]
            near = total[: 2 * tokens] + start[own_row : own_row + 2 * tokens, :HEAD_SIZE]
            low = jnp.concatenate([near, total[2 * tokens :]]).astype(jnp.bfloat16)
            keep_own[c, :, columns] = near[tokens:]
            keep_pc[c, :, columns] = total[2 * tokens : 3 * tokens]
            send[0, c, :, columns] = low[:tokens]
            send[1, c, :, columns] = low[3 * tokens :]
            up_kv[c] = up_kv[c] + mm(w_kv[c, :, columns], low, NT)
            own = slice(c * rank, (c + 1) * rank)
            grad_kv = mm(down_win[own, :], low)
            for r in range(rank):
                row, at = divmod((c * rank + r) * kv_width + g * HEAD_SIZE, grads.shape[1])
                grads[rank + row : rank + row + 1, at : at + HEAD_SIZE] = grad_kv[r : r + 1, :]
    sib, near, pc, px = (
        jnp.concatenate([up_kv[c][:, block * tokens : (block + 1) * tokens] for c in range(2)])
        for block in range(4)
    )
    grad_up[...] = (grads[...] * scale).astype(jnp.bfloat16)
    up_keep[...] = jnp.concatenate([near, pc])
    up_send[...] = jnp.concatenate([sib, px]).astype(jnp.bfloat16)


def attention(scale, flags, queries, grads, terms, w_q, down, kv_own, kv_sib):
    tokens, width = queries.shape
    kv_width = kv_own.shape[2]
    kv_local = kv_width // HEAD_SIZE
    per_kv = width // kv_width
    rank = w_q.shape[0]
    assert per_kv * rank == HEAD_SIZE
    f32, bf16 = jnp.float32, jnp.bfloat16
    shape = jax.ShapeDtypeStruct
    pairs = kv_local * per_kv * tokens * tokens
    smem = pl.BlockSpec(memory_space=pltpu.SMEM)
    vmem = pl.BlockSpec(memory_space=pltpu.VMEM)
    hbm = pl.BlockSpec(memory_space=pltpu.HBM)

    def scratch(blocks):
        rows = blocks * tokens
        slot = [
            pltpu.VMEM((rows, tokens), f32),
            pltpu.VMEM((rows, tokens), bf16),
            pltpu.VMEM((rows, tokens), bf16),
            pltpu.VMEM((1, tokens), f32),
        ]
        return [
            pltpu.SMEM((kv_local * per_kv + 1,), jnp.int32),
            pltpu.VMEM((tokens, width), bf16),
            pltpu.VMEM((tokens, width), bf16),
            pltpu.SemaphoreType.DMA((kv_local,)),
            pltpu.SemaphoreType.DMA((kv_local,)),
            pltpu.VMEM((kv_local * HEAD_SIZE, rows), bf16),
        ] + slot * 2

    def call(kernel, out_shape, scratch_shapes, work, name, *args):
        return pl.pallas_call(
            functools.partial(kernel, per_kv, rank),
            in_specs=[smem, hbm, hbm] + [vmem] * (len(args) - 3),
            out_specs=[vmem] * len(out_shape),
            out_shape=out_shape,
            scratch_shapes=scratch_shapes,
            compiler_params=pltpu.CompilerParams(vmem_limit_bytes=VMEM_LIMIT),
            cost_estimate=pl.CostEstimate(
                flops=work * pairs * HEAD_SIZE, bytes_accessed=6 * tokens * width, transcendentals=pairs
            ),
            name=name,
        )(*args)

    queries, grads = (pltpu.with_memory_space_constraint(a, pltpu.HBM) for a in (queries, grads))
    common = (flags, queries, grads, terms, w_q, down, kv_own, kv_sib)

    def own():
        return call(
            own_kernel,
            [
                shape((rank, tokens), f32),
                shape((2 * tokens * kv_local, 2 * HEAD_SIZE), f32),
                shape((2 * tokens * kv_local, HEAD_SIZE), f32),
            ],
            scratch(2),
            40,
            "own_chip_heads",
            *common,
        )

    def previous(kv_pc, kv_px, own_grads, w_kv, down_win):
        grad_rows = rank + 2 * rank * kv_width // width
        return call(
            functools.partial(previous_kernel, scale),
            [
                shape((2, tokens, kv_width), f32),
                shape((2, tokens, kv_width), f32),
                shape((2, 2, tokens, kv_width), bf16),
                shape((rank, tokens), f32),
                shape((4 * rank, tokens), f32),
                shape((4 * rank, tokens), bf16),
                shape((grad_rows, width), bf16),
            ],
            [
                pltpu.VMEM((4 * tokens * kv_local, 2 * HEAD_SIZE), f32),
                pltpu.VMEM((4 * tokens * kv_local, HEAD_SIZE), f32),
                pltpu.VMEM((grad_rows, width), f32),
            ]
            + scratch(4),
            80,
            "previous_chip_heads",
            *common,
            kv_pc,
            kv_px,
            *own_grads,
            w_kv,
            down_win,
        )

    return own, previous


def exchanged(value, axis, bit):
    return lax.ppermute(value, axis, [(i, i ^ bit) for i in range(lax.axis_size(axis))])


def moved(value, axis, by):
    count = lax.axis_size(axis)
    return lax.ppermute(value, axis, [(i, (i + by) % count) for i in range(count)])


def summed(value, axis):
    bit = 1
    while bit < lax.axis_size(axis):
        value = value + exchanged(value, axis, bit)
        bit *= 2
    return value


def small_call(kernel, out_shape, *args, scratch=(), limit=1):
    vmem = pl.BlockSpec(memory_space=pltpu.VMEM)
    return pl.pallas_call(
        kernel,
        in_specs=[vmem] * len(args),
        out_specs=[vmem] * len(out_shape),
        out_shape=out_shape,
        scratch_shapes=list(scratch),
        compiler_params=pltpu.CompilerParams(vmem_limit_bytes=limit * SMALL_VMEM),
    )(*args)


def place(unit, radix):
    return lax.axis_index("seq") // unit % radix


def lanes(index, wide):
    return pl.ds(pl.multiple_of(index * wide, HEAD_SIZE), wide)


def projected_and_stacked(down_weight, inputs, key_rows, value_rows):
    rows, width = down_weight.shape
    tokens, kv_width = key_rows.shape
    steps = kv_width // HEAD_SIZE
    args = [
        pltpu.with_memory_space_constraint(a, pltpu.HBM)
        for a in (down_weight, inputs, key_rows, value_rows)
    ]

    def kernel(weight, tokens_in, key, value, down, kv):
        part = mm(weight[...], tokens_in[...], NT)

        @pl.when(pl.program_id(0) == 0)
        def _():
            down[...] = part

        @pl.when(pl.program_id(0) > 0)
        def _():
            down[...] += part

        kv[0] = key[...]
        kv[1] = value[...]

    def columns(high, wide):
        return pl.BlockSpec((high, wide // steps), lambda g: (0, g))

    return pl.pallas_call(
        kernel,
        grid=(steps,),
        in_specs=[
            columns(rows, width),
            columns(tokens, width),
            columns(tokens, kv_width),
            columns(tokens, kv_width),
        ],
        out_specs=[
            pl.BlockSpec((rows, tokens), lambda g: (0, 0)),
            pl.BlockSpec((2, tokens, kv_width // steps), lambda g: (0, 0, g)),
        ],
        out_shape=[
            jax.ShapeDtypeStruct((rows, tokens), jnp.float32),
            jax.ShapeDtypeStruct((2, tokens, kv_width), jnp.bfloat16),
        ],
        compiler_params=pltpu.CompilerParams(
            dimension_semantics=("arbitrary",), vmem_limit_bytes=2 * SMALL_VMEM
        ),
    )(*args)


def up_sums(up_q, up_keep, received):
    rank, tokens = up_q.shape

    def kernel(up_q, keep, other, mine, to_send, previous):
        total = keep[...] + other[...].astype(jnp.float32)
        own = jnp.concatenate([up_q[...], total[: 2 * rank]])
        mine[...] = own
        to_send[...] = own.astype(jnp.bfloat16)
        previous[...] = total[2 * rank :].astype(jnp.bfloat16)

    shape = jax.ShapeDtypeStruct
    return small_call(
        kernel,
        [
            shape((3 * rank, tokens), jnp.float32),
            shape((3 * rank, tokens), jnp.bfloat16),
            shape((2 * rank, tokens), jnp.bfloat16),
        ],
        up_q,
        up_keep,
        received,
    )


def up_terms(mine, to_send, previous):
    heads, count = lax.axis_size("head"), lax.axis_size("seq")
    nearby = moved(previous, "seq", -2)
    if heads == 2:
        pairs = [
            (s * heads + h, (s - 2) % count * heads + 1 - h) for s in range(count) for h in range(heads)
        ]
        return [mine, exchanged(to_send, "head", 1), nearby, lax.ppermute(previous, ("seq", "head"), pairs)]
    rank = mine.shape[0] - previous.shape[0]
    total = jnp.concatenate([mine[:rank], mine[rank:] + nearby.astype(jnp.float32)])
    bit = 1
    while 2 * bit < heads:
        total = total + exchanged(total.astype(jnp.bfloat16), "head", bit).astype(jnp.float32)
        bit *= 2
    return [total, exchanged(total.astype(jnp.bfloat16), "head", bit)]


def weight_halves(terms, inputs, grad_up, scale):
    width = inputs.shape[1]
    wide = width // 2
    up_rows, tokens = terms[0].shape
    rows = up_rows + grad_up.shape[0]
    given = len(terms)

    def kernel(*refs):
        tokens_in, grads, up_low, *out = refs[given:]
        up = jnp.zeros((up_rows, tokens), jnp.float32)
        for term in refs[:given]:
            value = term[...].astype(jnp.float32)
            if value.shape[0] < up_rows:
                value = jnp.concatenate(
                    [jnp.zeros((up_rows - value.shape[0], tokens), jnp.float32), value]
                )
            up = up + value
        up = up.astype(jnp.bfloat16)
        up_low[...] = up
        for d in range(2):
            at = lanes(place(1, 2) ^ d, wide)
            out[d][...] = jnp.concatenate(
                [mm(up, tokens_in[:, at]) * scale, grads[:, at].astype(jnp.float32)]
            ).astype(jnp.bfloat16)

    shape = jax.ShapeDtypeStruct
    return small_call(
        kernel,
        [shape((up_rows, tokens), jnp.bfloat16)] + [shape((rows, wide), jnp.bfloat16)] * 2,
        *terms,
        inputs,
        grad_up,
        limit=2,
    )


def exchanged_pieces(pieces, unit):
    return [pieces[0]] + [exchanged(p, "seq", d * unit) for d, p in enumerate(pieces) if d]


def summed_and_cut(pieces, unit, radix):
    rows, whole = pieces[0].shape
    wide = whole // radix
    if wide % HEAD_SIZE:
        total = sum(p.astype(jnp.float32) for p in pieces).astype(jnp.bfloat16)
        return [
            lax.dynamic_slice_in_dim(total, (place(unit, radix) ^ d) * wide, wide, 1)
            for d in range(radix)
        ]
    given = len(pieces)

    def kernel(*refs):
        total = refs[-1]
        total[...] = sum(p[...].astype(jnp.float32) for p in refs[:given])
        for d in range(radix):
            refs[given + d][...] = total[:, lanes(place(unit, radix) ^ d, wide)].astype(jnp.bfloat16)

    return small_call(
        kernel,
        [jax.ShapeDtypeStruct((rows, wide), jnp.bfloat16)] * radix,
        *pieces,
        scratch=[pltpu.VMEM((rows, whole), jnp.float32)],
    )


def joined(pieces, unit):
    rows, wide = pieces[0].shape
    radix = len(pieces)
    if wide % HEAD_SIZE:
        whole = jnp.zeros((rows, radix * wide), jnp.bfloat16)
        for d in range(radix):
            whole = lax.dynamic_update_slice_in_dim(
                whole, pieces[d], (place(unit, radix) ^ d) * wide, 1
            )
        return whole

    def kernel(*refs):
        for d in range(radix):
            refs[radix][:, lanes(place(unit, radix) ^ d, wide)] = refs[d][...]

    return small_call(kernel, [jax.ShapeDtypeStruct((rows, radix * wide), jnp.bfloat16)], *pieces)[0]


def joined_outputs(pieces, rank, kv_shape):
    rows, wide = pieces[0].shape
    extra = rows - 4 * rank
    each = wide // kv_shape[1]
    per_row = kv_shape[0] // extra

    def kernel(one, two, down, up_q, up_kv):
        for d, half in enumerate((one, two)):
            at = place(1, 2) ^ d
            piece = half[...].astype(jnp.float32)
            down[:, lanes(at, wide)] = piece[: 3 * rank]
            up_q[:, lanes(at, wide)] = piece[3 * rank : 4 * rank]
            for i in range(extra):
                for b in range(each):
                    up_kv[pl.ds(per_row * i + each * at + b, 1), :] = piece[
                        4 * rank + i : 4 * rank + i + 1, b * kv_shape[1] : (b + 1) * kv_shape[1]
                    ]

    shape = jax.ShapeDtypeStruct
    return small_call(
        kernel,
        [
            shape((3 * rank, 2 * wide), jnp.float32),
            shape((rank, 2 * wide), jnp.float32),
            shape(kv_shape, jnp.float32),
        ],
        *pieces,
    )


def per_device(
    queries,
    layer_key_rows,
    layer_value_rows,
    output_gradient,
    output_row_sums,
    shifted_head_flags,
    inputs,
    adapter_down_weight,
    query_up_weight,
    key_value_up_weight,
):
    seq_count = lax.axis_size("seq")
    tokens, width = queries.shape
    kv_width = layer_key_rows.shape[1]
    whole_len = tokens * seq_count
    rank = adapter_down_weight.shape[1]
    assert GROUP == 4 * tokens and SHIFT == 2 * tokens
    levels = (seq_count.bit_length() - 1) // 2
    assert 4**levels == seq_count
    flattened_down = adapter_down_weight.reshape(3 * rank, width)
    scale = adapter_scale / math.sqrt(whole_len)
    down_part, kv_own = projected_and_stacked(flattened_down, inputs, layer_key_rows, layer_value_rows)
    kv_pc = moved(kv_own, "seq", 2)
    kv_sib = exchanged(kv_own, "seq", 1)

    down_low = summed(down_part, "head").astype(jnp.bfloat16)
    down_tiled = jnp.tile(down_low[:rank].T, (1, HEAD_SIZE // rank))
    down_own = down_low[rank:]
    down_pc = moved(down_own, "seq", 2)

    own, previous = attention(
        scale,
        shifted_head_flags,
        queries,
        output_gradient,
        output_row_sums,
        query_up_weight,
        down_tiled,
        kv_own,
        kv_sib,
    )
    own_grads, kv_pc, down_pc = lax.optimization_barrier((own(), kv_pc, down_pc))
    kv_px = exchanged(kv_pc, "seq", 1)
    down_others = exchanged(jnp.concatenate([down_own, down_pc]), "seq", 1)
    down_win = jnp.concatenate(
        [down_others[: 2 * rank], down_own, down_pc, down_others[2 * rank :]], axis=1
    )
    keep_own, keep_pc, send, up_q, up_keep, up_send, grad_up = previous(
        kv_pc, kv_px, own_grads, key_value_up_weight, down_win
    )

    up_received, send = lax.optimization_barrier((exchanged(up_send, "seq", 1), send))
    received = exchanged(send, "seq", 1)
    terms = up_terms(*up_sums(up_q, up_keep, up_received))
    back = (keep_pc + received[1].astype(jnp.float32)).astype(jnp.bfloat16)
    up_low, *pieces = weight_halves(terms, inputs, grad_up, scale)
    pieces = exchanged_pieces(summed_and_cut(exchanged_pieces(pieces, 1), 2, 2), 2)
    pieces, back = lax.optimization_barrier((pieces, back))
    back = moved(back, "seq", -2)
    for level in range(1, levels):
        pieces = exchanged_pieces(summed_and_cut(pieces, 4**level, 4), 4**level)
    total = sum(p.astype(jnp.float32) for p in pieces).astype(jnp.bfloat16)
    key_value_gradient = (
        keep_own + received[0].astype(jnp.float32) + back.astype(jnp.float32)
    ).astype(jnp.bfloat16)
    grad_inputs = (
        adapter_scale
        * lax.dot_general(
            up_low, flattened_down, (((0,), (0,)), ((), ())), preferred_element_type=jnp.float32
        )
    ).astype(jnp.bfloat16)
    for level in range(levels - 1, 0, -1):
        total = joined(exchanged_pieces([total] * 4, 4**level), 4**level)
    total, grad_inputs = lax.optimization_barrier((total, grad_inputs))
    total = joined(exchanged_pieces([total] * 2, 2), 2)
    total, key_value_gradient = lax.optimization_barrier((total, key_value_gradient))
    down_gradient, grad_up_q, grad_up_kv = joined_outputs(
        exchanged_pieces([total] * 2, 1), rank, (2 * rank, kv_width)
    )
    return (
        grad_inputs,
        key_value_gradient,
        down_gradient.reshape(3, rank, width),
        grad_up_q,
        grad_up_kv.reshape(2, rank, kv_width),
    )


def solution(mesh):
    placed = (
        P("seq", "head"),
        P("seq", "head"),
        P("seq", "head"),
        P("seq", "head"),
        P("head", "seq"),
        P("head"),
        P("seq", "head"),
        P(None, None, "head"),
        P(None, "head"),
        P(None, None, "head"),
    )
    return jax.shard_map(
        per_device,
        mesh=mesh,
        in_specs=placed,
        out_specs=(
            P("seq", "head"),
            P(None, "seq", "head"),
            P(None, None, "head"),
            P(None, "head"),
            P(None, None, "head"),
        ),
        check_vma=False,
    )
```

profile of v0, /device:TPU:0, one launch (start us, length us, event | category | flops | bytes accessed | tf_op | source)
XLA Modules:
  0.0 92.5 jit_solution(9660529260820239357)
XLA Ops:
  0.7 3.2 %shard_map.137 = (f32[48,256]{1,0:T(8,128)S(1)}, bf16[2,256,512]{2,1,0:T(8,128)(2,1)S(1)}) custom-call(bf16[48,4096]{1,0:T(8,128)(2,1)} %bitcast.18, bf16[256,4096]{1,0:T(8,128)(2,1)} %refs_4_.1, bf16[256,512]{1,0:T(8,128)(2,1)} %key.1, bf16[256,512]{1,0:T(8,128)(2,1)} %value.1), custom_call_target="tpu_custom_call" | custom-call | tf_op jit(solution)/shard_map/pallas_call | solution.py:392
  4.4 2.6 %collective-permute-start = (f32[48,256]{1,0:T(8,128)S(1)}, f32[48,256]{1,0:T(8,128)S(1)}, u32[]{:S(2)}, u32[]{:S(2)}) collective-permute-start(f32[48,256]{1,0:T(8,128)S(1)} %get-tuple-element.46), channel_id=1, source_target_pairs={{0,1},{1,0},{2,3},{3,2},{4,5},{5,4},{6,7},{7,6},{8,9},{9,8},{10,11... | collective-permute-start | bytes 147464 | tf_op jit(solution)/shard_map/ppermute | solution.py:330
  7.0 1.5 %collective-permute-start.2 = (bf16[2,256,512]{2,1,0:T(8,128)(2,1)S(1)}, bf16[2,256,512]{2,1,0:T(8,128)(2,1)S(1)}, u32[]{:S(2)}, u32[]{:S(2)}) collective-permute-start(bf16[2,256,512]{2,1,0:T(8,128)(2,1)S(1)} %get-tuple-element.47.kv_own), channel_id=1, source_target_pairs={{0,4},{2,6},{4,8},{6,10},{8,12},{10,14},{12,16},{14,18},{16,20},{1... | collective-permute-start | bytes 1572872 | tf_op jit(solution)/shard_map/ppermute | solution.py:335
  9.4 1.8 %collective-permute-start.3 = (bf16[32,256]{1,0:T(8,128)(2,1)S(1)}, bf16[32,256]{1,0:T(8,128)(2,1)S(1)}, u32[]{:S(2)}, u32[]{:S(2)}) collective-permute-start(bf16[32,256]{1,0:T(8,128)(2,1)S(1)} %slice.25), channel_id=1, source_target_pairs={{0,4},{2,6},{4,8},{6,10},{8,12},{10,14},{12,16},{14,18},{16,20},{1... | collective-permute-start | bytes 49160 | tf_op jit(solution)/shard_map/ppermute | solution.py:335
  11.3 8.4 %own_chip_heads.1 = (f32[16,256]{1,0:T(8,128)S(1)}, f32[2048,256]{1,0:T(8,128)S(1)}, f32[2048,128]{1,0:T(8,128)S(1)}) custom-call(s32[32]{0:T(128)S(1)} %copy-done.4, bf16[256,4096]{1,0:T(8,128)(2,1)} %q.3, bf16[256,4096]{1,0:T(8,128)(2,1)} %do.3, f32[32,256]{1,0:T(8,128)S(1)} %copy-done.2, bf16[16,4096]{1,0:T(8,128)(2,1)S(1)} %copy-done.1, ...), custom_call_target="tpu_custom_call" | custom-call | flops 10737418240 | bytes 6291456 | tf_op jit(solution)/shard_map/own_chip_heads/pallas_call | solution.py:267
  19.7 4.4 %collective-permute-done.3 = bf16[32,256]{1,0:T(8,128)(2,1)S(1)} collective-permute-done((bf16[32,256]{1,0:T(8,128)(2,1)S(1)}, bf16[32,256]{1,0:T(8,128)(2,1)S(1)}, u32[]{:S(2)}, u32[]{:S(2)}) %collective-permute-start.3) | collective-permute-done | bytes 16416 | tf_op jit(solution)/shard_map/ppermute | solution.py:335
  24.7 1.4 %collective-permute-done.5 = bf16[64,256]{1,0:T(8,128)(2,1)S(1)} collective-permute-done((bf16[64,256]{1,0:T(8,128)(2,1)S(1)}, bf16[64,256]{1,0:T(8,128)(2,1)S(1)}, u32[]{:S(2)}, u32[]{:S(2)}) %collective-permute-start.5) | collective-permute-done | bytes 32800 | tf_op jit(solution)/shard_map/ppermute | solution.py:330
  26.1 13.3 %previous_chip_heads.1 = (f32[2,256,512]{2,1,0:T(8,128)S(1)}, f32[2,256,512]{2,1,0:T(8,128)S(1)}, bf16[2,2,256,512]{3,2,1,0:T(8,128)(2,1)S(1)}, f32[16,256]{1,0:...) custom-call(s32[32]{0:T(128)S(1)} %copy-done.4, ...), custom_call_target="tpu_custom_call" | custom-call | flops 21474836480 | bytes 6291456 | tf_op jit(solution)/shard_map/previous_chip_heads/pallas_call | solution.py:267
  39.4 3.1 %collective-permute-start.6 = (bf16[64,256]{1,0:T(8,128)(2,1)S(1)}, bf16[64,256]{1,0:T(8,128)(2,1)S(1)}, u32[]{:S(2)}, u32[]{:S(2)}) collective-permute-start(bf16[64,256]{1,0:T(8,128)(2,1)S(1)} %get-tuple-element.58), channel_id=1, source_target_pairs={{0,2},{2,0},{4,6},{6,4},{8,10},{10,8},{12,14},{14,12},{16,18},{18,... | collective-permute-start | bytes 98312 | tf_op jit(solution)/shard_map/ppermute | solution.py:330
  43.7 4.0 %collective-permute-start.7 = (bf16[48,256]{1,0:T(8,128)(2,1)S(1)}, bf16[48,256]{1,0:T(8,128)(2,1)S(1)}, u32[]{:S(2)}, u32[]{:S(2)}) collective-permute-start(bf16[48,256]{1,0:T(8,128)(2,1)S(1)} %get-tuple-element.62), channel_id=1, source_target_pairs={{0,1},{1,0},{2,3},{3,2},{4,5},{5,4},{6,7},{7,6},{8,9},{9,8},{10,11... | collective-permute-start | bytes 73736 | tf_op jit(solution)/shard_map/ppermute | solution.py:330
  47.7 2.7 %collective-permute-start.9 = (bf16[32,256]{1,0:T(8,128)(2,1)S(1)}, bf16[32,256]{1,0:T(8,128)(2,1)S(1)}, u32[]{:S(2)}, u32[]{:S(2)}) collective-permute-start(bf16[32,256]{1,0:T(8,128)(2,1)S(1)} %get-tuple-element.63), channel_id=1, source_target_pairs={{0,29},{1,28},{2,31},{3,30},{4,1},{5,0},{6,3},{7,2},{8,5},{9,4},{1... | collective-permute-start | bytes 49160 | tf_op jit(solution)/shard_map/ppermute | solution.py:446
  50.4 1.9 %collective-permute-done.9.refs_3_ = bf16[32,256]{1,0:T(8,128)(2,1)S(1)} collective-permute-done((bf16[32,256]{1,0:T(8,128)(2,1)S(1)}, bf16[32,256]{1,0:T(8,128)(2,1)S(1)}, u32[]{:S(2)}, u32[]{:S(2)}) %collective-permute-start.9) | collective-permute-done | bytes 16416 | tf_op jit(solution)/shard_map/ppermute | solution.py:446
  52.3 1.8 %collective-permute-done.8.refs_2_ = bf16[32,256]{1,0:T(8,128)(2,1)S(1)} collective-permute-done((bf16[32,256]{1,0:T(8,128)(2,1)S(1)}, bf16[32,256]{1,0:T(8,128)(2,1)S(1)}, u32[]{:S(2)}, u32[]{:S(2)}) %collective-permute-start.8) | collective-permute-done | bytes 16416 | tf_op jit(solution)/shard_map/ppermute | solution.py:335
  54.8 1.6 %collective-permute-done.10.refs_1_ = bf16[68,2048]{1,0:T(8,128)(2,1)S(1)} collective-permute-done((bf16[68,2048]{1,0:T(8,128)(2,1)S(1)}, bf16[68,2048]{1,0:T(8,128)(2,1)S(1)}, u32[]{:S(2)}, u32[]{:S(2)}) %collective-permute-start.10) | collective-permute-done | bytes 278560 | tf_op jit(solution)/shard_map/ppermute | solution.py:330
  56.7 5.7 %collective-permute-done.11.refs_1_ = bf16[68,1024]{1,0:T(8,128)(2,1)S(1)} collective-permute-done((bf16[68,1024]{1,0:T(8,128)(2,1)S(1)}, bf16[68,1024]{1,0:T(8,128)(2,1)S(1)}, u32[]{:S(2)}, u32[]{:S(2)}) %collective-permute-start.11) | collective-permute-done | bytes 139296 | tf_op jit(solution)/shard_map/ppermute | solution.py:330
  62.6 2.2 %collective-permute-start.14 = (bf16[68,256]{1,0:T(8,128)(2,1)S(1)}, bf16[68,256]{1,0:T(8,128)(2,1)S(1)}, u32[]{:S(2)}, u32[]{:S(2)}) collective-permute-start(bf16[68,256]{1,0:T(8,128)(2,1)S(1)} %get-tuple-element.75), channel_id=1, source_target_pairs={{0,16},{2,18},{4,20},{6,22},{8,24},{10,26},{12,28},{14,30},{16,0},... | collective-permute-start | bytes 104456 | tf_op jit(solution)/shard_map/ppermute | solution.py:330
  64.8 2.1 %collective-permute-start.15 = (bf16[68,256]{1,0:T(8,128)(2,1)S(1)}, bf16[68,256]{1,0:T(8,128)(2,1)S(1)}, u32[]{:S(2)}, u32[]{:S(2)}) collective-permute-start(bf16[68,256]{1,0:T(8,128)(2,1)S(1)} %get-tuple-element.76), channel_id=1, source_target_pairs={{0,24},{2,26},{4,28},{6,30},{8,16},{10,18},{12,20},{14,22},{16,8},... | collective-permute-start | bytes 104456 | tf_op jit(solution)/shard_map/ppermute | solution.py:330
  67.0 2.9 %collective-permute-start.20 = (bf16[2,256,512]{2,1,0:T(8,128)(2,1)S(1)}, bf16[2,256,512]{2,1,0:T(8,128)(2,1)S(1)}, u32[]{:S(2)}, u32[]{:S(2)}) collective-permute-start(bf16[2,256,512]{2,1,0:T(8,128)(2,1)S(1)} %fusion.3), channel_id=1, source_target_pairs={{0,28},{2,30},{4,0},{6,2},{8,4},{10,6},{12,8},{14,10},{16,12},{18,... | collective-permute-start | bytes 1572872 | tf_op jit(solution)/shard_map/ppermute | solution.py:335
  71.1 1.8 %collective-permute-start.18 = (bf16[68,256]{1,0:T(8,128)(2,1)S(1)}, bf16[68,256]{1,0:T(8,128)(2,1)S(1)}, u32[]{:S(2)}, u32[]{:S(2)}) collective-permute-start(bf16[68,256]{1,0:T(8,128)(2,1)S(1)} %add_convert_fusion.refs_0_), channel_id=1, source_target_pairs={{0,24},{2,26},{4,28},{6,30},{8,16},{10,18},{12,20},{14,22},{16,8},... | collective-permute-start | bytes 104456 | tf_op jit(solution)/shard_map/ppermute | solution.py:330
  72.9 2.6 %collective-permute-start.16 = (bf16[68,256]{1,0:T(8,128)(2,1)S(1)}, bf16[68,256]{1,0:T(8,128)(2,1)S(1)}, u32[]{:S(2)}, u32[]{:S(2)}) collective-permute-start(bf16[68,256]{1,0:T(8,128)(2,1)S(1)} %add_convert_fusion.refs_0_), channel_id=1, source_target_pairs={{0,8},{2,10},{4,12},{6,14},{8,0},{10,2},{12,4},{14,6},{16,24},{18,... | collective-permute-start | bytes 104456 | tf_op jit(solution)/shard_map/ppermute | solution.py:330
  75.5 2.0 %fusion = bf16[256,4096]{1,0:T(8,128)(2,1)} fusion(bf16[48,256]{1,0:T(8,128)(2,1)S(1)} %get-tuple-element.77, bf16[48,4096]{1,0:T(8,128)(2,1)S(1)} %bitcast.19), kind=kOutput, calls=%fused_computation.1 | convolution fusion | flops 102760448 | bytes 2514944 | tf_op jit(solution)/shard_map/dot_general | solution.py:637
  77.6 4.8 %collective-permute-done.18.refs_3_ = bf16[68,256]{1,0:T(8,128)(2,1)S(1)} collective-permute-done((bf16[68,256]{1,0:T(8,128)(2,1)S(1)}, bf16[68,256]{1,0:T(8,128)(2,1)S(1)}, u32[]{:S(2)}, u32[]{:S(2)}) %collective-permute-start.18) | collective-permute-done | bytes 34848 | tf_op jit(solution)/shard_map/ppermute | solution.py:330
  83.6 5.1 %collective-permute-done.19.refs_1_ = bf16[68,1024]{1,0:T(8,128)(2,1)S(1)} collective-permute-done((bf16[68,1024]{1,0:T(8,128)(2,1)S(1)}, bf16[68,1024]{1,0:T(8,128)(2,1)S(1)}, u32[]{:S(2)}, u32[]{:S(2)}) %collective-permute-start.19) | collective-permute-done | bytes 139296 | tf_op jit(solution)/shard_map/ppermute | solution.py:330
  89.8 1.6 %collective-permute-done.21.two = bf16[68,2048]{1,0:T(8,128)(2,1)S(1)} collective-permute-done((bf16[68,2048]{1,0:T(8,128)(2,1)S(1)}, bf16[68,2048]{1,0:T(8,128)(2,1)S(1)}, u32[]{:S(2)}, u32[]{:S(2)}) %collective-permute-start.21) | collective-permute-done | bytes 278560 | tf_op jit(solution)/shard_map/ppermute | solution.py:330
  (54 shorter events, 9.0 us)
Async XLA Ops:
  3.9 7.4 %collective-permute-start.1 = (bf16[2,256,512]{2,1,0:T(8,128)(2,1)S(1)}, bf16[2,256,512]{2,1,0:T(8,128)(2,1)S(1)}, u32[]{:S(2)}, u32[]{:S(2)}) collective-permute-start(bf16[2,256,512]{2,1,0:T(8,128)(2,1)S(1)} %get-tuple-element.47.kv_own), channel_id=1, source_target_pairs={{0,2},{2,0},{4,6},{6,4},{8,10},{10,8},{12,14},{14,12},{16,18},{18,... | collective-permute-start | bytes 1572872 | tf_op jit(solution)/shard_map/ppermute | solution.py:330
  4.4 4.9 %collective-permute-start = (f32[48,256]{1,0:T(8,128)S(1)}, f32[48,256]{1,0:T(8,128)S(1)}, u32[]{:S(2)}, u32[]{:S(2)}) collective-permute-start(f32[48,256]{1,0:T(8,128)S(1)} %get-tuple-element.46), channel_id=1, source_target_pairs={{0,1},{1,0},{2,3},{3,2},{4,5},{5,4},{6,7},{7,6},{8,9},{9,8},{10,11... | collective-permute-start | bytes 147464 | tf_op jit(solution)/shard_map/ppermute | solution.py:330
  7.0 17.1 %collective-permute-start.2 = (bf16[2,256,512]{2,1,0:T(8,128)(2,1)S(1)}, bf16[2,256,512]{2,1,0:T(8,128)(2,1)S(1)}, u32[]{:S(2)}, u32[]{:S(2)}) collective-permute-start(bf16[2,256,512]{2,1,0:T(8,128)(2,1)S(1)} %get-tuple-element.47.kv_own), channel_id=1, source_target_pairs={{0,4},{2,6},{4,8},{6,10},{8,12},{10,14},{12,16},{14,18},{16,20},{1... | collective-permute-start | bytes 1572872 | tf_op jit(solution)/shard_map/ppermute | solution.py:335
  9.4 14.8 %collective-permute-start.3 = (bf16[32,256]{1,0:T(8,128)(2,1)S(1)}, bf16[32,256]{1,0:T(8,128)(2,1)S(1)}, u32[]{:S(2)}, u32[]{:S(2)}) collective-permute-start(bf16[32,256]{1,0:T(8,128)(2,1)S(1)} %slice.25), channel_id=1, source_target_pairs={{0,4},{2,6},{4,8},{6,10},{8,12},{10,14},{12,16},{14,18},{16,20},{1... | collective-permute-start | bytes 49160 | tf_op jit(solution)/shard_map/ppermute | solution.py:335
  24.1 2.0 %collective-permute-start.4 = (bf16[2,256,512]{2,1,0:T(8,128)(2,1)S(1)}, bf16[2,256,512]{2,1,0:T(8,128)(2,1)S(1)}, u32[]{:S(2)}, u32[]{:S(2)}) collective-permute-start(bf16[2,256,512]{2,1,0:T(8,128)(2,1)S(1)} %collective-permute-done.2.kv_pc), channel_id=1, source_target_pairs={{0,2},{2,0},{4,6},{6,4},{8,10},{10,8},{12,14},{14,12},{16,18},{18,... | collective-permute-start | bytes 1572872 | tf_op jit(solution)/shard_map/ppermute | solution.py:330
  24.1 1.9 %collective-permute-start.5 = (bf16[64,256]{1,0:T(8,128)(2,1)S(1)}, bf16[64,256]{1,0:T(8,128)(2,1)S(1)}, u32[]{:S(2)}, u32[]{:S(2)}) collective-permute-start(bf16[64,256]{1,0:T(8,128)(2,1)S(1)} %pad_maximum_fusion.1), channel_id=1, source_target_pairs={{0,2},{2,0},{4,6},{6,4},{8,10},{10,8},{12,14},{14,12},{16,18},{18,... | collective-permute-start | bytes 98312 | tf_op jit(solution)/shard_map/ppermute | solution.py:330
  26.1 28.1 %copy-start = (bf16[256,4096]{1,0:T(8,128)(2,1)S(1)}, bf16[256,4096]{1,0:T(8,128)(2,1)}, u32[]{:S(2)}) copy-start(bf16[256,4096]{1,0:T(8,128)(2,1)} %refs_4_.1) | copy-start | bytes 6291460
  39.4 3.9 %collective-permute-start.6 = (bf16[64,256]{1,0:T(8,128)(2,1)S(1)}, bf16[64,256]{1,0:T(8,128)(2,1)S(1)}, u32[]{:S(2)}, u32[]{:S(2)}) collective-permute-start(bf16[64,256]{1,0:T(8,128)(2,1)S(1)} %get-tuple-element.58), channel_id=1, source_target_pairs={{0,2},{2,0},{4,6},{6,4},{8,10},{10,8},{12,14},{14,12},{16,18},{18,... | collective-permute-start | bytes 98312 | tf_op jit(solution)/shard_map/ppermute | solution.py:330
  43.4 13.2 %collective-permute-start.12 = (bf16[2,2,256,512]{3,2,1,0:T(8,128)(2,1)S(1)}, bf16[2,2,256,512]{3,2,1,0:T(8,128)(2,1)S(1)}, u32[]{:S(2)}, u32[]{:S(2)}) collective-permute-start(bf16[2,2,256,512]{3,2,1,0:T(8,128)(2,1)S(1)} %get-tuple-element.70), channel_id=1, source_target_pairs={{0,2},{2,0},{4,6},{6,4},{8,10},{10,8},{12,14},{14,12},{16,18},{18,... | collective-permute-start | bytes 3145736 | tf_op jit(solution)/shard_map/ppermute | solution.py:330
  43.7 10.4 %collective-permute-start.7 = (bf16[48,256]{1,0:T(8,128)(2,1)S(1)}, bf16[48,256]{1,0:T(8,128)(2,1)S(1)}, u32[]{:S(2)}, u32[]{:S(2)}) collective-permute-start(bf16[48,256]{1,0:T(8,128)(2,1)S(1)} %get-tuple-element.62), channel_id=1, source_target_pairs={{0,1},{1,0},{2,3},{3,2},{4,5},{5,4},{6,7},{7,6},{8,9},{9,8},{10,11... | collective-permute-start | bytes 73736 | tf_op jit(solution)/shard_map/ppermute | solution.py:330
  47.7 4.6 %collective-permute-start.9 = (bf16[32,256]{1,0:T(8,128)(2,1)S(1)}, bf16[32,256]{1,0:T(8,128)(2,1)S(1)}, u32[]{:S(2)}, u32[]{:S(2)}) collective-permute-start(bf16[32,256]{1,0:T(8,128)(2,1)S(1)} %get-tuple-element.63), channel_id=1, source_target_pairs={{0,29},{1,28},{2,31},{3,30},{4,1},{5,0},{6,3},{7,2},{8,5},{9,4},{1... | collective-permute-start | bytes 49160 | tf_op jit(solution)/shard_map/ppermute | solution.py:446
  50.4 3.7 %collective-permute-start.8 = (bf16[32,256]{1,0:T(8,128)(2,1)S(1)}, bf16[32,256]{1,0:T(8,128)(2,1)S(1)}, u32[]{:S(2)}, u32[]{:S(2)}) collective-permute-start(bf16[32,256]{1,0:T(8,128)(2,1)S(1)} %get-tuple-element.63), channel_id=1, source_target_pairs={{0,28},{2,30},{4,0},{6,2},{8,4},{10,6},{12,8},{14,10},{16,12},{18,... | collective-permute-start | bytes 49160 | tf_op jit(solution)/shard_map/ppermute | solution.py:335
  54.7 20.8 %copy-start.5 = (bf16[3,16,4096]{2,1,0:T(8,128)(2,1)S(1)}, bf16[3,16,4096]{2,1,0:T(8,128)(2,1)}, u32[]{:S(2)}) copy-start(bf16[3,16,4096]{2,1,0:T(8,128)(2,1)} %param.17) | copy-start | bytes 1179652
  54.7 1.6 %collective-permute-start.10 = (bf16[68,2048]{1,0:T(8,128)(2,1)S(1)}, bf16[68,2048]{1,0:T(8,128)(2,1)S(1)}, u32[]{:S(2)}, u32[]{:S(2)}) collective-permute-start(bf16[68,2048]{1,0:T(8,128)(2,1)S(1)} %get-tuple-element.66), channel_id=1, source_target_pairs={{0,2},{2,0},{4,6},{6,4},{8,10},{10,8},{12,14},{14,12},{16,18},{18,... | collective-permute-start | bytes 835592 | tf_op jit(solution)/shard_map/ppermute | solution.py:330
  56.5 6.0 %collective-permute-start.11 = (bf16[68,1024]{1,0:T(8,128)(2,1)S(1)}, bf16[68,1024]{1,0:T(8,128)(2,1)S(1)}, u32[]{:S(2)}, u32[]{:S(2)}) collective-permute-start(bf16[68,1024]{1,0:T(8,128)(2,1)S(1)} %get-tuple-element.68), channel_id=1, source_target_pairs={{0,4},{2,6},{4,0},{6,2},{8,12},{10,14},{12,8},{14,10},{16,20},{18,... | collective-permute-start | bytes 417800 | tf_op jit(solution)/shard_map/ppermute | solution.py:330
  62.5 7.3 %collective-permute-start.13 = (bf16[68,256]{1,0:T(8,128)(2,1)S(1)}, bf16[68,256]{1,0:T(8,128)(2,1)S(1)}, u32[]{:S(2)}, u32[]{:S(2)}) collective-permute-start(bf16[68,256]{1,0:T(8,128)(2,1)S(1)} %get-tuple-element.74), channel_id=1, source_target_pairs={{0,8},{2,10},{4,12},{6,14},{8,0},{10,2},{12,4},{14,6},{16,24},{18,... | collective-permute-start | bytes 104456 | tf_op jit(solution)/shard_map/ppermute | solution.py:330
  62.6 7.3 %collective-permute-start.14 = (bf16[68,256]{1,0:T(8,128)(2,1)S(1)}, bf16[68,256]{1,0:T(8,128)(2,1)S(1)}, u32[]{:S(2)}, u32[]{:S(2)}) collective-permute-start(bf16[68,256]{1,0:T(8,128)(2,1)S(1)} %get-tuple-element.75), channel_id=1, source_target_pairs={{0,16},{2,18},{4,20},{6,22},{8,24},{10,26},{12,28},{14,30},{16,0},... | collective-permute-start | bytes 104456 | tf_op jit(solution)/shard_map/ppermute | solution.py:330
  64.8 6.2 %collective-permute-start.15 = (bf16[68,256]{1,0:T(8,128)(2,1)S(1)}, bf16[68,256]{1,0:T(8,128)(2,1)S(1)}, u32[]{:S(2)}, u32[]{:S(2)}) collective-permute-start(bf16[68,256]{1,0:T(8,128)(2,1)S(1)} %get-tuple-element.76), channel_id=1, source_target_pairs={{0,24},{2,26},{4,28},{6,30},{8,16},{10,18},{12,20},{14,22},{16,8},... | collective-permute-start | bytes 104456 | tf_op jit(solution)/shard_map/ppermute | solution.py:330
  67.0 21.8 %collective-permute-start.20 = (bf16[2,256,512]{2,1,0:T(8,128)(2,1)S(1)}, bf16[2,256,512]{2,1,0:T(8,128)(2,1)S(1)}, u32[]{:S(2)}, u32[]{:S(2)}) collective-permute-start(bf16[2,256,512]{2,1,0:T(8,128)(2,1)S(1)} %fusion.3), channel_id=1, source_target_pairs={{0,28},{2,30},{4,0},{6,2},{8,4},{10,6},{12,8},{14,10},{16,12},{18,... | collective-permute-start | bytes 1572872 | tf_op jit(solution)/shard_map/ppermute | solution.py:335
  71.1 11.3 %collective-permute-start.18 = (bf16[68,256]{1,0:T(8,128)(2,1)S(1)}, bf16[68,256]{1,0:T(8,128)(2,1)S(1)}, u32[]{:S(2)}, u32[]{:S(2)}) collective-permute-start(bf16[68,256]{1,0:T(8,128)(2,1)S(1)} %add_convert_fusion.refs_0_), channel_id=1, source_target_pairs={{0,24},{2,26},{4,28},{6,30},{8,16},{10,18},{12,20},{14,22},{16,8},... | collective-permute-start | bytes 104456 | tf_op jit(solution)/shard_map/ppermute | solution.py:330
  72.9 10.6 %collective-permute-start.17 = (bf16[68,256]{1,0:T(8,128)(2,1)S(1)}, bf16[68,256]{1,0:T(8,128)(2,1)S(1)}, u32[]{:S(2)}, u32[]{:S(2)}) collective-permute-start(bf16[68,256]{1,0:T(8,128)(2,1)S(1)} %add_convert_fusion.refs_0_), channel_id=1, source_target_pairs={{0,16},{2,18},{4,20},{6,22},{8,24},{10,26},{12,28},{14,30},{16,0},... | collective-permute-start | bytes 104456 | tf_op jit(solution)/shard_map/ppermute | solution.py:330
  72.9 10.6 %collective-permute-start.16 = (bf16[68,256]{1,0:T(8,128)(2,1)S(1)}, bf16[68,256]{1,0:T(8,128)(2,1)S(1)}, u32[]{:S(2)}, u32[]{:S(2)}) collective-permute-start(bf16[68,256]{1,0:T(8,128)(2,1)S(1)} %add_convert_fusion.refs_0_), channel_id=1, source_target_pairs={{0,8},{2,10},{4,12},{6,14},{8,0},{10,2},{12,4},{14,6},{16,24},{18,... | collective-permute-start | bytes 104456 | tf_op jit(solution)/shard_map/ppermute | solution.py:330
  83.5 5.2 %collective-permute-start.19 = (bf16[68,1024]{1,0:T(8,128)(2,1)S(1)}, bf16[68,1024]{1,0:T(8,128)(2,1)S(1)}, u32[]{:S(2)}, u32[]{:S(2)}) collective-permute-start(bf16[68,1024]{1,0:T(8,128)(2,1)S(1)} %shard_map.142.refs_0_), channel_id=1, source_target_pairs={{0,4},{2,6},{4,0},{6,2},{8,12},{10,14},{12,8},{14,10},{16,20},{18,... | collective-permute-start | bytes 417800 | tf_op jit(solution)/shard_map/ppermute | solution.py:330
  89.8 1.6 %collective-permute-start.21 = (bf16[68,2048]{1,0:T(8,128)(2,1)S(1)}, bf16[68,2048]{1,0:T(8,128)(2,1)S(1)}, u32[]{:S(2)}, u32[]{:S(2)}) collective-permute-start(bf16[68,2048]{1,0:T(8,128)(2,1)S(1)} %shard_map.143.one), channel_id=1, source_target_pairs={{0,2},{2,0},{4,6},{6,4},{8,10},{10,8},{12,14},{14,12},{16,18},{18,... | collective-permute-start | bytes 835592 | tf_op jit(solution)/shard_map/ppermute | solution.py:330
  (4 other events, 46.9 us)
where the time goes:
time: 93 us; the launch traced here: 92.5 us
  waiting for transfers between devices  32.4 us (35%)
  starting transfers between devices  29 us (31%)
  Pallas kernels  26.7 us (29%)
  matrix products  2.04 us (2%)
  other arithmetic  1.26 us (1%)
    ppermute x17, waiting for transfers between devices, exchanged(): lax.ppermute(value, axis, [(i, i ^ bit) for i in range(lax.axis_size(axis...  24.2 us
    pallas_call x2, Pallas kernels, call(): pl.pallas_call(functools.partial(kernel, per_kv, rank), in_specs=[smem, h...  21.6 us
    ppermute x17, starting transfers between devices, exchanged(): lax.ppermute(value, axis, [(i, i ^ bit) for i in range(lax.axis_size(axis...  20.1 us
    ppermute x4, waiting for transfers between devices, moved(): lax.ppermute(value, axis, [(i, (i + by) % count) for i in range(count)])  6.24 us
    ppermute x4, starting transfers between devices, moved(): lax.ppermute(value, axis, [(i, (i + by) % count) for i in range(count)])  6.15 us
    pallas_call x1, Pallas kernels, projected_and_stacked(): pl.pallas_call(kernel, grid=(steps,), in_specs=[columns(rows, width), col...  3.22 us
    ppermute x1, starting transfers between devices, up_terms(): lax.ppermute(previous, ('seq', 'head'), pairs)  2.71 us
    dot_general x1, matrix products, per_device(): lax.dot_general(up_low, flattened_down, (((0,), (0,)), ((), ())), preferr...  2.04 us
  transfers between devices with their start and end apart: 22, of which 13 were waited for; matrix products, arithmetic and copies ran while one was open for 3% of the time, Pallas kernels for 10%

commit v1 on v0

--- a/solution.py
+++ b/solution.py
@@ -622,16 +622,25 @@
     received = exchanged(send, "seq", 1)
     terms = up_terms(*up_sums(up_q, up_keep, up_received))
     back = (keep_pc + received[1].astype(jnp.float32)).astype(jnp.bfloat16)
+    chunks = list(back.reshape(4, tokens // 2, kv_width))
+    beside = [(i, i - 2) for i in range(seq_count) if i % 4 >= 2]
+    before = [(i, (i - 2) % seq_count) for i in range(seq_count) if i % 4 < 2]
+
+    terms[1], chunks[0] = lax.optimization_barrier((terms[1], chunks[0]))
+    chunks[0] = lax.ppermute(chunks[0], "seq", before)
     up_low, *pieces = weight_halves(terms, inputs, grad_up, scale)
-    pieces = exchanged_pieces(summed_and_cut(exchanged_pieces(pieces, 1), 2, 2), 2)
-    pieces, back = lax.optimization_barrier((pieces, back))
-    back = moved(back, "seq", -2)
+    pieces = summed_and_cut(exchanged_pieces(pieces, 1), 2, 2)
+    pieces, chunks[:2] = lax.optimization_barrier((pieces, chunks[:2]))
+    chunks[1] = lax.ppermute(chunks[1], "seq", before)
+    pieces = exchanged_pieces(pieces, 2)
+    pieces, chunks, back = lax.optimization_barrier((pieces, chunks, back))
+    chunks[2] = lax.ppermute(chunks[2], "seq", before)
+    back = lax.ppermute(back, "seq", beside)
     for level in range(1, levels):
         pieces = exchanged_pieces(summed_and_cut(pieces, 4**level, 4), 4**level)
     total = sum(p.astype(jnp.float32) for p in pieces).astype(jnp.bfloat16)
-    key_value_gradient = (
-        keep_own + received[0].astype(jnp.float32) + back.astype(jnp.float32)
-    ).astype(jnp.bfloat16)
+    total, chunks = lax.optimization_barrier((total, chunks))
+    chunks[3] = lax.ppermute(chunks[3], "seq", before)
     grad_inputs = (
         adapter_scale
         * lax.dot_general(
@@ -640,7 +649,14 @@
     ).astype(jnp.bfloat16)
     for level in range(levels - 1, 0, -1):
         total = joined(exchanged_pieces([total] * 4, 4**level), 4**level)
-    total, grad_inputs = lax.optimization_barrier((total, grad_inputs))
+    total, grad_inputs, chunks = lax.optimization_barrier((total, grad_inputs, chunks))
+    parts = [a.reshape(4, tokens // 2, kv_width) for a in (keep_own, received[0], back)]
+    key_value_gradient = jnp.stack(
+        [
+            sum(a.astype(jnp.float32) for a in (*(p[i] for p in parts), chunk)).astype(jnp.bfloat16)
+            for i, chunk in enumerate(chunks)
+        ]
+    ).reshape(2, tokens, kv_width)
     total = joined(exchanged_pieces([total] * 2, 2), 2)
     total, key_value_gradient = lax.optimization_barrier((total, key_value_gradient))
     down_gradient, grad_up_q, grad_up_kv = joined_outputs(

time: 93 us -> 110 us (1.18)
  starting transfers between devices: 29 us -> 52.1 us
  waiting for transfers between devices: 32.4 us -> 26.1 us
    ppermute x0 -> x5, starting transfers between devices: none -> 26.7 us  [the longest x1 7.18 us: per_device(): chunks[2] = lax.ppermute(chunks[2], 'seq', before)]
    ppermute x17, waiting for transfers between devices: 24.2 us -> 13.2 us  [exchanged(): lax.ppermute(value, axis, [(i, i ^ bit) for i in range(lax.axis_size(axis...]
    ppermute x0 -> x5, waiting for transfers between devices: none -> 8.09 us  [the longest x1 3.34 us: per_device(): chunks[1] = lax.ppermute(chunks[1], 'seq', before)]
    ppermute x17, starting transfers between devices: 20.1 us -> 17 us  [exchanged(): lax.ppermute(value, axis, [(i, i ^ bit) for i in range(lax.axis_size(axis...]
    ppermute x1, waiting for transfers between devices: 1.92 us -> 0.01 us  [up_terms(): lax.ppermute(previous, ('seq', 'head'), pairs)]
    ppermute x4 -> x3, waiting for transfers between devices: 6.24 us -> 4.76 us  [moved(): lax.ppermute(value, axis, [(i, (i + by) % count) for i in range(count)])]
    another operation x0 -> x2, other arithmetic: none -> 1.17 us  [per_device(): jnp.stack([sum((a.astype(jnp.float32) for a in (*(p[i] for p in parts), c...]
    ppermute x4 -> x3, starting transfers between devices: 6.15 us -> 6.75 us  [moved(): lax.ppermute(value, axis, [(i, (i + by) % count) for i in range(count)])]
  transfers between devices with their start and end apart: 22 -> 26, of which waited for: 13 -> 11; matrix products, arithmetic and copies ran while one was open for 3% -> 2% of each run, Pallas kernels for 10% -> 8%
where the time goes in v1:
time: 110 us
  starting transfers between devices  52.1 us (47%)
  Pallas kernels  27.2 us (25%)
  waiting for transfers between devices  26.1 us (24%)
  matrix products  2.05 us (2%)
  other arithmetic  1.42 us (1%)
    pallas_call x2, Pallas kernels, call(): pl.pallas_call(functools.partial(kernel, per_kv, rank), in_specs=[smem, h...  22.1 us
    ppermute x17, starting transfers between devices, exchanged(): lax.ppermute(value, axis, [(i, i ^ bit) for i in range(lax.axis_size(axis...  17 us
    ppermute x17, waiting for transfers between devices, exchanged(): lax.ppermute(value, axis, [(i, i ^ bit) for i in range(lax.axis_size(axis...  13.2 us
    ppermute x1, starting transfers between devices, per_device(): chunks[2] = lax.ppermute(chunks[2], 'seq', before)  7.18 us
    ppermute x1, starting transfers between devices, per_device(): chunks[3] = lax.ppermute(chunks[3], 'seq', before)  7.13 us
    ppermute x3, starting transfers between devices, moved(): lax.ppermute(value, axis, [(i, (i + by) % count) for i in range(count)])  6.75 us
    ppermute x1, starting transfers between devices, per_device(): chunks[1] = lax.ppermute(chunks[1], 'seq', before)  6.58 us
    ppermute x3, waiting for transfers between devices, moved(): lax.ppermute(value, axis, [(i, (i + by) % count) for i in range(count)])  4.76 us
  transfers between devices with their start and end apart: 26, of which 11 were waited for; matrix products, arithmetic and copies ran while one was open for 2% of the time, Pallas kernels for 8%

profile of v1, /device:TPU:0, one launch (start us, length us, event | category | flops | bytes accessed | tf_op | source)
XLA Modules:
  0.0 110.1 jit_solution(15141534723087897601)
XLA Ops:
  0.7 3.2 %shard_map.137 = (f32[48,256]{1,0:T(8,128)S(1)}, bf16[2,256,512]{2,1,0:T(8,128)(2,1)S(1)}) custom-call(bf16[48,4096]{1,0:T(8,128)(2,1)} %bitcast.69, bf16[256,4096]{1,0:T(8,128)(2,1)} %refs_4_.1, bf16[256,512]{1,0:T(8,128)(2,1)} %key.1, bf16[256,512]{1,0:T(8,128)(2,1)} %value.1), custom_call_target="tpu_custom_call" | custom-call | tf_op jit(solution)/shard_map/pallas_call | solution.py:392
  4.4 2.6 %collective-permute-start = (f32[48,256]{1,0:T(8,128)S(1)}, f32[48,256]{1,0:T(8,128)S(1)}, u32[]{:S(2)}, u32[]{:S(2)}) collective-permute-start(f32[48,256]{1,0:T(8,128)S(1)} %get-tuple-element.65), channel_id=1, source_target_pairs={{0,1},{1,0},{2,3},{3,2},{4,5},{5,4},{6,7},{7,6},{8,9},{9,8},{10,11... | collective-permute-start | bytes 147464 | tf_op jit(solution)/shard_map/ppermute | solution.py:330
  7.0 1.5 %collective-permute-start.2 = (bf16[2,256,512]{2,1,0:T(8,128)(2,1)S(1)}, bf16[2,256,512]{2,1,0:T(8,128)(2,1)S(1)}, u32[]{:S(2)}, u32[]{:S(2)}) collective-permute-start(bf16[2,256,512]{2,1,0:T(8,128)(2,1)S(1)} %get-tuple-element.66.kv_own), channel_id=1, source_target_pairs={{0,4},{2,6},{4,8},{6,10},{8,12},{10,14},{12,16},{14,18},{16,20},{1... | collective-permute-start | bytes 1572872 | tf_op jit(solution)/shard_map/ppermute | solution.py:335
  9.4 1.8 %collective-permute-start.3 = (bf16[32,256]{1,0:T(8,128)(2,1)S(1)}, bf16[32,256]{1,0:T(8,128)(2,1)S(1)}, u32[]{:S(2)}, u32[]{:S(2)}) collective-permute-start(bf16[32,256]{1,0:T(8,128)(2,1)S(1)} %slice.73), channel_id=1, source_target_pairs={{0,4},{2,6},{4,8},{6,10},{8,12},{10,14},{12,16},{14,18},{16,20},{1... | collective-permute-start | bytes 49160 | tf_op jit(solution)/shard_map/ppermute | solution.py:335
  11.3 8.1 %own_chip_heads.1 = (f32[16,256]{1,0:T(8,128)S(1)}, f32[2048,256]{1,0:T(8,128)S(1)}, f32[2048,128]{1,0:T(8,128)S(1)}) custom-call(s32[32]{0:T(128)S(1)} %copy-done.4, bf16[256,4096]{1,0:T(8,128)(2,1)} %q.3, bf16[256,4096]{1,0:T(8,128)(2,1)} %do.3, f32[32,256]{1,0:T(8,128)S(1)} %copy-done.2, bf16[16,4096]{1,0:T(8,128)(2,1)S(1)} %copy-done.1, ...), custom_call_target="tpu_custom_call" | custom-call | flops 10737418240 | bytes 6291456 | tf_op jit(solution)/shard_map/own_chip_heads/pallas_call | solution.py:267
  19.4 4.8 %collective-permute-done.3 = bf16[32,256]{1,0:T(8,128)(2,1)S(1)} collective-permute-done((bf16[32,256]{1,0:T(8,128)(2,1)S(1)}, bf16[32,256]{1,0:T(8,128)(2,1)S(1)}, u32[]{:S(2)}, u32[]{:S(2)}) %collective-permute-start.3) | collective-permute-done | bytes 16416 | tf_op jit(solution)/shard_map/ppermute | solution.py:335
  24.7 1.4 %collective-permute-done.5 = bf16[64,256]{1,0:T(8,128)(2,1)S(1)} collective-permute-done((bf16[64,256]{1,0:T(8,128)(2,1)S(1)}, bf16[64,256]{1,0:T(8,128)(2,1)S(1)}, u32[]{:S(2)}, u32[]{:S(2)}) %collective-permute-start.5) | collective-permute-done | bytes 32800 | tf_op jit(solution)/shard_map/ppermute | solution.py:330
  26.1 14.1 %previous_chip_heads.1 = (f32[2,256,512]{2,1,0:T(8,128)S(1)}, f32[2,256,512]{2,1,0:T(8,128)S(1)}, bf16[2,2,256,512]{3,2,1,0:T(8,128)(2,1)S(1)}, f32[16,256]{1,0:...) custom-call(s32[32]{0:T(128)S(1)} %copy-done.4, ...), custom_call_target="tpu_custom_call" | custom-call | flops 21474836480 | bytes 6291456 | tf_op jit(solution)/shard_map/previous_chip_heads/pallas_call | solution.py:267
  40.2 3.4 %collective-permute-start.6 = (bf16[64,256]{1,0:T(8,128)(2,1)S(1)}, bf16[64,256]{1,0:T(8,128)(2,1)S(1)}, u32[]{:S(2)}, u32[]{:S(2)}) collective-permute-start(bf16[64,256]{1,0:T(8,128)(2,1)S(1)} %get-tuple-element.77), channel_id=1, source_target_pairs={{0,2},{2,0},{4,6},{6,4},{8,10},{10,8},{12,14},{14,12},{16,18},{18,... | collective-permute-start | bytes 98312 | tf_op jit(solution)/shard_map/ppermute | solution.py:330
  44.8 1.7 %collective-permute-start.10 = (bf16[32,256]{1,0:T(8,128)(2,1)S(1)}, bf16[32,256]{1,0:T(8,128)(2,1)S(1)}, u32[]{:S(2)}, u32[]{:S(2)}) collective-permute-start(bf16[32,256]{1,0:T(8,128)(2,1)S(1)} %get-tuple-element.85), channel_id=1, source_target_pairs={{0,29},{1,28},{2,31},{3,30},{4,1},{5,0},{6,3},{7,2},{8,5},{9,4},{1... | collective-permute-start | bytes 49160 | tf_op jit(solution)/shard_map/ppermute | solution.py:446
  46.6 3.5 %collective-permute-start.9 = (bf16[32,256]{1,0:T(8,128)(2,1)S(1)}, bf16[32,256]{1,0:T(8,128)(2,1)S(1)}, u32[]{:S(2)}, u32[]{:S(2)}) collective-permute-start(bf16[32,256]{1,0:T(8,128)(2,1)S(1)} %get-tuple-element.85), channel_id=1, source_target_pairs={{0,28},{2,30},{4,0},{6,2},{8,4},{10,6},{12,8},{14,10},{16,12},{18,... | collective-permute-start | bytes 49160 | tf_op jit(solution)/shard_map/ppermute | solution.py:335
  50.3 3.6 %collective-permute-done.7.refs_1_ = bf16[48,256]{1,0:T(8,128)(2,1)S(1)} collective-permute-done((bf16[48,256]{1,0:T(8,128)(2,1)S(1)}, bf16[48,256]{1,0:T(8,128)(2,1)S(1)}, u32[]{:S(2)}, u32[]{:S(2)}) %collective-permute-start.7) | collective-permute-done | bytes 24608 | tf_op jit(solution)/shard_map/ppermute | solution.py:330
  54.5 4.5 %collective-permute-start.12 = (bf16[128,512]{1,0:T(8,128)(2,1)S(1)}, bf16[128,512]{1,0:T(8,128)(2,1)S(1)}, u32[]{:S(2)}, u32[]{:S(2)}) collective-permute-start(bf16[128,512]{1,0:T(8,128)(2,1)S(1)} %get-tuple-element.91), channel_id=1, source_target_pairs={{0,28},{2,30},{8,4},{10,6},{16,12},{18,14},{24,20},{26,22},{1,29},... | collective-permute-start | bytes 393224 | tf_op jit(solution)/shard_map/ppermute | solution.py:630
  59.1 3.2 %collective-permute-done.12 = bf16[128,512]{1,0:T(8,128)(2,1)S(1)} collective-permute-done((bf16[128,512]{1,0:T(8,128)(2,1)S(1)}, bf16[128,512]{1,0:T(8,128)(2,1)S(1)}, u32[]{:S(2)}, u32[]{:S(2)}) %collective-permute-start.12) | collective-permute-done | bytes 131104 | tf_op jit(solution)/shard_map/ppermute | solution.py:630
  62.9 6.6 %collective-permute-start.14 = (bf16[128,512]{1,0:T(8,128)(2,1)S(1)}, bf16[128,512]{1,0:T(8,128)(2,1)S(1)}, u32[]{:S(2)}, u32[]{:S(2)}) collective-permute-start(bf16[128,512]{1,0:T(8,128)(2,1)S(1)} %get-tuple-element.95), channel_id=1, source_target_pairs={{0,28},{2,30},{8,4},{10,6},{16,12},{18,14},{24,20},{26,22},{1,29},... | collective-permute-start | bytes 393224 | tf_op jit(solution)/shard_map/ppermute | solution.py:634
  69.5 3.3 %collective-permute-done.14 = bf16[128,512]{1,0:T(8,128)(2,1)S(1)} collective-permute-done((bf16[128,512]{1,0:T(8,128)(2,1)S(1)}, bf16[128,512]{1,0:T(8,128)(2,1)S(1)}, u32[]{:S(2)}, u32[]{:S(2)}) %collective-permute-start.14) | collective-permute-done | bytes 131104 | tf_op jit(solution)/shard_map/ppermute | solution.py:634
  73.1 4.2 %collective-permute-start.17 = (bf16[68,256]{1,0:T(8,128)(2,1)S(1)}, bf16[68,256]{1,0:T(8,128)(2,1)S(1)}, u32[]{:S(2)}, u32[]{:S(2)}) collective-permute-start(bf16[68,256]{1,0:T(8,128)(2,1)S(1)} %get-tuple-element.101), channel_id=1, source_target_pairs={{0,24},{2,26},{4,28},{6,30},{8,16},{10,18},{12,20},{14,22},{16,8},... | collective-permute-start | bytes 104456 | tf_op jit(solution)/shard_map/ppermute | solution.py:330
  77.3 7.2 %collective-permute-start.18 = (bf16[128,512]{1,0:T(8,128)(2,1)S(1)}, bf16[128,512]{1,0:T(8,128)(2,1)S(1)}, u32[]{:S(2)}, u32[]{:S(2)}) collective-permute-start(bf16[128,512]{1,0:T(8,128)(2,1)S(1)} %get-tuple-element.104), channel_id=1, source_target_pairs={{0,28},{2,30},{8,4},{10,6},{16,12},{18,14},{24,20},{26,22},{1,29},... | collective-permute-start | bytes 393224 | tf_op jit(solution)/shard_map/ppermute | solution.py:637
  84.5 1.3 %collective-permute-start.24 = (bf16[2,256,512]{2,1,0:T(8,128)(2,1)S(1)}, bf16[2,256,512]{2,1,0:T(8,128)(2,1)S(1)}, u32[]{:S(2)}, u32[]{:S(2)}) collective-permute-start(bf16[2,256,512]{2,1,0:T(8,128)(2,1)S(1)} %fusion.1), channel_id=1, source_target_pairs={{4,0},{6,2},{12,8},{14,10},{20,16},{22,18},{28,24},{30,26},{5,1},{... | collective-permute-start | bytes 1572872 | tf_op jit(solution)/shard_map/ppermute | solution.py:638
  87.0 4.4 %collective-permute-start.19 = (bf16[68,256]{1,0:T(8,128)(2,1)S(1)}, bf16[68,256]{1,0:T(8,128)(2,1)S(1)}, u32[]{:S(2)}, u32[]{:S(2)}) collective-permute-start(bf16[68,256]{1,0:T(8,128)(2,1)S(1)} %add_convert_fusion.refs_0_), channel_id=1, source_target_pairs={{0,8},{2,10},{4,12},{6,14},{8,0},{10,2},{12,4},{14,6},{16,24},{18,... | collective-permute-start | bytes 104456 | tf_op jit(solution)/shard_map/ppermute | solution.py:330
  91.4 7.1 %collective-permute-start.22 = (bf16[128,512]{1,0:T(8,128)(2,1)S(1)}, bf16[128,512]{1,0:T(8,128)(2,1)S(1)}, u32[]{:S(2)}, u32[]{:S(2)}) collective-permute-start(bf16[128,512]{1,0:T(8,128)(2,1)S(1)} %get-tuple-element.111), channel_id=1, source_target_pairs={{0,28},{2,30},{8,4},{10,6},{16,12},{18,14},{24,20},{26,22},{1,29},... | collective-permute-start | bytes 393224 | tf_op jit(solution)/shard_map/ppermute | solution.py:643
  98.6 2.1 %fusion = bf16[256,4096]{1,0:T(8,128)(2,1)} fusion(bf16[48,256]{1,0:T(8,128)(2,1)S(1)} %get-tuple-element.107, bf16[48,4096]{1,0:T(8,128)(2,1)S(1)} %bitcast.70), kind=kOutput, calls=%fused_computation.1 | convolution fusion | flops 102760448 | bytes 2514944 | tf_op jit(solution)/shard_map/dot_general | solution.py:646
  101.3 4.9 %collective-permute-done.23.refs_1_ = bf16[68,1024]{1,0:T(8,128)(2,1)S(1)} collective-permute-done((bf16[68,1024]{1,0:T(8,128)(2,1)S(1)}, bf16[68,1024]{1,0:T(8,128)(2,1)S(1)}, u32[]{:S(2)}, u32[]{:S(2)}) %collective-permute-start.23) | collective-permute-done | bytes 139296 | tf_op jit(solution)/shard_map/ppermute | solution.py:330
  107.4 1.6 %collective-permute-done.25.two = bf16[68,2048]{1,0:T(8,128)(2,1)S(1)} collective-permute-done((bf16[68,2048]{1,0:T(8,128)(2,1)S(1)}, bf16[68,2048]{1,0:T(8,128)(2,1)S(1)}, u32[]{:S(2)}, u32[]{:S(2)}) %collective-permute-start.25) | collective-permute-done | bytes 278560 | tf_op jit(solution)/shard_map/ppermute | solution.py:330
  (65 shorter events, 9.1 us)
Async XLA Ops:
  3.9 7.4 %collective-permute-start.1 = (bf16[2,256,512]{2,1,0:T(8,128)(2,1)S(1)}, bf16[2,256,512]{2,1,0:T(8,128)(2,1)S(1)}, u32[]{:S(2)}, u32[]{:S(2)}) collective-permute-start(bf16[2,256,512]{2,1,0:T(8,128)(2,1)S(1)} %get-tuple-element.66.kv_own), channel_id=1, source_target_pairs={{0,2},{2,0},{4,6},{6,4},{8,10},{10,8},{12,14},{14,12},{16,18},{18,... | collective-permute-start | bytes 1572872 | tf_op jit(solution)/shard_map/ppermute | solution.py:330
  4.4 4.9 %collective-permute-start = (f32[48,256]{1,0:T(8,128)S(1)}, f32[48,256]{1,0:T(8,128)S(1)}, u32[]{:S(2)}, u32[]{:S(2)}) collective-permute-start(f32[48,256]{1,0:T(8,128)S(1)} %get-tuple-element.65), channel_id=1, source_target_pairs={{0,1},{1,0},{2,3},{3,2},{4,5},{5,4},{6,7},{7,6},{8,9},{9,8},{10,11... | collective-permute-start | bytes 147464 | tf_op jit(solution)/shard_map/ppermute | solution.py:330
  7.0 17.1 %collective-permute-start.2 = (bf16[2,256,512]{2,1,0:T(8,128)(2,1)S(1)}, bf16[2,256,512]{2,1,0:T(8,128)(2,1)S(1)}, u32[]{:S(2)}, u32[]{:S(2)}) collective-permute-start(bf16[2,256,512]{2,1,0:T(8,128)(2,1)S(1)} %get-tuple-element.66.kv_own), channel_id=1, source_target_pairs={{0,4},{2,6},{4,8},{6,10},{8,12},{10,14},{12,16},{14,18},{16,20},{1... | collective-permute-start | bytes 1572872 | tf_op jit(solution)/shard_map/ppermute | solution.py:335
  9.4 14.8 %collective-permute-start.3 = (bf16[32,256]{1,0:T(8,128)(2,1)S(1)}, bf16[32,256]{1,0:T(8,128)(2,1)S(1)}, u32[]{:S(2)}, u32[]{:S(2)}) collective-permute-start(bf16[32,256]{1,0:T(8,128)(2,1)S(1)} %slice.73), channel_id=1, source_target_pairs={{0,4},{2,6},{4,8},{6,10},{8,12},{10,14},{12,16},{14,18},{16,20},{1... | collective-permute-start | bytes 49160 | tf_op jit(solution)/shard_map/ppermute | solution.py:335
  24.1 2.0 %collective-permute-start.4 = (bf16[2,256,512]{2,1,0:T(8,128)(2,1)S(1)}, bf16[2,256,512]{2,1,0:T(8,128)(2,1)S(1)}, u32[]{:S(2)}, u32[]{:S(2)}) collective-permute-start(bf16[2,256,512]{2,1,0:T(8,128)(2,1)S(1)} %collective-permute-done.2.kv_pc), channel_id=1, source_target_pairs={{0,2},{2,0},{4,6},{6,4},{8,10},{10,8},{12,14},{14,12},{16,18},{18,... | collective-permute-start | bytes 1572872 | tf_op jit(solution)/shard_map/ppermute | solution.py:330
  40.2 4.3 %collective-permute-start.6 = (bf16[64,256]{1,0:T(8,128)(2,1)S(1)}, bf16[64,256]{1,0:T(8,128)(2,1)S(1)}, u32[]{:S(2)}, u32[]{:S(2)}) collective-permute-start(bf16[64,256]{1,0:T(8,128)(2,1)S(1)} %get-tuple-element.77), channel_id=1, source_target_pairs={{0,2},{2,0},{4,6},{6,4},{8,10},{10,8},{12,14},{14,12},{16,18},{18,... | collective-permute-start | bytes 98312 | tf_op jit(solution)/shard_map/ppermute | solution.py:330
  44.5 5.6 %collective-permute-start.8 = (bf16[2,2,256,512]{3,2,1,0:T(8,128)(2,1)S(1)}, bf16[2,2,256,512]{3,2,1,0:T(8,128)(2,1)S(1)}, u32[]{:S(2)}, u32[]{:S(2)}) collective-permute-start(bf16[2,2,256,512]{3,2,1,0:T(8,128)(2,1)S(1)} %get-tuple-element.83), channel_id=1, source_target_pairs={{0,2},{2,0},{4,6},{6,4},{8,10},{10,8},{12,14},{14,12},{16,18},{18,... | collective-permute-start | bytes 3145736 | tf_op jit(solution)/shard_map/ppermute | solution.py:330
  44.8 9.0 %collective-permute-start.10 = (bf16[32,256]{1,0:T(8,128)(2,1)S(1)}, bf16[32,256]{1,0:T(8,128)(2,1)S(1)}, u32[]{:S(2)}, u32[]{:S(2)}) collective-permute-start(bf16[32,256]{1,0:T(8,128)(2,1)S(1)} %get-tuple-element.85), channel_id=1, source_target_pairs={{0,29},{1,28},{2,31},{3,30},{4,1},{5,0},{6,3},{7,2},{8,5},{9,4},{1... | collective-permute-start | bytes 49160 | tf_op jit(solution)/shard_map/ppermute | solution.py:446
  46.6 7.3 %collective-permute-start.9 = (bf16[32,256]{1,0:T(8,128)(2,1)S(1)}, bf16[32,256]{1,0:T(8,128)(2,1)S(1)}, u32[]{:S(2)}, u32[]{:S(2)}) collective-permute-start(bf16[32,256]{1,0:T(8,128)(2,1)S(1)} %get-tuple-element.85), channel_id=1, source_target_pairs={{0,28},{2,30},{4,0},{6,2},{8,4},{10,6},{12,8},{14,10},{16,12},{18,... | collective-permute-start | bytes 49160 | tf_op jit(solution)/shard_map/ppermute | solution.py:335
  50.0 3.8 %collective-permute-start.7 = (bf16[48,256]{1,0:T(8,128)(2,1)S(1)}, bf16[48,256]{1,0:T(8,128)(2,1)S(1)}, u32[]{:S(2)}, u32[]{:S(2)}) collective-permute-start(bf16[48,256]{1,0:T(8,128)(2,1)S(1)} %get-tuple-element.81), channel_id=1, source_target_pairs={{0,1},{1,0},{2,3},{3,2},{4,5},{5,4},{6,7},{7,6},{8,9},{9,8},{10,11... | collective-permute-start | bytes 73736 | tf_op jit(solution)/shard_map/ppermute | solution.py:330
  54.4 4.6 %collective-permute-start.11 = (bf16[68,2048]{1,0:T(8,128)(2,1)S(1)}, bf16[68,2048]{1,0:T(8,128)(2,1)S(1)}, u32[]{:S(2)}, u32[]{:S(2)}) collective-permute-start(bf16[68,2048]{1,0:T(8,128)(2,1)S(1)} %get-tuple-element.88), channel_id=1, source_target_pairs={{0,2},{2,0},{4,6},{6,4},{8,10},{10,8},{12,14},{14,12},{16,18},{18,... | collective-permute-start | bytes 835592 | tf_op jit(solution)/shard_map/ppermute | solution.py:330
  54.5 7.9 %collective-permute-start.12 = (bf16[128,512]{1,0:T(8,128)(2,1)S(1)}, bf16[128,512]{1,0:T(8,128)(2,1)S(1)}, u32[]{:S(2)}, u32[]{:S(2)}) collective-permute-start(bf16[128,512]{1,0:T(8,128)(2,1)S(1)} %get-tuple-element.91), channel_id=1, source_target_pairs={{0,28},{2,30},{8,4},{10,6},{16,12},{18,14},{24,20},{26,22},{1,29},... | collective-permute-start | bytes 393224 | tf_op jit(solution)/shard_map/ppermute | solution.py:630
  62.4 10.4 %collective-permute-start.13 = (bf16[68,1024]{1,0:T(8,128)(2,1)S(1)}, bf16[68,1024]{1,0:T(8,128)(2,1)S(1)}, u32[]{:S(2)}, u32[]{:S(2)}) collective-permute-start(bf16[68,1024]{1,0:T(8,128)(2,1)S(1)} %get-tuple-element.93), channel_id=1, source_target_pairs={{0,4},{2,6},{4,0},{6,2},{8,12},{10,14},{12,8},{14,10},{16,20},{18,... | collective-permute-start | bytes 417800 | tf_op jit(solution)/shard_map/ppermute | solution.py:330
  62.9 9.9 %collective-permute-start.14 = (bf16[128,512]{1,0:T(8,128)(2,1)S(1)}, bf16[128,512]{1,0:T(8,128)(2,1)S(1)}, u32[]{:S(2)}, u32[]{:S(2)}) collective-permute-start(bf16[128,512]{1,0:T(8,128)(2,1)S(1)} %get-tuple-element.95), channel_id=1, source_target_pairs={{0,28},{2,30},{8,4},{10,6},{16,12},{18,14},{24,20},{26,22},{1,29},... | collective-permute-start | bytes 393224 | tf_op jit(solution)/shard_map/ppermute | solution.py:634
  72.9 12.9 %collective-permute-start.15 = (bf16[68,256]{1,0:T(8,128)(2,1)S(1)}, bf16[68,256]{1,0:T(8,128)(2,1)S(1)}, u32[]{:S(2)}, u32[]{:S(2)}) collective-permute-start(bf16[68,256]{1,0:T(8,128)(2,1)S(1)} %get-tuple-element.99), channel_id=1, source_target_pairs={{0,8},{2,10},{4,12},{6,14},{8,0},{10,2},{12,4},{14,6},{16,24},{18,... | collective-permute-start | bytes 104456 | tf_op jit(solution)/shard_map/ppermute | solution.py:330
  73.0 12.9 %collective-permute-start.16 = (bf16[68,256]{1,0:T(8,128)(2,1)S(1)}, bf16[68,256]{1,0:T(8,128)(2,1)S(1)}, u32[]{:S(2)}, u32[]{:S(2)}) collective-permute-start(bf16[68,256]{1,0:T(8,128)(2,1)S(1)} %get-tuple-element.100), channel_id=1, source_target_pairs={{0,16},{2,18},{4,20},{6,22},{8,24},{10,26},{12,28},{14,30},{16,0},... | collective-permute-start | bytes 104456 | tf_op jit(solution)/shard_map/ppermute | solution.py:330
  73.1 12.7 %collective-permute-start.17 = (bf16[68,256]{1,0:T(8,128)(2,1)S(1)}, bf16[68,256]{1,0:T(8,128)(2,1)S(1)}, u32[]{:S(2)}, u32[]{:S(2)}) collective-permute-start(bf16[68,256]{1,0:T(8,128)(2,1)S(1)} %get-tuple-element.101), channel_id=1, source_target_pairs={{0,24},{2,26},{4,28},{6,30},{8,16},{10,18},{12,20},{14,22},{16,8},... | collective-permute-start | bytes 104456 | tf_op jit(solution)/shard_map/ppermute | solution.py:330
  77.3 9.7 %collective-permute-start.18 = (bf16[128,512]{1,0:T(8,128)(2,1)S(1)}, bf16[128,512]{1,0:T(8,128)(2,1)S(1)}, u32[]{:S(2)}, u32[]{:S(2)}) collective-permute-start(bf16[128,512]{1,0:T(8,128)(2,1)S(1)} %get-tuple-element.104), channel_id=1, source_target_pairs={{0,28},{2,30},{8,4},{10,6},{16,12},{18,14},{24,20},{26,22},{1,29},... | collective-permute-start | bytes 393224 | tf_op jit(solution)/shard_map/ppermute | solution.py:637
  84.5 21.7 %collective-permute-start.24 = (bf16[2,256,512]{2,1,0:T(8,128)(2,1)S(1)}, bf16[2,256,512]{2,1,0:T(8,128)(2,1)S(1)}, u32[]{:S(2)}, u32[]{:S(2)}) collective-permute-start(bf16[2,256,512]{2,1,0:T(8,128)(2,1)S(1)} %fusion.1), channel_id=1, source_target_pairs={{4,0},{6,2},{12,8},{14,10},{20,16},{22,18},{28,24},{30,26},{5,1},{... | collective-permute-start | bytes 1572872 | tf_op jit(solution)/shard_map/ppermute | solution.py:638
  87.0 13.6 %collective-permute-start.21 = (bf16[68,256]{1,0:T(8,128)(2,1)S(1)}, bf16[68,256]{1,0:T(8,128)(2,1)S(1)}, u32[]{:S(2)}, u32[]{:S(2)}) collective-permute-start(bf16[68,256]{1,0:T(8,128)(2,1)S(1)} %add_convert_fusion.refs_0_), channel_id=1, source_target_pairs={{0,24},{2,26},{4,28},{6,30},{8,16},{10,18},{12,20},{14,22},{16,8},... | collective-permute-start | bytes 104456 | tf_op jit(solution)/shard_map/ppermute | solution.py:330
  87.0 13.6 %collective-permute-start.20 = (bf16[68,256]{1,0:T(8,128)(2,1)S(1)}, bf16[68,256]{1,0:T(8,128)(2,1)S(1)}, u32[]{:S(2)}, u32[]{:S(2)}) collective-permute-start(bf16[68,256]{1,0:T(8,128)(2,1)S(1)} %add_convert_fusion.refs_0_), channel_id=1, source_target_pairs={{0,16},{2,18},{4,20},{6,22},{8,24},{10,26},{12,28},{14,30},{16,0},... | collective-permute-start | bytes 104456 | tf_op jit(solution)/shard_map/ppermute | solution.py:330
  87.0 13.6 %collective-permute-start.19 = (bf16[68,256]{1,0:T(8,128)(2,1)S(1)}, bf16[68,256]{1,0:T(8,128)(2,1)S(1)}, u32[]{:S(2)}, u32[]{:S(2)}) collective-permute-start(bf16[68,256]{1,0:T(8,128)(2,1)S(1)} %add_convert_fusion.refs_0_), channel_id=1, source_target_pairs={{0,8},{2,10},{4,12},{6,14},{8,0},{10,2},{12,4},{14,6},{16,24},{18,... | collective-permute-start | bytes 104456 | tf_op jit(solution)/shard_map/ppermute | solution.py:330
  91.4 9.6 %collective-permute-start.22 = (bf16[128,512]{1,0:T(8,128)(2,1)S(1)}, bf16[128,512]{1,0:T(8,128)(2,1)S(1)}, u32[]{:S(2)}, u32[]{:S(2)}) collective-permute-start(bf16[128,512]{1,0:T(8,128)(2,1)S(1)} %get-tuple-element.111), channel_id=1, source_target_pairs={{0,28},{2,30},{8,4},{10,6},{16,12},{18,14},{24,20},{26,22},{1,29},... | collective-permute-start | bytes 393224 | tf_op jit(solution)/shard_map/ppermute | solution.py:643
  101.0 5.1 %collective-permute-start.23 = (bf16[68,1024]{1,0:T(8,128)(2,1)S(1)}, bf16[68,1024]{1,0:T(8,128)(2,1)S(1)}, u32[]{:S(2)}, u32[]{:S(2)}) collective-permute-start(bf16[68,1024]{1,0:T(8,128)(2,1)S(1)} %shard_map.142.refs_0_), channel_id=1, source_target_pairs={{0,4},{2,6},{4,0},{6,2},{8,12},{10,14},{12,8},{14,10},{16,20},{18,... | collective-permute-start | bytes 417800 | tf_op jit(solution)/shard_map/ppermute | solution.py:330
  (8 other events, 112.4 us)

commit v2 on v0

--- a/solution.py
+++ b/solution.py
@@ -28,54 +28,86 @@
     return lax.dot_general(left, right, dims, preferred_element_type=jnp.float32)
 
 
-def scores_and_softmax(head, low, diag, keys, values, q_ref, do_ref, term_ref, slot):
-    tokens = q_ref.shape[0]
-    s_ref, e_ref, ds_ref, inv_ref = slot
-    group, column, key_column = head
-    query = q_ref[:, column]
-    grad = do_ref[:, column]
-    term = term_ref[pl.ds(group[0], 1), :]
-    top = None
-    for block in range(low, len(keys)):
-        rows = slice(block * tokens, (block + 1) * tokens)
-        scores = mm(keys[block][:, key_column], query, NT)
-        if block == diag:
-            key_row = lax.broadcasted_iota(jnp.int32, (tokens, tokens), 0)
-            query_row = lax.broadcasted_iota(jnp.int32, (tokens, tokens), 1)
-            scores = jnp.where(key_row <= query_row, scores, masked_score)
-        s_ref[rows, :] = scores
-        here = jnp.max(scores.reshape(tokens // 8, 8, tokens), axis=0)
-        top = here if top is None else jnp.maximum(top, here)
-    top = jnp.max(top, axis=0, keepdims=True)
-    total = jnp.zeros((8, tokens), jnp.float32)
-    for block in range(low, len(keys)):
-        grad_probs = mm(values[block][:, key_column], grad, NT)
-        for at in range(0, tokens, CHUNK):
-            rows = slice(block * tokens + at, block * tokens + at + CHUNK)
-            weights = jnp.exp2((s_ref[rows, :] - top) * exp2_scale)
-            total = total + jnp.sum(weights.reshape(CHUNK // 8, 8, tokens), axis=0)
-            e_ref[rows, :] = weights.astype(jnp.bfloat16)
-            ds_ref[rows, :] = (weights * (grad_probs[at : at + CHUNK, :] - term)).astype(jnp.bfloat16)
-    inv_ref[...] = 1.0 / jnp.sum(total, axis=0, keepdims=True)
-
-
-def add_gradients(head, valid, low, high, rank, q_ref, do_ref, down, up_q, wk, dk_acc, dv_acc, slot):
-    tokens = q_ref.shape[0]
-    _, e_ref, ds_ref, inv_ref = slot
-    (_, group, inner), column, _ = head
-    height = wk.shape[1]
-    inverse = inv_ref[...] * valid
+def heads_in_flight(blocks, rank, coming, current, last, valid, keys, values, q, do, term_ref, down, up_q, wk, dk, dv):
+    tokens = q.shape[0]
+
+    (_, column, key_column), (s_new, _, _, top_new, _) = coming
+    query = q[:, column]
+
+    (numbers, now_column, now_key), (s_ref, e_ref, ds_ref, top_ref, inv_ref) = current
+    grad = do[:, now_column]
+    term = term_ref[pl.ds(numbers[0], 1), :]
+    top_now = top_ref[...]
+
+    ((_, group, inner), last_column, _), (_, e_old, ds_old, _, inv_old) = last
+    inverse = inv_old[...] * valid
     inverse_rows = jnp.broadcast_to(inverse, (HEAD_SIZE, tokens)).T
     scaled = inverse_rows * score_scale
     lane = lax.broadcasted_iota(jnp.int32, (tokens, HEAD_SIZE), 1) // rank
     own_columns = jnp.where(lane == inner, down[...].astype(jnp.float32), 0.0)
-    grad_n = (do_ref[:, column].astype(jnp.float32) * inverse_rows).astype(jnp.bfloat16)
+    grad_n = (do[:, last_column].astype(jnp.float32) * inverse_rows).astype(jnp.bfloat16)
     query_n = jnp.concatenate(
-        [q_ref[:, column].astype(jnp.float32) * scaled, own_columns * scaled], axis=1
+        [q[:, last_column].astype(jnp.float32) * scaled, own_columns * scaled], axis=1
     ).astype(jnp.bfloat16)
-    rows = pl.ds(pl.multiple_of(group * height + low, tokens), high - low)
-    dv_acc[rows, :] += mm(e_ref[low:high, :], grad_n)
-    dk_acc[rows, :] += mm(ds_ref[low:high, :], query_n)
+    own = pl.ds(pl.multiple_of(group * HEAD_SIZE + inner * rank, rank), rank)
+    base = pl.multiple_of(group * wk.shape[1], tokens)
+
+    top = None
+    total = jnp.zeros((8, tokens), jnp.float32)
+    back = None
+    for block in blocks:
+        rows = slice(block * tokens, (block + 1) * tokens)
+        top = merged_top(top, scores_block(block, keys[block][:, key_column], query, s_new, rows))
+
+        grad_probs = mm(values[block][:, now_key], grad, NT)
+        for at in range(0, tokens, CHUNK):
+            part = slice(block * tokens + at, block * tokens + at + CHUNK)
+            weights = jnp.exp2((s_ref[part, :] - top_now) * exp2_scale)
+            total = total + jnp.sum(weights.reshape(CHUNK // 8, 8, tokens), axis=0)
+            e_ref[part, :] = weights.astype(jnp.bfloat16)
+            ds_ref[part, :] = (weights * (grad_probs[at : at + CHUNK, :] - term)).astype(jnp.bfloat16)
+
+        to = pl.ds(base + block * tokens, tokens)
+        dv[to, :] += mm(e_old[rows, :], grad_n)
+        dk[to, :] += mm(ds_old[rows, :], query_n)
+        part = mm(wk[own, rows], ds_old[rows, :])
+        back = part if back is None else back + part
+    top_new[...] = jnp.max(top, axis=0, keepdims=True)
+    inv_ref[...] = 1.0 / jnp.sum(total, axis=0, keepdims=True)
+    up_q[...] += back * (inverse * score_scale)
+
+
+def merged_top(top, here):
+    return here if top is None else jnp.maximum(top, here)
+
+
+def scores_block(block, key, query, s_ref, rows):
+    tokens = query.shape[0]
+    scores = mm(key, query, NT)
+    if block == 1:
+        key_row = lax.broadcasted_iota(jnp.int32, (tokens, tokens), 0)
+        query_row = lax.broadcasted_iota(jnp.int32, (tokens, tokens), 1)
+        scores = jnp.where(key_row <= query_row, scores, masked_score)
+    s_ref[rows, :] = scores
+    return jnp.max(scores.reshape(tokens // 8, 8, tokens), axis=0)
+
+
+def last_gradients(blocks, rank, last, q, do, down, up_q, wk, dk, dv):
+    tokens = q.shape[0]
+    ((_, group, inner), column, _), (_, e_ref, ds_ref, _, inv_ref) = last
+    low, high = blocks[0] * tokens, (blocks[-1] + 1) * tokens
+    inverse = inv_ref[...]
+    inverse_rows = jnp.broadcast_to(inverse, (HEAD_SIZE, tokens)).T
+    scaled = inverse_rows * score_scale
+    lane = lax.broadcasted_iota(jnp.int32, (tokens, HEAD_SIZE), 1) // rank
+    own_columns = jnp.where(lane == inner, down[...].astype(jnp.float32), 0.0)
+    grad_n = (do[:, column].astype(jnp.float32) * inverse_rows).astype(jnp.bfloat16)
+    query_n = jnp.concatenate(
+        [q[:, column].astype(jnp.float32) * scaled, own_columns * scaled], axis=1
+    ).astype(jnp.bfloat16)
+    rows = pl.ds(pl.multiple_of(group * wk.shape[1] + low, tokens), high - low)
+    dv[rows, :] += mm(e_ref[low:high, :], grad_n)
+    dk[rows, :] += mm(ds_ref[low:high, :], query_n)
     own = pl.ds(pl.multiple_of(group * HEAD_SIZE + inner * rank, rank), rank)
     up_q[...] += mm(wk[own, low:high], ds_ref[low:high, :]) * (inverse * score_scale)
 
@@ -118,8 +150,8 @@
             ).astype(jnp.bfloat16)
     dk[...] = jnp.zeros_like(dk)
     dv[...] = jnp.zeros_like(dv)
-    slots = (buffers[:4], buffers[4:])
-    for _, e_ref, ds_ref, inv_ref in slots:
+    slots = (buffers[:5], buffers[5:])
+    for _, e_ref, ds_ref, _, inv_ref in slots:
         e_ref[...] = jnp.zeros_like(e_ref)
         ds_ref[...] = jnp.zeros_like(ds_ref)
         inv_ref[...] = jnp.zeros_like(inv_ref)
@@ -143,33 +175,48 @@
         )
 
     for which in range(2):
-        low = 1 - which
-
-        def softmax(i, slot):
-            scores_and_softmax(head_at(i), low, 1, keys, values, q, do, term, slot)
-
-        def gradients(i, slot):
-            valid = jnp.where((i >= 0) & (i < count), 1.0, 0.0).astype(jnp.float32)
-            add_gradients(
-                head_at(i), valid, low * tokens, height, rank, q, do, down, up_q, wk, dk, dv, slot
+        blocks = range(1 - which, len(keys))
+
+        def step(i, slot, other):
+            valid = jnp.where(i > 0, 1.0, 0.0).astype(jnp.float32)
+            heads_in_flight(
+                blocks, rank, (head_at(i + 1), other), (head_at(i), slot), (head_at(i - 1), other), valid,
+                keys, values, q, do, term, down, up_q, wk, dk, dv,
             )
+
+        def finish(slot):
+            last_gradients(blocks, rank, (head_at(count - 1), slot), q, do, down, up_q, wk, dk, dv)
 
         @pl.when((core == which) & (count > 0))
         def _():
+            held = wait_between(jnp.int32(0), head_at(0)[0][1])
+            s_ref, _, _, top_ref, _ = slots[0]
+            _, column, key_column = head_at(0)
+            top = None
+            for block in blocks:
+                rows = slice(block * tokens, (block + 1) * tokens)
+                top = merged_top(
+                    top, scores_block(block, keys[block][:, key_column], q[:, column], s_ref, rows)
+                )
+            top_ref[...] = jnp.max(top, axis=0, keepdims=True)
+
             def two(t, held):
-                held = wait_between(held, head_at(2 * t + 1)[0][1])
-                softmax(2 * t, slots[0])
-                gradients(2 * t - 1, slots[1])
-                softmax(2 * t + 1, slots[1])
-                gradients(2 * t, slots[0])
+                held = wait_between(held, head_at(2 * t + 2)[0][1])
+                step(2 * t, *slots)
+                step(2 * t + 1, *slots[::-1])
                 return held
 
-            held = lax.fori_loop(0, (count + 1) // 2, two, jnp.int32(0))
+            held = lax.fori_loop(0, count // 2, two, held)
             wait_between(held, jnp.int32(groups - 1))
+
+            @pl.when(count % 2 == 1)
+            def _():
+                step(count - 1, *slots)
+                finish(slots[0])
 
             @pl.when(count % 2 == 0)
             def _():
-                gradients(count - 1, slots[1])
+                finish(slots[1])
 
     @pl.when(count == 0)
     def _():
@@ -253,6 +300,7 @@
             pltpu.VMEM((rows, tokens), bf16),
             pltpu.VMEM((rows, tokens), bf16),
             pltpu.VMEM((1, tokens), f32),
+            pltpu.VMEM((1, tokens), f32),
         ]
         return [
             pltpu.SMEM((kv_local * per_kv + 1,), jnp.int32),

time: 93 us -> 91.3 us (0.982)
  waiting for transfers between devices: 32.4 us -> 30.5 us
    ppermute x4, starting transfers between devices: 6.15 us -> 8.91 us  [moved(): lax.ppermute(value, axis, [(i, (i + by) % count) for i in range(count)])]
    ppermute x17, starting transfers between devices: 20.1 us -> 17.9 us  [exchanged(): lax.ppermute(value, axis, [(i, i ^ bit) for i in range(lax.axis_size(axis...]
    ppermute x17, waiting for transfers between devices: 24.2 us -> 22.7 us  [exchanged(): lax.ppermute(value, axis, [(i, i ^ bit) for i in range(lax.axis_size(axis...]
    ppermute x1, waiting for transfers between devices: 1.92 us -> 0.42 us  [up_terms(): lax.ppermute(previous, ('seq', 'head'), pairs)]
    ppermute x4, waiting for transfers between devices: 6.24 us -> 7.33 us  [moved(): lax.ppermute(value, axis, [(i, (i + by) % count) for i in range(count)])]
  transfers between devices with their start and end apart: 22 -> 22, of which waited for: 13 -> 13; matrix products, arithmetic and copies ran while one was open for 3% -> 3% of each run, Pallas kernels for 10% -> 9%
where the time goes in v2:
time: 91.3 us; the launch traced here: 91.1 us
  waiting for transfers between devices  30.5 us (33%)
  starting transfers between devices  29.5 us (32%)
  Pallas kernels  26.8 us (29%)
  matrix products  2.05 us (2%)
  other arithmetic  1.26 us (1%)
    ppermute x17, waiting for transfers between devices, exchanged(): lax.ppermute(value, axis, [(i, i ^ bit) for i in range(lax.axis_size(axis...  22.7 us
    pallas_call x2, Pallas kernels, call(): pl.pallas_call(functools.partial(kernel, per_kv, rank), in_specs=[smem, h...  21.7 us
    ppermute x17, starting transfers between devices, exchanged(): lax.ppermute(value, axis, [(i, i ^ bit) for i in range(lax.axis_size(axis...  17.9 us
    ppermute x4, starting transfers between devices, moved(): lax.ppermute(value, axis, [(i, (i + by) % count) for i in range(count)])  8.91 us
    ppermute x4, waiting for transfers between devices, moved(): lax.ppermute(value, axis, [(i, (i + by) % count) for i in range(count)])  7.33 us
    pallas_call x1, Pallas kernels, projected_and_stacked(): pl.pallas_call(kernel, grid=(steps,), in_specs=[columns(rows, width), col...  3.22 us
    ppermute x1, starting transfers between devices, up_terms(): lax.ppermute(previous, ('seq', 'head'), pairs)  2.74 us
    dot_general x1, matrix products, per_device(): lax.dot_general(up_low, flattened_down, (((0,), (0,)), ((), ())), preferr...  2.05 us
  transfers between devices with their start and end apart: 22, of which 13 were waited for; matrix products, arithmetic and copies ran while one was open for 3% of the time, Pallas kernels for 9%

profile of v2, /device:TPU:0, one launch (start us, length us, event | category | flops | bytes accessed | tf_op | source)
XLA Modules:
  0.0 91.1 jit_solution(18322007144218308288)
XLA Ops:
  0.7 3.2 %shard_map.137 = (f32[48,256]{1,0:T(8,128)S(1)}, bf16[2,256,512]{2,1,0:T(8,128)(2,1)S(1)}) custom-call(bf16[48,4096]{1,0:T(8,128)(2,1)} %bitcast.18, bf16[256,4096]{1,0:T(8,128)(2,1)} %refs_4_.1, bf16[256,512]{1,0:T(8,128)(2,1)} %key.1, bf16[256,512]{1,0:T(8,128)(2,1)} %value.1), custom_call_target="tpu_custom_call" | custom-call | tf_op jit(solution)/shard_map/pallas_call | solution.py:440
  4.4 2.6 %collective-permute-start = (f32[48,256]{1,0:T(8,128)S(1)}, f32[48,256]{1,0:T(8,128)S(1)}, u32[]{:S(2)}, u32[]{:S(2)}) collective-permute-start(f32[48,256]{1,0:T(8,128)S(1)} %get-tuple-element.46), channel_id=1, source_target_pairs={{0,1},{1,0},{2,3},{3,2},{4,5},{5,4},{6,7},{7,6},{8,9},{9,8},{10,11... | collective-permute-start | bytes 147464 | tf_op jit(solution)/shard_map/ppermute | solution.py:378
  7.0 1.5 %collective-permute-start.2 = (bf16[2,256,512]{2,1,0:T(8,128)(2,1)S(1)}, bf16[2,256,512]{2,1,0:T(8,128)(2,1)S(1)}, u32[]{:S(2)}, u32[]{:S(2)}) collective-permute-start(bf16[2,256,512]{2,1,0:T(8,128)(2,1)S(1)} %get-tuple-element.47.kv_own), channel_id=1, source_target_pairs={{0,4},{2,6},{4,8},{6,10},{8,12},{10,14},{12,16},{14,18},{16,20},{1... | collective-permute-start | bytes 1572872 | tf_op jit(solution)/shard_map/ppermute | solution.py:383
  9.4 1.8 %collective-permute-start.3 = (bf16[32,256]{1,0:T(8,128)(2,1)S(1)}, bf16[32,256]{1,0:T(8,128)(2,1)S(1)}, u32[]{:S(2)}, u32[]{:S(2)}) collective-permute-start(bf16[32,256]{1,0:T(8,128)(2,1)S(1)} %slice.25), channel_id=1, source_target_pairs={{0,4},{2,6},{4,8},{6,10},{8,12},{10,14},{12,16},{14,18},{16,20},{1... | collective-permute-start | bytes 49160 | tf_op jit(solution)/shard_map/ppermute | solution.py:383
  11.3 7.3 %own_chip_heads.1 = (f32[16,256]{1,0:T(8,128)S(1)}, f32[2048,256]{1,0:T(8,128)S(1)}, f32[2048,128]{1,0:T(8,128)S(1)}) custom-call(s32[32]{0:T(128)S(1)} %copy-done.4, bf16[256,4096]{1,0:T(8,128)(2,1)} %q.3, bf16[256,4096]{1,0:T(8,128)(2,1)} %do.3, f32[32,256]{1,0:T(8,128)S(1)} %copy-done.2, bf16[16,4096]{1,0:T(8,128)(2,1)S(1)} %copy-done.1, ...), custom_call_target="tpu_custom_call" | custom-call | flops 10737418240 | bytes 6291456 | tf_op jit(solution)/shard_map/own_chip_heads/pallas_call | solution.py:315
  18.7 5.5 %collective-permute-done.3 = bf16[32,256]{1,0:T(8,128)(2,1)S(1)} collective-permute-done((bf16[32,256]{1,0:T(8,128)(2,1)S(1)}, bf16[32,256]{1,0:T(8,128)(2,1)S(1)}, u32[]{:S(2)}, u32[]{:S(2)}) %collective-permute-start.3) | collective-permute-done | bytes 16416 | tf_op jit(solution)/shard_map/ppermute | solution.py:383
  24.7 1.4 %collective-permute-done.5 = bf16[64,256]{1,0:T(8,128)(2,1)S(1)} collective-permute-done((bf16[64,256]{1,0:T(8,128)(2,1)S(1)}, bf16[64,256]{1,0:T(8,128)(2,1)S(1)}, u32[]{:S(2)}, u32[]{:S(2)}) %collective-permute-start.5) | collective-permute-done | bytes 32800 | tf_op jit(solution)/shard_map/ppermute | solution.py:378
  26.1 14.4 %previous_chip_heads.1 = (f32[2,256,512]{2,1,0:T(8,128)S(1)}, f32[2,256,512]{2,1,0:T(8,128)S(1)}, bf16[2,2,256,512]{3,2,1,0:T(8,128)(2,1)S(1)}, f32[16,256]{1,0:...) custom-call(s32[32]{0:T(128)S(1)} %copy-done.4, ...), custom_call_target="tpu_custom_call" | custom-call | flops 21474836480 | bytes 6291456 | tf_op jit(solution)/shard_map/previous_chip_heads/pallas_call | solution.py:315
  40.5 3.1 %collective-permute-start.6 = (bf16[64,256]{1,0:T(8,128)(2,1)S(1)}, bf16[64,256]{1,0:T(8,128)(2,1)S(1)}, u32[]{:S(2)}, u32[]{:S(2)}) collective-permute-start(bf16[64,256]{1,0:T(8,128)(2,1)S(1)} %get-tuple-element.58), channel_id=1, source_target_pairs={{0,2},{2,0},{4,6},{6,4},{8,10},{10,8},{12,14},{14,12},{16,18},{18,... | collective-permute-start | bytes 98312 | tf_op jit(solution)/shard_map/ppermute | solution.py:378
  45.3 2.7 %collective-permute-start.9 = (bf16[32,256]{1,0:T(8,128)(2,1)S(1)}, bf16[32,256]{1,0:T(8,128)(2,1)S(1)}, u32[]{:S(2)}, u32[]{:S(2)}) collective-permute-start(bf16[32,256]{1,0:T(8,128)(2,1)S(1)} %get-tuple-element.63), channel_id=1, source_target_pairs={{0,29},{1,28},{2,31},{3,30},{4,1},{5,0},{6,3},{7,2},{8,5},{9,4},{1... | collective-permute-start | bytes 49160 | tf_op jit(solution)/shard_map/ppermute | solution.py:494
  48.1 1.5 %collective-permute-start.8 = (bf16[32,256]{1,0:T(8,128)(2,1)S(1)}, bf16[32,256]{1,0:T(8,128)(2,1)S(1)}, u32[]{:S(2)}, u32[]{:S(2)}) collective-permute-start(bf16[32,256]{1,0:T(8,128)(2,1)S(1)} %get-tuple-element.63), channel_id=1, source_target_pairs={{0,28},{2,30},{4,0},{6,2},{8,4},{10,6},{12,8},{14,10},{16,12},{18,... | collective-permute-start | bytes 49160 | tf_op jit(solution)/shard_map/ppermute | solution.py:383
  50.0 1.8 %collective-permute-done.8.refs_2_ = bf16[32,256]{1,0:T(8,128)(2,1)S(1)} collective-permute-done((bf16[32,256]{1,0:T(8,128)(2,1)S(1)}, bf16[32,256]{1,0:T(8,128)(2,1)S(1)}, u32[]{:S(2)}, u32[]{:S(2)}) %collective-permute-start.8) | collective-permute-done | bytes 16416 | tf_op jit(solution)/shard_map/ppermute | solution.py:383
  52.4 1.6 %collective-permute-done.10.refs_1_ = bf16[68,2048]{1,0:T(8,128)(2,1)S(1)} collective-permute-done((bf16[68,2048]{1,0:T(8,128)(2,1)S(1)}, bf16[68,2048]{1,0:T(8,128)(2,1)S(1)}, u32[]{:S(2)}, u32[]{:S(2)}) %collective-permute-start.10) | collective-permute-done | bytes 278560 | tf_op jit(solution)/shard_map/ppermute | solution.py:378
  54.1 1.3 %collective-permute-start.11 = (bf16[68,1024]{1,0:T(8,128)(2,1)S(1)}, bf16[68,1024]{1,0:T(8,128)(2,1)S(1)}, u32[]{:S(2)}, u32[]{:S(2)}) collective-permute-start(bf16[68,1024]{1,0:T(8,128)(2,1)S(1)} %get-tuple-element.68), channel_id=1, source_target_pairs={{0,4},{2,6},{4,0},{6,2},{8,12},{10,14},{12,8},{14,10},{16,20},{18,... | collective-permute-start | bytes 417800 | tf_op jit(solution)/shard_map/ppermute | solution.py:378
  55.6 4.5 %collective-permute-done.11.refs_1_ = bf16[68,1024]{1,0:T(8,128)(2,1)S(1)} collective-permute-done((bf16[68,1024]{1,0:T(8,128)(2,1)S(1)}, bf16[68,1024]{1,0:T(8,128)(2,1)S(1)}, u32[]{:S(2)}, u32[]{:S(2)}) %collective-permute-start.11) | collective-permute-done | bytes 139296 | tf_op jit(solution)/shard_map/ppermute | solution.py:378
  60.2 3.5 %collective-permute-start.14 = (bf16[68,256]{1,0:T(8,128)(2,1)S(1)}, bf16[68,256]{1,0:T(8,128)(2,1)S(1)}, u32[]{:S(2)}, u32[]{:S(2)}) collective-permute-start(bf16[68,256]{1,0:T(8,128)(2,1)S(1)} %get-tuple-element.75), channel_id=1, source_target_pairs={{0,16},{2,18},{4,20},{6,22},{8,24},{10,26},{12,28},{14,30},{16,0},... | collective-permute-start | bytes 104456 | tf_op jit(solution)/shard_map/ppermute | solution.py:378
  64.6 4.2 %collective-permute-start.20 = (bf16[2,256,512]{2,1,0:T(8,128)(2,1)S(1)}, bf16[2,256,512]{2,1,0:T(8,128)(2,1)S(1)}, u32[]{:S(2)}, u32[]{:S(2)}) collective-permute-start(bf16[2,256,512]{2,1,0:T(8,128)(2,1)S(1)} %fusion.3), channel_id=1, source_target_pairs={{0,28},{2,30},{4,0},{6,2},{8,4},{10,6},{12,8},{14,10},{16,12},{18,... | collective-permute-start | bytes 1572872 | tf_op jit(solution)/shard_map/ppermute | solution.py:383
  68.8 1.2 %collective-permute-done.15 = bf16[68,256]{1,0:T(8,128)(2,1)S(1)} collective-permute-done((bf16[68,256]{1,0:T(8,128)(2,1)S(1)}, bf16[68,256]{1,0:T(8,128)(2,1)S(1)}, u32[]{:S(2)}, u32[]{:S(2)}) %collective-permute-start.15) | collective-permute-done | bytes 34848 | tf_op jit(solution)/shard_map/ppermute | solution.py:378
  70.5 4.0 %collective-permute-start.16 = (bf16[68,256]{1,0:T(8,128)(2,1)S(1)}, bf16[68,256]{1,0:T(8,128)(2,1)S(1)}, u32[]{:S(2)}, u32[]{:S(2)}) collective-permute-start(bf16[68,256]{1,0:T(8,128)(2,1)S(1)} %add_convert_fusion.refs_0_), channel_id=1, source_target_pairs={{0,8},{2,10},{4,12},{6,14},{8,0},{10,2},{12,4},{14,6},{16,24},{18,... | collective-permute-start | bytes 104456 | tf_op jit(solution)/shard_map/ppermute | solution.py:378
  74.5 2.0 %fusion = bf16[256,4096]{1,0:T(8,128)(2,1)} fusion(bf16[48,256]{1,0:T(8,128)(2,1)S(1)} %get-tuple-element.77, bf16[48,4096]{1,0:T(8,128)(2,1)S(1)} %bitcast.19), kind=kOutput, calls=%fused_computation.1 | convolution fusion | flops 102760448 | bytes 2514944 | tf_op jit(solution)/shard_map/dot_general | solution.py:685
  76.5 4.4 %collective-permute-done.18.refs_3_ = bf16[68,256]{1,0:T(8,128)(2,1)S(1)} collective-permute-done((bf16[68,256]{1,0:T(8,128)(2,1)S(1)}, bf16[68,256]{1,0:T(8,128)(2,1)S(1)}, u32[]{:S(2)}, u32[]{:S(2)}) %collective-permute-start.18) | collective-permute-done | bytes 34848 | tf_op jit(solution)/shard_map/ppermute | solution.py:378
  80.9 1.2 %collective-permute-done.17.refs_2_ = bf16[68,256]{1,0:T(8,128)(2,1)S(1)} collective-permute-done((bf16[68,256]{1,0:T(8,128)(2,1)S(1)}, bf16[68,256]{1,0:T(8,128)(2,1)S(1)}, u32[]{:S(2)}, u32[]{:S(2)}) %collective-permute-start.17) | collective-permute-done | bytes 34848 | tf_op jit(solution)/shard_map/ppermute | solution.py:378
  82.2 5.1 %collective-permute-done.19.refs_1_ = bf16[68,1024]{1,0:T(8,128)(2,1)S(1)} collective-permute-done((bf16[68,1024]{1,0:T(8,128)(2,1)S(1)}, bf16[68,1024]{1,0:T(8,128)(2,1)S(1)}, u32[]{:S(2)}, u32[]{:S(2)}) %collective-permute-start.19) | collective-permute-done | bytes 139296 | tf_op jit(solution)/shard_map/ppermute | solution.py:378
  88.5 1.6 %collective-permute-done.21.two = bf16[68,2048]{1,0:T(8,128)(2,1)S(1)} collective-permute-done((bf16[68,2048]{1,0:T(8,128)(2,1)S(1)}, bf16[68,2048]{1,0:T(8,128)(2,1)S(1)}, u32[]{:S(2)}, u32[]{:S(2)}) %collective-permute-start.21) | collective-permute-done | bytes 278560 | tf_op jit(solution)/shard_map/ppermute | solution.py:378
  (54 shorter events, 8.8 us)
Async XLA Ops:
  3.9 7.4 %collective-permute-start.1 = (bf16[2,256,512]{2,1,0:T(8,128)(2,1)S(1)}, bf16[2,256,512]{2,1,0:T(8,128)(2,1)S(1)}, u32[]{:S(2)}, u32[]{:S(2)}) collective-permute-start(bf16[2,256,512]{2,1,0:T(8,128)(2,1)S(1)} %get-tuple-element.47.kv_own), channel_id=1, source_target_pairs={{0,2},{2,0},{4,6},{6,4},{8,10},{10,8},{12,14},{14,12},{16,18},{18,... | collective-permute-start | bytes 1572872 | tf_op jit(solution)/shard_map/ppermute | solution.py:378
  4.4 4.9 %collective-permute-start = (f32[48,256]{1,0:T(8,128)S(1)}, f32[48,256]{1,0:T(8,128)S(1)}, u32[]{:S(2)}, u32[]{:S(2)}) collective-permute-start(f32[48,256]{1,0:T(8,128)S(1)} %get-tuple-element.46), channel_id=1, source_target_pairs={{0,1},{1,0},{2,3},{3,2},{4,5},{5,4},{6,7},{7,6},{8,9},{9,8},{10,11... | collective-permute-start | bytes 147464 | tf_op jit(solution)/shard_map/ppermute | solution.py:378
  7.0 17.1 %collective-permute-start.2 = (bf16[2,256,512]{2,1,0:T(8,128)(2,1)S(1)}, bf16[2,256,512]{2,1,0:T(8,128)(2,1)S(1)}, u32[]{:S(2)}, u32[]{:S(2)}) collective-permute-start(bf16[2,256,512]{2,1,0:T(8,128)(2,1)S(1)} %get-tuple-element.47.kv_own), channel_id=1, source_target_pairs={{0,4},{2,6},{4,8},{6,10},{8,12},{10,14},{12,16},{14,18},{16,20},{1... | collective-permute-start | bytes 1572872 | tf_op jit(solution)/shard_map/ppermute | solution.py:383
  9.4 14.8 %collective-permute-start.3 = (bf16[32,256]{1,0:T(8,128)(2,1)S(1)}, bf16[32,256]{1,0:T(8,128)(2,1)S(1)}, u32[]{:S(2)}, u32[]{:S(2)}) collective-permute-start(bf16[32,256]{1,0:T(8,128)(2,1)S(1)} %slice.25), channel_id=1, source_target_pairs={{0,4},{2,6},{4,8},{6,10},{8,12},{10,14},{12,16},{14,18},{16,20},{1... | collective-permute-start | bytes 49160 | tf_op jit(solution)/shard_map/ppermute | solution.py:383
  24.1 2.0 %collective-permute-start.4 = (bf16[2,256,512]{2,1,0:T(8,128)(2,1)S(1)}, bf16[2,256,512]{2,1,0:T(8,128)(2,1)S(1)}, u32[]{:S(2)}, u32[]{:S(2)}) collective-permute-start(bf16[2,256,512]{2,1,0:T(8,128)(2,1)S(1)} %collective-permute-done.2.kv_pc), channel_id=1, source_target_pairs={{0,2},{2,0},{4,6},{6,4},{8,10},{10,8},{12,14},{14,12},{16,18},{18,... | collective-permute-start | bytes 1572872 | tf_op jit(solution)/shard_map/ppermute | solution.py:378
  24.1 1.9 %collective-permute-start.5 = (bf16[64,256]{1,0:T(8,128)(2,1)S(1)}, bf16[64,256]{1,0:T(8,128)(2,1)S(1)}, u32[]{:S(2)}, u32[]{:S(2)}) collective-permute-start(bf16[64,256]{1,0:T(8,128)(2,1)S(1)} %pad_maximum_fusion.1), channel_id=1, source_target_pairs={{0,2},{2,0},{4,6},{6,4},{8,10},{10,8},{12,14},{14,12},{16,18},{18,... | collective-permute-start | bytes 98312 | tf_op jit(solution)/shard_map/ppermute | solution.py:378
  26.1 25.7 %copy-start = (bf16[256,4096]{1,0:T(8,128)(2,1)S(1)}, bf16[256,4096]{1,0:T(8,128)(2,1)}, u32[]{:S(2)}) copy-start(bf16[256,4096]{1,0:T(8,128)(2,1)} %refs_4_.1) | copy-start | bytes 6291460
  40.5 4.0 %collective-permute-start.6 = (bf16[64,256]{1,0:T(8,128)(2,1)S(1)}, bf16[64,256]{1,0:T(8,128)(2,1)S(1)}, u32[]{:S(2)}, u32[]{:S(2)}) collective-permute-start(bf16[64,256]{1,0:T(8,128)(2,1)S(1)} %get-tuple-element.58), channel_id=1, source_target_pairs={{0,2},{2,0},{4,6},{6,4},{8,10},{10,8},{12,14},{14,12},{16,18},{18,... | collective-permute-start | bytes 98312 | tf_op jit(solution)/shard_map/ppermute | solution.py:378
  44.5 10.9 %collective-permute-start.12 = (bf16[2,2,256,512]{3,2,1,0:T(8,128)(2,1)S(1)}, bf16[2,2,256,512]{3,2,1,0:T(8,128)(2,1)S(1)}, u32[]{:S(2)}, u32[]{:S(2)}) collective-permute-start(bf16[2,2,256,512]{3,2,1,0:T(8,128)(2,1)S(1)} %get-tuple-element.70), channel_id=1, source_target_pairs={{0,2},{2,0},{4,6},{6,4},{8,10},{10,8},{12,14},{14,12},{16,18},{18,... | collective-permute-start | bytes 3145736 | tf_op jit(solution)/shard_map/ppermute | solution.py:378
  44.8 7.0 %collective-permute-start.7 = (bf16[48,256]{1,0:T(8,128)(2,1)S(1)}, bf16[48,256]{1,0:T(8,128)(2,1)S(1)}, u32[]{:S(2)}, u32[]{:S(2)}) collective-permute-start(bf16[48,256]{1,0:T(8,128)(2,1)S(1)} %get-tuple-element.62), channel_id=1, source_target_pairs={{0,1},{1,0},{2,3},{3,2},{4,5},{5,4},{6,7},{7,6},{8,9},{9,8},{10,11... | collective-permute-start | bytes 73736 | tf_op jit(solution)/shard_map/ppermute | solution.py:378
  45.3 4.6 %collective-permute-start.9 = (bf16[32,256]{1,0:T(8,128)(2,1)S(1)}, bf16[32,256]{1,0:T(8,128)(2,1)S(1)}, u32[]{:S(2)}, u32[]{:S(2)}) collective-permute-start(bf16[32,256]{1,0:T(8,128)(2,1)S(1)} %get-tuple-element.63), channel_id=1, source_target_pairs={{0,29},{1,28},{2,31},{3,30},{4,1},{5,0},{6,3},{7,2},{8,5},{9,4},{1... | collective-permute-start | bytes 49160 | tf_op jit(solution)/shard_map/ppermute | solution.py:494
  48.1 3.7 %collective-permute-start.8 = (bf16[32,256]{1,0:T(8,128)(2,1)S(1)}, bf16[32,256]{1,0:T(8,128)(2,1)S(1)}, u32[]{:S(2)}, u32[]{:S(2)}) collective-permute-start(bf16[32,256]{1,0:T(8,128)(2,1)S(1)} %get-tuple-element.63), channel_id=1, source_target_pairs={{0,28},{2,30},{4,0},{6,2},{8,4},{10,6},{12,8},{14,10},{16,12},{18,... | collective-permute-start | bytes 49160 | tf_op jit(solution)/shard_map/ppermute | solution.py:383
  52.3 22.1 %copy-start.5 = (bf16[3,16,4096]{2,1,0:T(8,128)(2,1)S(1)}, bf16[3,16,4096]{2,1,0:T(8,128)(2,1)}, u32[]{:S(2)}) copy-start(bf16[3,16,4096]{2,1,0:T(8,128)(2,1)} %param.17) | copy-start | bytes 1179652
  52.4 1.6 %collective-permute-start.10 = (bf16[68,2048]{1,0:T(8,128)(2,1)S(1)}, bf16[68,2048]{1,0:T(8,128)(2,1)S(1)}, u32[]{:S(2)}, u32[]{:S(2)}) collective-permute-start(bf16[68,2048]{1,0:T(8,128)(2,1)S(1)} %get-tuple-element.66), channel_id=1, source_target_pairs={{0,2},{2,0},{4,6},{6,4},{8,10},{10,8},{12,14},{14,12},{16,18},{18,... | collective-permute-start | bytes 835592 | tf_op jit(solution)/shard_map/ppermute | solution.py:378
  54.1 6.0 %collective-permute-start.11 = (bf16[68,1024]{1,0:T(8,128)(2,1)S(1)}, bf16[68,1024]{1,0:T(8,128)(2,1)S(1)}, u32[]{:S(2)}, u32[]{:S(2)}) collective-permute-start(bf16[68,1024]{1,0:T(8,128)(2,1)S(1)} %get-tuple-element.68), channel_id=1, source_target_pairs={{0,4},{2,6},{4,0},{6,2},{8,12},{10,14},{12,8},{14,10},{16,20},{18,... | collective-permute-start | bytes 417800 | tf_op jit(solution)/shard_map/ppermute | solution.py:378
  60.2 8.6 %collective-permute-start.13 = (bf16[68,256]{1,0:T(8,128)(2,1)S(1)}, bf16[68,256]{1,0:T(8,128)(2,1)S(1)}, u32[]{:S(2)}, u32[]{:S(2)}) collective-permute-start(bf16[68,256]{1,0:T(8,128)(2,1)S(1)} %get-tuple-element.74), channel_id=1, source_target_pairs={{0,8},{2,10},{4,12},{6,14},{8,0},{10,2},{12,4},{14,6},{16,24},{18,... | collective-permute-start | bytes 104456 | tf_op jit(solution)/shard_map/ppermute | solution.py:378
  60.2 8.5 %collective-permute-start.14 = (bf16[68,256]{1,0:T(8,128)(2,1)S(1)}, bf16[68,256]{1,0:T(8,128)(2,1)S(1)}, u32[]{:S(2)}, u32[]{:S(2)}) collective-permute-start(bf16[68,256]{1,0:T(8,128)(2,1)S(1)} %get-tuple-element.75), channel_id=1, source_target_pairs={{0,16},{2,18},{4,20},{6,22},{8,24},{10,26},{12,28},{14,30},{16,0},... | collective-permute-start | bytes 104456 | tf_op jit(solution)/shard_map/ppermute | solution.py:378
  63.8 6.2 %collective-permute-start.15 = (bf16[68,256]{1,0:T(8,128)(2,1)S(1)}, bf16[68,256]{1,0:T(8,128)(2,1)S(1)}, u32[]{:S(2)}, u32[]{:S(2)}) collective-permute-start(bf16[68,256]{1,0:T(8,128)(2,1)S(1)} %get-tuple-element.76), channel_id=1, source_target_pairs={{0,24},{2,26},{4,28},{6,30},{8,16},{10,18},{12,20},{14,22},{16,8},... | collective-permute-start | bytes 104456 | tf_op jit(solution)/shard_map/ppermute | solution.py:378
  64.6 22.8 %collective-permute-start.20 = (bf16[2,256,512]{2,1,0:T(8,128)(2,1)S(1)}, bf16[2,256,512]{2,1,0:T(8,128)(2,1)S(1)}, u32[]{:S(2)}, u32[]{:S(2)}) collective-permute-start(bf16[2,256,512]{2,1,0:T(8,128)(2,1)S(1)} %fusion.3), channel_id=1, source_target_pairs={{0,28},{2,30},{4,0},{6,2},{8,4},{10,6},{12,8},{14,10},{16,12},{18,... | collective-permute-start | bytes 1572872 | tf_op jit(solution)/shard_map/ppermute | solution.py:383
  70.0 10.9 %collective-permute-start.18 = (bf16[68,256]{1,0:T(8,128)(2,1)S(1)}, bf16[68,256]{1,0:T(8,128)(2,1)S(1)}, u32[]{:S(2)}, u32[]{:S(2)}) collective-permute-start(bf16[68,256]{1,0:T(8,128)(2,1)S(1)} %add_convert_fusion.refs_0_), channel_id=1, source_target_pairs={{0,24},{2,26},{4,28},{6,30},{8,16},{10,18},{12,20},{14,22},{16,8},... | collective-permute-start | bytes 104456 | tf_op jit(solution)/shard_map/ppermute | solution.py:378
  70.5 11.7 %collective-permute-start.17 = (bf16[68,256]{1,0:T(8,128)(2,1)S(1)}, bf16[68,256]{1,0:T(8,128)(2,1)S(1)}, u32[]{:S(2)}, u32[]{:S(2)}) collective-permute-start(bf16[68,256]{1,0:T(8,128)(2,1)S(1)} %add_convert_fusion.refs_0_), channel_id=1, source_target_pairs={{0,16},{2,18},{4,20},{6,22},{8,24},{10,26},{12,28},{14,30},{16,0},... | collective-permute-start | bytes 104456 | tf_op jit(solution)/shard_map/ppermute | solution.py:378
  70.5 11.7 %collective-permute-start.16 = (bf16[68,256]{1,0:T(8,128)(2,1)S(1)}, bf16[68,256]{1,0:T(8,128)(2,1)S(1)}, u32[]{:S(2)}, u32[]{:S(2)}) collective-permute-start(bf16[68,256]{1,0:T(8,128)(2,1)S(1)} %add_convert_fusion.refs_0_), channel_id=1, source_target_pairs={{0,8},{2,10},{4,12},{6,14},{8,0},{10,2},{12,4},{14,6},{16,24},{18,... | collective-permute-start | bytes 104456 | tf_op jit(solution)/shard_map/ppermute | solution.py:378
  82.2 5.2 %collective-permute-start.19 = (bf16[68,1024]{1,0:T(8,128)(2,1)S(1)}, bf16[68,1024]{1,0:T(8,128)(2,1)S(1)}, u32[]{:S(2)}, u32[]{:S(2)}) collective-permute-start(bf16[68,1024]{1,0:T(8,128)(2,1)S(1)} %shard_map.142.refs_0_), channel_id=1, source_target_pairs={{0,4},{2,6},{4,0},{6,2},{8,12},{10,14},{12,8},{14,10},{16,20},{18,... | collective-permute-start | bytes 417800 | tf_op jit(solution)/shard_map/ppermute | solution.py:378
  88.5 1.6 %collective-permute-start.21 = (bf16[68,2048]{1,0:T(8,128)(2,1)S(1)}, bf16[68,2048]{1,0:T(8,128)(2,1)S(1)}, u32[]{:S(2)}, u32[]{:S(2)}) collective-permute-start(bf16[68,2048]{1,0:T(8,128)(2,1)S(1)} %shard_map.143.one), channel_id=1, source_target_pairs={{0,2},{2,0},{4,6},{6,4},{8,10},{10,8},{12,14},{14,12},{16,18},{18,... | collective-permute-start | bytes 835592 | tf_op jit(solution)/shard_map/ppermute | solution.py:378
  (4 other events, 46.9 us)

commit v3 on v2

--- a/solution.py
+++ b/solution.py
@@ -12,6 +12,7 @@
 GROUP = 1024
 SHIFT = 512
 CHUNK = 32
+CUT_WORK = 5 * 10**9
 SMALL_VMEM = 8 * 1024 * 1024
 VMEM_LIMIT = 32 * 1024 * 1024
 
@@ -151,10 +152,10 @@
     dk[...] = jnp.zeros_like(dk)
     dv[...] = jnp.zeros_like(dv)
     slots = (buffers[:5], buffers[5:])
-    for _, e_ref, ds_ref, _, inv_ref in slots:
-        e_ref[...] = jnp.zeros_like(e_ref)
-        ds_ref[...] = jnp.zeros_like(ds_ref)
-        inv_ref[...] = jnp.zeros_like(inv_ref)
+    _, e_ref, ds_ref, _, inv_ref = slots[1]
+    e_ref[...] = jnp.zeros_like(e_ref)
+    ds_ref[...] = jnp.zeros_like(ds_ref)
+    inv_ref[...] = jnp.zeros_like(inv_ref)
     wait(0)
     index = lax.axis_index("seq")
     core = index % 2
@@ -391,7 +392,7 @@
     return value
 
 
-def small_call(kernel, out_shape, *args, scratch=(), limit=1):
+def small_call(kernel, out_shape, *args, scratch=(), limit=1, work=0):
     vmem = pl.BlockSpec(memory_space=pltpu.VMEM)
     return pl.pallas_call(
         kernel,
@@ -400,6 +401,7 @@
         out_shape=out_shape,
         scratch_shapes=list(scratch),
         compiler_params=pltpu.CompilerParams(vmem_limit_bytes=limit * SMALL_VMEM),
+        cost_estimate=pl.CostEstimate(flops=work, bytes_accessed=1 << 20, transcendentals=0),
     )(*args)
 
 
@@ -541,7 +543,7 @@
     return [pieces[0]] + [exchanged(p, "seq", d * unit) for d, p in enumerate(pieces) if d]
 
 
-def summed_and_cut(pieces, unit, radix):
+def summed_and_cut(pieces, unit, radix, work=0):
     rows, whole = pieces[0].shape
     wide = whole // radix
     if wide % HEAD_SIZE:
@@ -563,6 +565,7 @@
         [jax.ShapeDtypeStruct((rows, wide), jnp.bfloat16)] * radix,
         *pieces,
         scratch=[pltpu.VMEM((rows, whole), jnp.float32)],
+        work=work,
     )
 
 
@@ -670,13 +673,15 @@
     received = exchanged(send, "seq", 1)
     terms = up_terms(*up_sums(up_q, up_keep, up_received))
     back = (keep_pc + received[1].astype(jnp.float32)).astype(jnp.bfloat16)
+    terms[1], back = lax.optimization_barrier((terms[1], back))
     up_low, *pieces = weight_halves(terms, inputs, grad_up, scale)
-    pieces = exchanged_pieces(summed_and_cut(exchanged_pieces(pieces, 1), 2, 2), 2)
-    pieces, back = lax.optimization_barrier((pieces, back))
+    pieces, back = lax.optimization_barrier((summed_and_cut(exchanged_pieces(pieces, 1), 2, 2), back))
+    pieces = exchanged_pieces(pieces, 2)
     back = moved(back, "seq", -2)
     for level in range(1, levels):
-        pieces = exchanged_pieces(summed_and_cut(pieces, 4**level, 4), 4**level)
+        pieces = exchanged_pieces(summed_and_cut(pieces, 4**level, 4, CUT_WORK), 4**level)
     total = sum(p.astype(jnp.float32) for p in pieces).astype(jnp.bfloat16)
+    total, back = lax.optimization_barrier((total, back))
     key_value_gradient = (
         keep_own + received[0].astype(jnp.float32) + back.astype(jnp.float32)
     ).astype(jnp.bfloat16)

time: 91.3 us -> 93.7 us (1.026)
  waiting for transfers between devices: 30.5 us -> 33.1 us
    ppermute x17, waiting for transfers between devices: 22.7 us -> 27.6 us  [exchanged(): lax.ppermute(value, axis, [(i, i ^ bit) for i in range(lax.axis_size(axis...]
    ppermute x17, starting transfers between devices: 17.9 us -> 19.7 us  [exchanged(): lax.ppermute(value, axis, [(i, i ^ bit) for i in range(lax.axis_size(axis...]
    ppermute x4, waiting for transfers between devices: 7.33 us -> 5.5 us  [moved(): lax.ppermute(value, axis, [(i, (i + by) % count) for i in range(count)])]
    ppermute x1, starting transfers between devices: 2.74 us -> 1.75 us  [up_terms(): lax.ppermute(previous, ('seq', 'head'), pairs)]
  transfers between devices with their start and end apart: 22 -> 22, of which waited for: 13 -> 12; matrix products, arithmetic and copies ran while one was open for 3% -> 4% of each run, Pallas kernels for 9% -> 8%
where the time goes in v3:
time: 93.7 us; the launch traced here: 93.8 us
  waiting for transfers between devices  33.1 us (35%)
  starting transfers between devices  30.4 us (32%)
  Pallas kernels  26 us (28%)
  matrix products  2.05 us (2%)
  other arithmetic  1.28 us (1%)
    ppermute x17, waiting for transfers between devices, exchanged(): lax.ppermute(value, axis, [(i, i ^ bit) for i in range(lax.axis_size(axis...  27.6 us
    pallas_call x2, Pallas kernels, call(): pl.pallas_call(functools.partial(kernel, per_kv, rank), in_specs=[smem, h...  20.9 us
    ppermute x17, starting transfers between devices, exchanged(): lax.ppermute(value, axis, [(i, i ^ bit) for i in range(lax.axis_size(axis...  19.7 us
    ppermute x4, starting transfers between devices, moved(): lax.ppermute(value, axis, [(i, (i + by) % count) for i in range(count)])  8.88 us
    ppermute x4, waiting for transfers between devices, moved(): lax.ppermute(value, axis, [(i, (i + by) % count) for i in range(count)])  5.5 us
    pallas_call x1, Pallas kernels, projected_and_stacked(): pl.pallas_call(kernel, grid=(steps,), in_specs=[columns(rows, width), col...  3.22 us
    dot_general x1, matrix products, per_device(): lax.dot_general(up_low, flattened_down, (((0,), (0,)), ((), ())), preferr...  2.05 us
  transfers between devices with their start and end apart: 22, of which 12 were waited for; matrix products, arithmetic and copies ran while one was open for 4% of the time, Pallas kernels for 8%

profile of v3, /device:TPU:0, one launch (start us, length us, event | category | flops | bytes accessed | tf_op | source)
XLA Modules:
  0.0 93.8 jit_solution(8013869374073469826)
XLA Ops:
  0.7 3.2 %shard_map.137 = (f32[48,256]{1,0:T(8,128)S(1)}, bf16[2,256,512]{2,1,0:T(8,128)(2,1)S(1)}) custom-call(bf16[48,4096]{1,0:T(8,128)(2,1)} %bitcast.18, bf16[256,4096]{1,0:T(8,128)(2,1)} %refs_4_.1, bf16[256,512]{1,0:T(8,128)(2,1)} %key.1, bf16[256,512]{1,0:T(8,128)(2,1)} %value.1), custom_call_target="tpu_custom_call" | custom-call | tf_op jit(solution)/shard_map/pallas_call | solution.py:442
  4.4 2.6 %collective-permute-start = (f32[48,256]{1,0:T(8,128)S(1)}, f32[48,256]{1,0:T(8,128)S(1)}, u32[]{:S(2)}, u32[]{:S(2)}) collective-permute-start(f32[48,256]{1,0:T(8,128)S(1)} %get-tuple-element.50), channel_id=1, source_target_pairs={{0,1},{1,0},{2,3},{3,2},{4,5},{5,4},{6,7},{7,6},{8,9},{9,8},{10,11... | collective-permute-start | bytes 147464 | tf_op jit(solution)/shard_map/ppermute | solution.py:379
  7.0 1.5 %collective-permute-start.2 = (bf16[2,256,512]{2,1,0:T(8,128)(2,1)S(1)}, bf16[2,256,512]{2,1,0:T(8,128)(2,1)S(1)}, u32[]{:S(2)}, u32[]{:S(2)}) collective-permute-start(bf16[2,256,512]{2,1,0:T(8,128)(2,1)S(1)} %get-tuple-element.51.kv_own), channel_id=1, source_target_pairs={{0,4},{2,6},{4,8},{6,10},{8,12},{10,14},{12,16},{14,18},{16,20},{1... | collective-permute-start | bytes 1572872 | tf_op jit(solution)/shard_map/ppermute | solution.py:384
  9.4 1.8 %collective-permute-start.3 = (bf16[32,256]{1,0:T(8,128)(2,1)S(1)}, bf16[32,256]{1,0:T(8,128)(2,1)S(1)}, u32[]{:S(2)}, u32[]{:S(2)}) collective-permute-start(bf16[32,256]{1,0:T(8,128)(2,1)S(1)} %slice.25), channel_id=1, source_target_pairs={{0,4},{2,6},{4,8},{6,10},{8,12},{10,14},{12,16},{14,18},{16,20},{1... | collective-permute-start | bytes 49160 | tf_op jit(solution)/shard_map/ppermute | solution.py:384
  11.3 7.3 %own_chip_heads.1 = (f32[16,256]{1,0:T(8,128)S(1)}, f32[2048,256]{1,0:T(8,128)S(1)}, f32[2048,128]{1,0:T(8,128)S(1)}) custom-call(s32[32]{0:T(128)S(1)} %copy-done.4, bf16[256,4096]{1,0:T(8,128)(2,1)} %q.3, bf16[256,4096]{1,0:T(8,128)(2,1)} %do.3, f32[32,256]{1,0:T(8,128)S(1)} %copy-done.2, bf16[16,4096]{1,0:T(8,128)(2,1)S(1)} %copy-done.1, ...), custom_call_target="tpu_custom_call" | custom-call | flops 10737418240 | bytes 6291456 | tf_op jit(solution)/shard_map/own_chip_heads/pallas_call | solution.py:316
  18.6 5.5 %collective-permute-done.3 = bf16[32,256]{1,0:T(8,128)(2,1)S(1)} collective-permute-done((bf16[32,256]{1,0:T(8,128)(2,1)S(1)}, bf16[32,256]{1,0:T(8,128)(2,1)S(1)}, u32[]{:S(2)}, u32[]{:S(2)}) %collective-permute-start.3) | collective-permute-done | bytes 16416 | tf_op jit(solution)/shard_map/ppermute | solution.py:384
  24.7 1.4 %collective-permute-done.5 = bf16[64,256]{1,0:T(8,128)(2,1)S(1)} collective-permute-done((bf16[64,256]{1,0:T(8,128)(2,1)S(1)}, bf16[64,256]{1,0:T(8,128)(2,1)S(1)}, u32[]{:S(2)}, u32[]{:S(2)}) %collective-permute-start.5) | collective-permute-done | bytes 32800 | tf_op jit(solution)/shard_map/ppermute | solution.py:379
  26.1 13.6 %previous_chip_heads.1 = (f32[2,256,512]{2,1,0:T(8,128)S(1)}, f32[2,256,512]{2,1,0:T(8,128)S(1)}, bf16[2,2,256,512]{3,2,1,0:T(8,128)(2,1)S(1)}, f32[16,256]{1,0:...) custom-call(s32[32]{0:T(128)S(1)} %copy-done.4, ...), custom_call_target="tpu_custom_call" | custom-call | flops 21474836480 | bytes 6291456 | tf_op jit(solution)/shard_map/previous_chip_heads/pallas_call | solution.py:316
  39.7 2.9 %collective-permute-start.6 = (bf16[64,256]{1,0:T(8,128)(2,1)S(1)}, bf16[64,256]{1,0:T(8,128)(2,1)S(1)}, u32[]{:S(2)}, u32[]{:S(2)}) collective-permute-start(bf16[64,256]{1,0:T(8,128)(2,1)S(1)} %get-tuple-element.62), channel_id=1, source_target_pairs={{0,2},{2,0},{4,6},{6,4},{8,10},{10,8},{12,14},{14,12},{16,18},{18,... | collective-permute-start | bytes 98312 | tf_op jit(solution)/shard_map/ppermute | solution.py:379
  43.8 1.7 %collective-permute-start.10 = (bf16[32,256]{1,0:T(8,128)(2,1)S(1)}, bf16[32,256]{1,0:T(8,128)(2,1)S(1)}, u32[]{:S(2)}, u32[]{:S(2)}) collective-permute-start(bf16[32,256]{1,0:T(8,128)(2,1)S(1)} %get-tuple-element.70), channel_id=1, source_target_pairs={{0,29},{1,28},{2,31},{3,30},{4,1},{5,0},{6,3},{7,2},{8,5},{9,4},{1... | collective-permute-start | bytes 49160 | tf_op jit(solution)/shard_map/ppermute | solution.py:496
  45.6 3.0 %collective-permute-start.9 = (bf16[32,256]{1,0:T(8,128)(2,1)S(1)}, bf16[32,256]{1,0:T(8,128)(2,1)S(1)}, u32[]{:S(2)}, u32[]{:S(2)}) collective-permute-start(bf16[32,256]{1,0:T(8,128)(2,1)S(1)} %get-tuple-element.70), channel_id=1, source_target_pairs={{0,28},{2,30},{4,0},{6,2},{8,4},{10,6},{12,8},{14,10},{16,12},{18,... | collective-permute-start | bytes 49160 | tf_op jit(solution)/shard_map/ppermute | solution.py:384
  48.8 3.5 %collective-permute-done.7.refs_1_ = bf16[48,256]{1,0:T(8,128)(2,1)S(1)} collective-permute-done((bf16[48,256]{1,0:T(8,128)(2,1)S(1)}, bf16[48,256]{1,0:T(8,128)(2,1)S(1)}, u32[]{:S(2)}, u32[]{:S(2)}) %collective-permute-start.7) | collective-permute-done | bytes 24608 | tf_op jit(solution)/shard_map/ppermute | solution.py:379
  53.0 1.6 %collective-permute-done.11.refs_1_ = bf16[68,2048]{1,0:T(8,128)(2,1)S(1)} collective-permute-done((bf16[68,2048]{1,0:T(8,128)(2,1)S(1)}, bf16[68,2048]{1,0:T(8,128)(2,1)S(1)}, u32[]{:S(2)}, u32[]{:S(2)}) %collective-permute-start.11) | collective-permute-done | bytes 278560 | tf_op jit(solution)/shard_map/ppermute | solution.py:379
  54.9 2.6 %collective-permute-start.16 = (bf16[2,256,512]{2,1,0:T(8,128)(2,1)S(1)}, bf16[2,256,512]{2,1,0:T(8,128)(2,1)S(1)}, u32[]{:S(2)}, u32[]{:S(2)}) collective-permute-start(bf16[2,256,512]{2,1,0:T(8,128)(2,1)S(1)} %fusion.3), channel_id=1, source_target_pairs={{0,28},{2,30},{4,0},{6,2},{8,4},{10,6},{12,8},{14,10},{16,12},{18,... | collective-permute-start | bytes 1572872 | tf_op jit(solution)/shard_map/ppermute | solution.py:384
  57.4 11.4 %collective-permute-done.12.refs_1_ = bf16[68,1024]{1,0:T(8,128)(2,1)S(1)} collective-permute-done((bf16[68,1024]{1,0:T(8,128)(2,1)S(1)}, bf16[68,1024]{1,0:T(8,128)(2,1)S(1)}, u32[]{:S(2)}, u32[]{:S(2)}) %collective-permute-start.12) | collective-permute-done | bytes 139296 | tf_op jit(solution)/shard_map/ppermute | solution.py:379
  69.7 3.7 %collective-permute-start.15 = (bf16[68,256]{1,0:T(8,128)(2,1)S(1)}, bf16[68,256]{1,0:T(8,128)(2,1)S(1)}, u32[]{:S(2)}, u32[]{:S(2)}) collective-permute-start(bf16[68,256]{1,0:T(8,128)(2,1)S(1)} %get-tuple-element.82), channel_id=1, source_target_pairs={{0,24},{2,26},{4,28},{6,30},{8,16},{10,18},{12,20},{14,22},{16,8},... | collective-permute-start | bytes 104456 | tf_op jit(solution)/shard_map/ppermute | solution.py:379
  73.4 1.2 %collective-permute-done.14 = bf16[68,256]{1,0:T(8,128)(2,1)S(1)} collective-permute-done((bf16[68,256]{1,0:T(8,128)(2,1)S(1)}, bf16[68,256]{1,0:T(8,128)(2,1)S(1)}, u32[]{:S(2)}, u32[]{:S(2)}) %collective-permute-start.14) | collective-permute-done | bytes 34848 | tf_op jit(solution)/shard_map/ppermute | solution.py:379
  74.5 1.3 %collective-permute-done.15 = bf16[68,256]{1,0:T(8,128)(2,1)S(1)} collective-permute-done((bf16[68,256]{1,0:T(8,128)(2,1)S(1)}, bf16[68,256]{1,0:T(8,128)(2,1)S(1)}, u32[]{:S(2)}, u32[]{:S(2)}) %collective-permute-start.15) | collective-permute-done | bytes 34848 | tf_op jit(solution)/shard_map/ppermute | solution.py:379
  75.8 3.5 %collective-permute-start.19 = (bf16[68,256]{1,0:T(8,128)(2,1)S(1)}, bf16[68,256]{1,0:T(8,128)(2,1)S(1)}, u32[]{:S(2)}, u32[]{:S(2)}) collective-permute-start(bf16[68,256]{1,0:T(8,128)(2,1)S(1)} %add_convert_fusion.refs_0_), channel_id=1, source_target_pairs={{0,24},{2,26},{4,28},{6,30},{8,16},{10,18},{12,20},{14,22},{16,8},... | collective-permute-start | bytes 104456 | tf_op jit(solution)/shard_map/ppermute | solution.py:379
  80.3 2.0 %fusion = bf16[256,4096]{1,0:T(8,128)(2,1)} fusion(bf16[48,256]{1,0:T(8,128)(2,1)S(1)} %get-tuple-element.85, bf16[48,4096]{1,0:T(8,128)(2,1)S(1)} %bitcast.19), kind=kOutput, calls=%fused_computation.1 | convolution fusion | flops 102760448 | bytes 2514944 | tf_op jit(solution)/shard_map/dot_general | solution.py:690
  82.3 1.8 %collective-permute-done.18.refs_2_ = bf16[68,256]{1,0:T(8,128)(2,1)S(1)} collective-permute-done((bf16[68,256]{1,0:T(8,128)(2,1)S(1)}, bf16[68,256]{1,0:T(8,128)(2,1)S(1)}, u32[]{:S(2)}, u32[]{:S(2)}) %collective-permute-start.18) | collective-permute-done | bytes 34848 | tf_op jit(solution)/shard_map/ppermute | solution.py:379
  84.2 3.7 %collective-permute-start.20 = (bf16[68,1024]{1,0:T(8,128)(2,1)S(1)}, bf16[68,1024]{1,0:T(8,128)(2,1)S(1)}, u32[]{:S(2)}, u32[]{:S(2)}) collective-permute-start(bf16[68,1024]{1,0:T(8,128)(2,1)S(1)} %shard_map.142.refs_0_), channel_id=1, source_target_pairs={{0,4},{2,6},{4,0},{6,2},{8,12},{10,14},{12,8},{14,10},{16,20},{18,... | collective-permute-start | bytes 417800 | tf_op jit(solution)/shard_map/ppermute | solution.py:379
  88.9 2.1 %collective-permute-done.20.refs_1_ = bf16[68,1024]{1,0:T(8,128)(2,1)S(1)} collective-permute-done((bf16[68,1024]{1,0:T(8,128)(2,1)S(1)}, bf16[68,1024]{1,0:T(8,128)(2,1)S(1)}, u32[]{:S(2)}, u32[]{:S(2)}) %collective-permute-start.20) | collective-permute-done | bytes 139296 | tf_op jit(solution)/shard_map/ppermute | solution.py:379
  91.2 1.6 %collective-permute-done.21.two = bf16[68,2048]{1,0:T(8,128)(2,1)S(1)} collective-permute-done((bf16[68,2048]{1,0:T(8,128)(2,1)S(1)}, bf16[68,2048]{1,0:T(8,128)(2,1)S(1)}, u32[]{:S(2)}, u32[]{:S(2)}) %collective-permute-start.21) | collective-permute-done | bytes 278560 | tf_op jit(solution)/shard_map/ppermute | solution.py:379
  (54 shorter events, 8.5 us)
Async XLA Ops:
  3.9 7.4 %collective-permute-start.1 = (bf16[2,256,512]{2,1,0:T(8,128)(2,1)S(1)}, bf16[2,256,512]{2,1,0:T(8,128)(2,1)S(1)}, u32[]{:S(2)}, u32[]{:S(2)}) collective-permute-start(bf16[2,256,512]{2,1,0:T(8,128)(2,1)S(1)} %get-tuple-element.51.kv_own), channel_id=1, source_target_pairs={{0,2},{2,0},{4,6},{6,4},{8,10},{10,8},{12,14},{14,12},{16,18},{18,... | collective-permute-start | bytes 1572872 | tf_op jit(solution)/shard_map/ppermute | solution.py:379
  4.4 4.9 %collective-permute-start = (f32[48,256]{1,0:T(8,128)S(1)}, f32[48,256]{1,0:T(8,128)S(1)}, u32[]{:S(2)}, u32[]{:S(2)}) collective-permute-start(f32[48,256]{1,0:T(8,128)S(1)} %get-tuple-element.50), channel_id=1, source_target_pairs={{0,1},{1,0},{2,3},{3,2},{4,5},{5,4},{6,7},{7,6},{8,9},{9,8},{10,11... | collective-permute-start | bytes 147464 | tf_op jit(solution)/shard_map/ppermute | solution.py:379
  7.0 17.1 %collective-permute-start.2 = (bf16[2,256,512]{2,1,0:T(8,128)(2,1)S(1)}, bf16[2,256,512]{2,1,0:T(8,128)(2,1)S(1)}, u32[]{:S(2)}, u32[]{:S(2)}) collective-permute-start(bf16[2,256,512]{2,1,0:T(8,128)(2,1)S(1)} %get-tuple-element.51.kv_own), channel_id=1, source_target_pairs={{0,4},{2,6},{4,8},{6,10},{8,12},{10,14},{12,16},{14,18},{16,20},{1... | collective-permute-start | bytes 1572872 | tf_op jit(solution)/shard_map/ppermute | solution.py:384
  9.4 14.8 %collective-permute-start.3 = (bf16[32,256]{1,0:T(8,128)(2,1)S(1)}, bf16[32,256]{1,0:T(8,128)(2,1)S(1)}, u32[]{:S(2)}, u32[]{:S(2)}) collective-permute-start(bf16[32,256]{1,0:T(8,128)(2,1)S(1)} %slice.25), channel_id=1, source_target_pairs={{0,4},{2,6},{4,8},{6,10},{8,12},{10,14},{12,16},{14,18},{16,20},{1... | collective-permute-start | bytes 49160 | tf_op jit(solution)/shard_map/ppermute | solution.py:384
  11.3 14.9 %copy-start.3 = (bf16[2,16,512]{2,1,0:T(8,128)(2,1)S(1)}, bf16[2,16,512]{2,1,0:T(8,128)(2,1)}, u32[]{:S(2)}) copy-start(bf16[2,16,512]{2,1,0:T(8,128)(2,1)} %w_kv.1) | copy-start | bytes 98308
  24.1 2.0 %collective-permute-start.4 = (bf16[2,256,512]{2,1,0:T(8,128)(2,1)S(1)}, bf16[2,256,512]{2,1,0:T(8,128)(2,1)S(1)}, u32[]{:S(2)}, u32[]{:S(2)}) collective-permute-start(bf16[2,256,512]{2,1,0:T(8,128)(2,1)S(1)} %collective-permute-done.2.kv_pc), channel_id=1, source_target_pairs={{0,2},{2,0},{4,6},{6,4},{8,10},{10,8},{12,14},{14,12},{16,18},{18,... | collective-permute-start | bytes 1572872 | tf_op jit(solution)/shard_map/ppermute | solution.py:379
  24.1 1.9 %collective-permute-start.5 = (bf16[64,256]{1,0:T(8,128)(2,1)S(1)}, bf16[64,256]{1,0:T(8,128)(2,1)S(1)}, u32[]{:S(2)}, u32[]{:S(2)}) collective-permute-start(bf16[64,256]{1,0:T(8,128)(2,1)S(1)} %pad_maximum_fusion.1), channel_id=1, source_target_pairs={{0,2},{2,0},{4,6},{6,4},{8,10},{10,8},{12,14},{14,12},{16,18},{18,... | collective-permute-start | bytes 98312 | tf_op jit(solution)/shard_map/ppermute | solution.py:379
  39.7 3.7 %collective-permute-start.6 = (bf16[64,256]{1,0:T(8,128)(2,1)S(1)}, bf16[64,256]{1,0:T(8,128)(2,1)S(1)}, u32[]{:S(2)}, u32[]{:S(2)}) collective-permute-start(bf16[64,256]{1,0:T(8,128)(2,1)S(1)} %get-tuple-element.62), channel_id=1, source_target_pairs={{0,2},{2,0},{4,6},{6,4},{8,10},{10,8},{12,14},{14,12},{16,18},{18,... | collective-permute-start | bytes 98312 | tf_op jit(solution)/shard_map/ppermute | solution.py:379
  43.4 5.2 %collective-permute-start.8 = (bf16[2,2,256,512]{3,2,1,0:T(8,128)(2,1)S(1)}, bf16[2,2,256,512]{3,2,1,0:T(8,128)(2,1)S(1)}, u32[]{:S(2)}, u32[]{:S(2)}) collective-permute-start(bf16[2,2,256,512]{3,2,1,0:T(8,128)(2,1)S(1)} %get-tuple-element.68), channel_id=1, source_target_pairs={{0,2},{2,0},{4,6},{6,4},{8,10},{10,8},{12,14},{14,12},{16,18},{18,... | collective-permute-start | bytes 3145736 | tf_op jit(solution)/shard_map/ppermute | solution.py:379
  43.8 8.6 %collective-permute-start.10 = (bf16[32,256]{1,0:T(8,128)(2,1)S(1)}, bf16[32,256]{1,0:T(8,128)(2,1)S(1)}, u32[]{:S(2)}, u32[]{:S(2)}) collective-permute-start(bf16[32,256]{1,0:T(8,128)(2,1)S(1)} %get-tuple-element.70), channel_id=1, source_target_pairs={{0,29},{1,28},{2,31},{3,30},{4,1},{5,0},{6,3},{7,2},{8,5},{9,4},{1... | collective-permute-start | bytes 49160 | tf_op jit(solution)/shard_map/ppermute | solution.py:496
  45.6 6.8 %collective-permute-start.9 = (bf16[32,256]{1,0:T(8,128)(2,1)S(1)}, bf16[32,256]{1,0:T(8,128)(2,1)S(1)}, u32[]{:S(2)}, u32[]{:S(2)}) collective-permute-start(bf16[32,256]{1,0:T(8,128)(2,1)S(1)} %get-tuple-element.70), channel_id=1, source_target_pairs={{0,28},{2,30},{4,0},{6,2},{8,4},{10,6},{12,8},{14,10},{16,12},{18,... | collective-permute-start | bytes 49160 | tf_op jit(solution)/shard_map/ppermute | solution.py:384
  48.6 3.8 %collective-permute-start.7 = (bf16[48,256]{1,0:T(8,128)(2,1)S(1)}, bf16[48,256]{1,0:T(8,128)(2,1)S(1)}, u32[]{:S(2)}, u32[]{:S(2)}) collective-permute-start(bf16[48,256]{1,0:T(8,128)(2,1)S(1)} %get-tuple-element.66), channel_id=1, source_target_pairs={{0,1},{1,0},{2,3},{3,2},{4,5},{5,4},{6,7},{7,6},{8,9},{9,8},{10,11... | collective-permute-start | bytes 73736 | tf_op jit(solution)/shard_map/ppermute | solution.py:379
  52.9 1.6 %collective-permute-start.11 = (bf16[68,2048]{1,0:T(8,128)(2,1)S(1)}, bf16[68,2048]{1,0:T(8,128)(2,1)S(1)}, u32[]{:S(2)}, u32[]{:S(2)}) collective-permute-start(bf16[68,2048]{1,0:T(8,128)(2,1)S(1)} %get-tuple-element.73), channel_id=1, source_target_pairs={{0,2},{2,0},{4,6},{6,4},{8,10},{10,8},{12,14},{14,12},{16,18},{18,... | collective-permute-start | bytes 835592 | tf_op jit(solution)/shard_map/ppermute | solution.py:379
  54.7 25.6 %copy-start.5 = (bf16[3,16,4096]{2,1,0:T(8,128)(2,1)S(1)}, bf16[3,16,4096]{2,1,0:T(8,128)(2,1)}, u32[]{:S(2)}) copy-start(bf16[3,16,4096]{2,1,0:T(8,128)(2,1)} %param.17) | copy-start | bytes 1179652
  54.7 14.1 %collective-permute-start.12 = (bf16[68,1024]{1,0:T(8,128)(2,1)S(1)}, bf16[68,1024]{1,0:T(8,128)(2,1)S(1)}, u32[]{:S(2)}, u32[]{:S(2)}) collective-permute-start(bf16[68,1024]{1,0:T(8,128)(2,1)S(1)} %get-tuple-element.78), channel_id=1, source_target_pairs={{0,4},{2,6},{4,0},{6,2},{8,12},{10,14},{12,8},{14,10},{16,20},{18,... | collective-permute-start | bytes 417800 | tf_op jit(solution)/shard_map/ppermute | solution.py:379
  54.9 21.0 %collective-permute-start.16 = (bf16[2,256,512]{2,1,0:T(8,128)(2,1)S(1)}, bf16[2,256,512]{2,1,0:T(8,128)(2,1)S(1)}, u32[]{:S(2)}, u32[]{:S(2)}) collective-permute-start(bf16[2,256,512]{2,1,0:T(8,128)(2,1)S(1)} %fusion.3), channel_id=1, source_target_pairs={{0,28},{2,30},{4,0},{6,2},{8,4},{10,6},{12,8},{14,10},{16,12},{18,... | collective-permute-start | bytes 1572872 | tf_op jit(solution)/shard_map/ppermute | solution.py:384
  68.9 4.5 %collective-permute-start.13 = (bf16[68,256]{1,0:T(8,128)(2,1)S(1)}, bf16[68,256]{1,0:T(8,128)(2,1)S(1)}, u32[]{:S(2)}, u32[]{:S(2)}) collective-permute-start(bf16[68,256]{1,0:T(8,128)(2,1)S(1)} %get-tuple-element.80), channel_id=1, source_target_pairs={{0,8},{2,10},{4,12},{6,14},{8,0},{10,2},{12,4},{14,6},{16,24},{18,... | collective-permute-start | bytes 104456 | tf_op jit(solution)/shard_map/ppermute | solution.py:379
  69.7 4.9 %collective-permute-start.14 = (bf16[68,256]{1,0:T(8,128)(2,1)S(1)}, bf16[68,256]{1,0:T(8,128)(2,1)S(1)}, u32[]{:S(2)}, u32[]{:S(2)}) collective-permute-start(bf16[68,256]{1,0:T(8,128)(2,1)S(1)} %get-tuple-element.81), channel_id=1, source_target_pairs={{0,16},{2,18},{4,20},{6,22},{8,24},{10,26},{12,28},{14,30},{16,0},... | collective-permute-start | bytes 104456 | tf_op jit(solution)/shard_map/ppermute | solution.py:379
  69.7 6.1 %collective-permute-start.15 = (bf16[68,256]{1,0:T(8,128)(2,1)S(1)}, bf16[68,256]{1,0:T(8,128)(2,1)S(1)}, u32[]{:S(2)}, u32[]{:S(2)}) collective-permute-start(bf16[68,256]{1,0:T(8,128)(2,1)S(1)} %get-tuple-element.82), channel_id=1, source_target_pairs={{0,24},{2,26},{4,28},{6,30},{8,16},{10,18},{12,20},{14,22},{16,8},... | collective-permute-start | bytes 104456 | tf_op jit(solution)/shard_map/ppermute | solution.py:379
  75.8 6.5 %collective-permute-start.19 = (bf16[68,256]{1,0:T(8,128)(2,1)S(1)}, bf16[68,256]{1,0:T(8,128)(2,1)S(1)}, u32[]{:S(2)}, u32[]{:S(2)}) collective-permute-start(bf16[68,256]{1,0:T(8,128)(2,1)S(1)} %add_convert_fusion.refs_0_), channel_id=1, source_target_pairs={{0,24},{2,26},{4,28},{6,30},{8,16},{10,18},{12,20},{14,22},{16,8},... | collective-permute-start | bytes 104456 | tf_op jit(solution)/shard_map/ppermute | solution.py:379
  79.3 4.9 %collective-permute-start.18 = (bf16[68,256]{1,0:T(8,128)(2,1)S(1)}, bf16[68,256]{1,0:T(8,128)(2,1)S(1)}, u32[]{:S(2)}, u32[]{:S(2)}) collective-permute-start(bf16[68,256]{1,0:T(8,128)(2,1)S(1)} %add_convert_fusion.refs_0_), channel_id=1, source_target_pairs={{0,16},{2,18},{4,20},{6,22},{8,24},{10,26},{12,28},{14,30},{16,0},... | collective-permute-start | bytes 104456 | tf_op jit(solution)/shard_map/ppermute | solution.py:379
  79.3 4.9 %collective-permute-start.17 = (bf16[68,256]{1,0:T(8,128)(2,1)S(1)}, bf16[68,256]{1,0:T(8,128)(2,1)S(1)}, u32[]{:S(2)}, u32[]{:S(2)}) collective-permute-start(bf16[68,256]{1,0:T(8,128)(2,1)S(1)} %add_convert_fusion.refs_0_), channel_id=1, source_target_pairs={{0,8},{2,10},{4,12},{6,14},{8,0},{10,2},{12,4},{14,6},{16,24},{18,... | collective-permute-start | bytes 104456 | tf_op jit(solution)/shard_map/ppermute | solution.py:379
  84.2 6.8 %collective-permute-start.20 = (bf16[68,1024]{1,0:T(8,128)(2,1)S(1)}, bf16[68,1024]{1,0:T(8,128)(2,1)S(1)}, u32[]{:S(2)}, u32[]{:S(2)}) collective-permute-start(bf16[68,1024]{1,0:T(8,128)(2,1)S(1)} %shard_map.142.refs_0_), channel_id=1, source_target_pairs={{0,4},{2,6},{4,0},{6,2},{8,12},{10,14},{12,8},{14,10},{16,20},{18,... | collective-permute-start | bytes 417800 | tf_op jit(solution)/shard_map/ppermute | solution.py:379
  91.1 1.6 %collective-permute-start.21 = (bf16[68,2048]{1,0:T(8,128)(2,1)S(1)}, bf16[68,2048]{1,0:T(8,128)(2,1)S(1)}, u32[]{:S(2)}, u32[]{:S(2)}) collective-permute-start(bf16[68,2048]{1,0:T(8,128)(2,1)S(1)} %shard_map.143.one), channel_id=1, source_target_pairs={{0,2},{2,0},{4,6},{6,4},{8,10},{10,8},{12,14},{14,12},{16,18},{18,... | collective-permute-start | bytes 835592 | tf_op jit(solution)/shard_map/ppermute | solution.py:379
  (4 other events, 44.7 us)

commit v4 on v2

--- a/solution.py
+++ b/solution.py
@@ -151,10 +151,10 @@
     dk[...] = jnp.zeros_like(dk)
     dv[...] = jnp.zeros_like(dv)
     slots = (buffers[:5], buffers[5:])
-    for _, e_ref, ds_ref, _, inv_ref in slots:
-        e_ref[...] = jnp.zeros_like(e_ref)
-        ds_ref[...] = jnp.zeros_like(ds_ref)
-        inv_ref[...] = jnp.zeros_like(inv_ref)
+    _, e_ref, ds_ref, _, inv_ref = slots[1]
+    e_ref[...] = jnp.zeros_like(e_ref)
+    ds_ref[...] = jnp.zeros_like(ds_ref)
+    inv_ref[...] = jnp.zeros_like(inv_ref)
     wait(0)
     index = lax.axis_index("seq")
     core = index % 2
@@ -677,9 +677,6 @@
     for level in range(1, levels):
         pieces = exchanged_pieces(summed_and_cut(pieces, 4**level, 4), 4**level)
     total = sum(p.astype(jnp.float32) for p in pieces).astype(jnp.bfloat16)
-    key_value_gradient = (
-        keep_own + received[0].astype(jnp.float32) + back.astype(jnp.float32)
-    ).astype(jnp.bfloat16)
     grad_inputs = (
         adapter_scale
         * lax.dot_general(
@@ -688,7 +685,10 @@
     ).astype(jnp.bfloat16)
     for level in range(levels - 1, 0, -1):
         total = joined(exchanged_pieces([total] * 4, 4**level), 4**level)
-    total, grad_inputs = lax.optimization_barrier((total, grad_inputs))
+    total, grad_inputs, back = lax.optimization_barrier((total, grad_inputs, back))
+    key_value_gradient = (
+        keep_own + received[0].astype(jnp.float32) + back.astype(jnp.float32)
+    ).astype(jnp.bfloat16)
     total = joined(exchanged_pieces([total] * 2, 2), 2)
     total, key_value_gradient = lax.optimization_barrier((total, key_value_gradient))
     down_gradient, grad_up_q, grad_up_kv = joined_outputs(

time: 91.3 us -> 90.3 us (0.989)
    ppermute x17, waiting for transfers between devices: 22.7 us -> 21.8 us  [exchanged(): lax.ppermute(value, axis, [(i, i ^ bit) for i in range(lax.axis_size(axis...]
  transfers between devices with their start and end apart: 22 -> 22, of which waited for: 13 -> 13; matrix products, arithmetic and copies ran while one was open for 3% -> 4% of each run, Pallas kernels for 9% -> 9%
where the time goes in v4:
time: 90.3 us; the launch traced here: 90.2 us
  waiting for transfers between devices  29.7 us (33%)
  starting transfers between devices  29.5 us (33%)
  Pallas kernels  26.6 us (29%)
  matrix products  2.05 us (2%)
  other arithmetic  1.26 us (1%)
    ppermute x17, waiting for transfers between devices, exchanged(): lax.ppermute(value, axis, [(i, i ^ bit) for i in range(lax.axis_size(axis...  21.8 us
    pallas_call x2, Pallas kernels, call(): pl.pallas_call(functools.partial(kernel, per_kv, rank), in_specs=[smem, h...  21.5 us
    ppermute x17, starting transfers between devices, exchanged(): lax.ppermute(value, axis, [(i, i ^ bit) for i in range(lax.axis_size(axis...  18 us
    ppermute x4, starting transfers between devices, moved(): lax.ppermute(value, axis, [(i, (i + by) % count) for i in range(count)])  8.81 us
    ppermute x4, waiting for transfers between devices, moved(): lax.ppermute(value, axis, [(i, (i + by) % count) for i in range(count)])  7.44 us
    pallas_call x1, Pallas kernels, projected_and_stacked(): pl.pallas_call(kernel, grid=(steps,), in_specs=[columns(rows, width), col...  3.22 us
    ppermute x1, starting transfers between devices, up_terms(): lax.ppermute(previous, ('seq', 'head'), pairs)  2.72 us
    dot_general x1, matrix products, per_device(): lax.dot_general(up_low, flattened_down, (((0,), (0,)), ((), ())), preferr...  2.05 us
  transfers between devices with their start and end apart: 22, of which 13 were waited for; matrix products, arithmetic and copies ran while one was open for 4% of the time, Pallas kernels for 9%

profile of v4, /device:TPU:0, one launch (start us, length us, event | category | flops | bytes accessed | tf_op | source)
XLA Modules:
  0.0 90.2 jit_solution(11266271477338435164)
XLA Ops:
  0.7 3.2 %shard_map.137 = (f32[48,256]{1,0:T(8,128)S(1)}, bf16[2,256,512]{2,1,0:T(8,128)(2,1)S(1)}) custom-call(bf16[48,4096]{1,0:T(8,128)(2,1)} %bitcast.18, bf16[256,4096]{1,0:T(8,128)(2,1)} %refs_4_.1, bf16[256,512]{1,0:T(8,128)(2,1)} %key.1, bf16[256,512]{1,0:T(8,128)(2,1)} %value.1), custom_call_target="tpu_custom_call" | custom-call | tf_op jit(solution)/shard_map/pallas_call | solution.py:440
  4.4 2.6 %collective-permute-start = (f32[48,256]{1,0:T(8,128)S(1)}, f32[48,256]{1,0:T(8,128)S(1)}, u32[]{:S(2)}, u32[]{:S(2)}) collective-permute-start(f32[48,256]{1,0:T(8,128)S(1)} %get-tuple-element.47), channel_id=1, source_target_pairs={{0,1},{1,0},{2,3},{3,2},{4,5},{5,4},{6,7},{7,6},{8,9},{9,8},{10,11... | collective-permute-start | bytes 147464 | tf_op jit(solution)/shard_map/ppermute | solution.py:378
  7.0 1.5 %collective-permute-start.2 = (bf16[2,256,512]{2,1,0:T(8,128)(2,1)S(1)}, bf16[2,256,512]{2,1,0:T(8,128)(2,1)S(1)}, u32[]{:S(2)}, u32[]{:S(2)}) collective-permute-start(bf16[2,256,512]{2,1,0:T(8,128)(2,1)S(1)} %get-tuple-element.48.kv_own), channel_id=1, source_target_pairs={{0,4},{2,6},{4,8},{6,10},{8,12},{10,14},{12,16},{14,18},{16,20},{1... | collective-permute-start | bytes 1572872 | tf_op jit(solution)/shard_map/ppermute | solution.py:383
  9.4 1.8 %collective-permute-start.3 = (bf16[32,256]{1,0:T(8,128)(2,1)S(1)}, bf16[32,256]{1,0:T(8,128)(2,1)S(1)}, u32[]{:S(2)}, u32[]{:S(2)}) collective-permute-start(bf16[32,256]{1,0:T(8,128)(2,1)S(1)} %slice.25), channel_id=1, source_target_pairs={{0,4},{2,6},{4,8},{6,10},{8,12},{10,14},{12,16},{14,18},{16,20},{1... | collective-permute-start | bytes 49160 | tf_op jit(solution)/shard_map/ppermute | solution.py:383
  11.3 7.2 %own_chip_heads.1 = (f32[16,256]{1,0:T(8,128)S(1)}, f32[2048,256]{1,0:T(8,128)S(1)}, f32[2048,128]{1,0:T(8,128)S(1)}) custom-call(s32[32]{0:T(128)S(1)} %copy-done.4, bf16[256,4096]{1,0:T(8,128)(2,1)} %q.3, bf16[256,4096]{1,0:T(8,128)(2,1)} %do.3, f32[32,256]{1,0:T(8,128)S(1)} %copy-done.2, bf16[16,4096]{1,0:T(8,128)(2,1)S(1)} %copy-done.1, ...), custom_call_target="tpu_custom_call" | custom-call | flops 10737418240 | bytes 6291456 | tf_op jit(solution)/shard_map/own_chip_heads/pallas_call | solution.py:315
  18.5 5.6 %collective-permute-done.3 = bf16[32,256]{1,0:T(8,128)(2,1)S(1)} collective-permute-done((bf16[32,256]{1,0:T(8,128)(2,1)S(1)}, bf16[32,256]{1,0:T(8,128)(2,1)S(1)}, u32[]{:S(2)}, u32[]{:S(2)}) %collective-permute-start.3) | collective-permute-done | bytes 16416 | tf_op jit(solution)/shard_map/ppermute | solution.py:383
  24.7 1.4 %collective-permute-done.5 = bf16[64,256]{1,0:T(8,128)(2,1)S(1)} collective-permute-done((bf16[64,256]{1,0:T(8,128)(2,1)S(1)}, bf16[64,256]{1,0:T(8,128)(2,1)S(1)}, u32[]{:S(2)}, u32[]{:S(2)}) %collective-permute-start.5) | collective-permute-done | bytes 32800 | tf_op jit(solution)/shard_map/ppermute | solution.py:378
  26.1 14.3 %previous_chip_heads.1 = (f32[2,256,512]{2,1,0:T(8,128)S(1)}, f32[2,256,512]{2,1,0:T(8,128)S(1)}, bf16[2,2,256,512]{3,2,1,0:T(8,128)(2,1)S(1)}, f32[16,256]{1,0:...) custom-call(s32[32]{0:T(128)S(1)} %copy-done.4, ...), custom_call_target="tpu_custom_call" | custom-call | flops 21474836480 | bytes 6291456 | tf_op jit(solution)/shard_map/previous_chip_heads/pallas_call | solution.py:315
  40.5 3.1 %collective-permute-start.6 = (bf16[64,256]{1,0:T(8,128)(2,1)S(1)}, bf16[64,256]{1,0:T(8,128)(2,1)S(1)}, u32[]{:S(2)}, u32[]{:S(2)}) collective-permute-start(bf16[64,256]{1,0:T(8,128)(2,1)S(1)} %get-tuple-element.59), channel_id=1, source_target_pairs={{0,2},{2,0},{4,6},{6,4},{8,10},{10,8},{12,14},{14,12},{16,18},{18,... | collective-permute-start | bytes 98312 | tf_op jit(solution)/shard_map/ppermute | solution.py:378
  45.4 2.7 %collective-permute-start.9 = (bf16[32,256]{1,0:T(8,128)(2,1)S(1)}, bf16[32,256]{1,0:T(8,128)(2,1)S(1)}, u32[]{:S(2)}, u32[]{:S(2)}) collective-permute-start(bf16[32,256]{1,0:T(8,128)(2,1)S(1)} %get-tuple-element.64), channel_id=1, source_target_pairs={{0,29},{1,28},{2,31},{3,30},{4,1},{5,0},{6,3},{7,2},{8,5},{9,4},{1... | collective-permute-start | bytes 49160 | tf_op jit(solution)/shard_map/ppermute | solution.py:494
  48.1 1.4 %collective-permute-start.8 = (bf16[32,256]{1,0:T(8,128)(2,1)S(1)}, bf16[32,256]{1,0:T(8,128)(2,1)S(1)}, u32[]{:S(2)}, u32[]{:S(2)}) collective-permute-start(bf16[32,256]{1,0:T(8,128)(2,1)S(1)} %get-tuple-element.64), channel_id=1, source_target_pairs={{0,28},{2,30},{4,0},{6,2},{8,4},{10,6},{12,8},{14,10},{16,12},{18,... | collective-permute-start | bytes 49160 | tf_op jit(solution)/shard_map/ppermute | solution.py:383
  50.0 1.8 %collective-permute-done.8.refs_2_ = bf16[32,256]{1,0:T(8,128)(2,1)S(1)} collective-permute-done((bf16[32,256]{1,0:T(8,128)(2,1)S(1)}, bf16[32,256]{1,0:T(8,128)(2,1)S(1)}, u32[]{:S(2)}, u32[]{:S(2)}) %collective-permute-start.8) | collective-permute-done | bytes 16416 | tf_op jit(solution)/shard_map/ppermute | solution.py:383
  52.4 1.6 %collective-permute-done.10.refs_1_ = bf16[68,2048]{1,0:T(8,128)(2,1)S(1)} collective-permute-done((bf16[68,2048]{1,0:T(8,128)(2,1)S(1)}, bf16[68,2048]{1,0:T(8,128)(2,1)S(1)}, u32[]{:S(2)}, u32[]{:S(2)}) %collective-permute-start.10) | collective-permute-done | bytes 278560 | tf_op jit(solution)/shard_map/ppermute | solution.py:378
  54.1 1.2 %collective-permute-start.11 = (bf16[68,1024]{1,0:T(8,128)(2,1)S(1)}, bf16[68,1024]{1,0:T(8,128)(2,1)S(1)}, u32[]{:S(2)}, u32[]{:S(2)}) collective-permute-start(bf16[68,1024]{1,0:T(8,128)(2,1)S(1)} %get-tuple-element.69), channel_id=1, source_target_pairs={{0,4},{2,6},{4,0},{6,2},{8,12},{10,14},{12,8},{14,10},{16,20},{18,... | collective-permute-start | bytes 417800 | tf_op jit(solution)/shard_map/ppermute | solution.py:378
  55.5 4.6 %collective-permute-done.11.refs_1_ = bf16[68,1024]{1,0:T(8,128)(2,1)S(1)} collective-permute-done((bf16[68,1024]{1,0:T(8,128)(2,1)S(1)}, bf16[68,1024]{1,0:T(8,128)(2,1)S(1)}, u32[]{:S(2)}, u32[]{:S(2)}) %collective-permute-start.11) | collective-permute-done | bytes 139296 | tf_op jit(solution)/shard_map/ppermute | solution.py:378
  60.2 3.5 %collective-permute-start.14 = (bf16[68,256]{1,0:T(8,128)(2,1)S(1)}, bf16[68,256]{1,0:T(8,128)(2,1)S(1)}, u32[]{:S(2)}, u32[]{:S(2)}) collective-permute-start(bf16[68,256]{1,0:T(8,128)(2,1)S(1)} %get-tuple-element.76), channel_id=1, source_target_pairs={{0,16},{2,18},{4,20},{6,22},{8,24},{10,26},{12,28},{14,30},{16,0},... | collective-permute-start | bytes 104456 | tf_op jit(solution)/shard_map/ppermute | solution.py:378
  64.6 4.1 %collective-permute-start.19 = (bf16[2,256,512]{2,1,0:T(8,128)(2,1)S(1)}, bf16[2,256,512]{2,1,0:T(8,128)(2,1)S(1)}, u32[]{:S(2)}, u32[]{:S(2)}) collective-permute-start(bf16[2,256,512]{2,1,0:T(8,128)(2,1)S(1)} %fusion.3), channel_id=1, source_target_pairs={{0,28},{2,30},{4,0},{6,2},{8,4},{10,6},{12,8},{14,10},{16,12},{18,... | collective-permute-start | bytes 1572872 | tf_op jit(solution)/shard_map/ppermute | solution.py:383
  68.7 1.2 %collective-permute-done.15 = bf16[68,256]{1,0:T(8,128)(2,1)S(1)} collective-permute-done((bf16[68,256]{1,0:T(8,128)(2,1)S(1)}, bf16[68,256]{1,0:T(8,128)(2,1)S(1)}, u32[]{:S(2)}, u32[]{:S(2)}) %collective-permute-start.15) | collective-permute-done | bytes 34848 | tf_op jit(solution)/shard_map/ppermute | solution.py:378
  70.5 4.0 %collective-permute-start.16 = (bf16[68,256]{1,0:T(8,128)(2,1)S(1)}, bf16[68,256]{1,0:T(8,128)(2,1)S(1)}, u32[]{:S(2)}, u32[]{:S(2)}) collective-permute-start(bf16[68,256]{1,0:T(8,128)(2,1)S(1)} %add_convert_fusion.refs_0_), channel_id=1, source_target_pairs={{0,8},{2,10},{4,12},{6,14},{8,0},{10,2},{12,4},{14,6},{16,24},{18,... | collective-permute-start | bytes 104456 | tf_op jit(solution)/shard_map/ppermute | solution.py:378
  74.4 2.0 %fusion = bf16[256,4096]{1,0:T(8,128)(2,1)} fusion(bf16[48,256]{1,0:T(8,128)(2,1)S(1)} %get-tuple-element.78, bf16[48,4096]{1,0:T(8,128)(2,1)S(1)} %bitcast.19), kind=kOutput, calls=%fused_computation.1 | convolution fusion | flops 102760448 | bytes 2514944 | tf_op jit(solution)/shard_map/dot_general | solution.py:682
  76.5 4.4 %collective-permute-done.18.refs_3_ = bf16[68,256]{1,0:T(8,128)(2,1)S(1)} collective-permute-done((bf16[68,256]{1,0:T(8,128)(2,1)S(1)}, bf16[68,256]{1,0:T(8,128)(2,1)S(1)}, u32[]{:S(2)}, u32[]{:S(2)}) %collective-permute-start.18) | collective-permute-done | bytes 34848 | tf_op jit(solution)/shard_map/ppermute | solution.py:378
  80.9 1.2 %collective-permute-done.17.refs_2_ = bf16[68,256]{1,0:T(8,128)(2,1)S(1)} collective-permute-done((bf16[68,256]{1,0:T(8,128)(2,1)S(1)}, bf16[68,256]{1,0:T(8,128)(2,1)S(1)}, u32[]{:S(2)}, u32[]{:S(2)}) %collective-permute-start.17) | collective-permute-done | bytes 34848 | tf_op jit(solution)/shard_map/ppermute | solution.py:378
  83.3 4.1 %collective-permute-done.20.refs_1_ = bf16[68,1024]{1,0:T(8,128)(2,1)S(1)} collective-permute-done((bf16[68,1024]{1,0:T(8,128)(2,1)S(1)}, bf16[68,1024]{1,0:T(8,128)(2,1)S(1)}, u32[]{:S(2)}, u32[]{:S(2)}) %collective-permute-start.20) | collective-permute-done | bytes 139296 | tf_op jit(solution)/shard_map/ppermute | solution.py:378
  87.5 1.6 %collective-permute-done.21.two = bf16[68,2048]{1,0:T(8,128)(2,1)S(1)} collective-permute-done((bf16[68,2048]{1,0:T(8,128)(2,1)S(1)}, bf16[68,2048]{1,0:T(8,128)(2,1)S(1)}, u32[]{:S(2)}, u32[]{:S(2)}) %collective-permute-start.21) | collective-permute-done | bytes 278560 | tf_op jit(solution)/shard_map/ppermute | solution.py:378
  (54 shorter events, 9.1 us)
Async XLA Ops:
  3.9 7.4 %collective-permute-start.1 = (bf16[2,256,512]{2,1,0:T(8,128)(2,1)S(1)}, bf16[2,256,512]{2,1,0:T(8,128)(2,1)S(1)}, u32[]{:S(2)}, u32[]{:S(2)}) collective-permute-start(bf16[2,256,512]{2,1,0:T(8,128)(2,1)S(1)} %get-tuple-element.48.kv_own), channel_id=1, source_target_pairs={{0,2},{2,0},{4,6},{6,4},{8,10},{10,8},{12,14},{14,12},{16,18},{18,... | collective-permute-start | bytes 1572872 | tf_op jit(solution)/shard_map/ppermute | solution.py:378
  4.4 4.9 %collective-permute-start = (f32[48,256]{1,0:T(8,128)S(1)}, f32[48,256]{1,0:T(8,128)S(1)}, u32[]{:S(2)}, u32[]{:S(2)}) collective-permute-start(f32[48,256]{1,0:T(8,128)S(1)} %get-tuple-element.47), channel_id=1, source_target_pairs={{0,1},{1,0},{2,3},{3,2},{4,5},{5,4},{6,7},{7,6},{8,9},{9,8},{10,11... | collective-permute-start | bytes 147464 | tf_op jit(solution)/shard_map/ppermute | solution.py:378
  7.0 17.1 %collective-permute-start.2 = (bf16[2,256,512]{2,1,0:T(8,128)(2,1)S(1)}, bf16[2,256,512]{2,1,0:T(8,128)(2,1)S(1)}, u32[]{:S(2)}, u32[]{:S(2)}) collective-permute-start(bf16[2,256,512]{2,1,0:T(8,128)(2,1)S(1)} %get-tuple-element.48.kv_own), channel_id=1, source_target_pairs={{0,4},{2,6},{4,8},{6,10},{8,12},{10,14},{12,16},{14,18},{16,20},{1... | collective-permute-start | bytes 1572872 | tf_op jit(solution)/shard_map/ppermute | solution.py:383
  9.4 14.8 %collective-permute-start.3 = (bf16[32,256]{1,0:T(8,128)(2,1)S(1)}, bf16[32,256]{1,0:T(8,128)(2,1)S(1)}, u32[]{:S(2)}, u32[]{:S(2)}) collective-permute-start(bf16[32,256]{1,0:T(8,128)(2,1)S(1)} %slice.25), channel_id=1, source_target_pairs={{0,4},{2,6},{4,8},{6,10},{8,12},{10,14},{12,16},{14,18},{16,20},{1... | collective-permute-start | bytes 49160 | tf_op jit(solution)/shard_map/ppermute | solution.py:383
  24.1 2.0 %collective-permute-start.4 = (bf16[2,256,512]{2,1,0:T(8,128)(2,1)S(1)}, bf16[2,256,512]{2,1,0:T(8,128)(2,1)S(1)}, u32[]{:S(2)}, u32[]{:S(2)}) collective-permute-start(bf16[2,256,512]{2,1,0:T(8,128)(2,1)S(1)} %collective-permute-done.2.kv_pc), channel_id=1, source_target_pairs={{0,2},{2,0},{4,6},{6,4},{8,10},{10,8},{12,14},{14,12},{16,18},{18,... | collective-permute-start | bytes 1572872 | tf_op jit(solution)/shard_map/ppermute | solution.py:378
  24.1 1.9 %collective-permute-start.5 = (bf16[64,256]{1,0:T(8,128)(2,1)S(1)}, bf16[64,256]{1,0:T(8,128)(2,1)S(1)}, u32[]{:S(2)}, u32[]{:S(2)}) collective-permute-start(bf16[64,256]{1,0:T(8,128)(2,1)S(1)} %pad_maximum_fusion.1), channel_id=1, source_target_pairs={{0,2},{2,0},{4,6},{6,4},{8,10},{10,8},{12,14},{14,12},{16,18},{18,... | collective-permute-start | bytes 98312 | tf_op jit(solution)/shard_map/ppermute | solution.py:378
  26.1 25.7 %copy-start = (bf16[256,4096]{1,0:T(8,128)(2,1)S(1)}, bf16[256,4096]{1,0:T(8,128)(2,1)}, u32[]{:S(2)}) copy-start(bf16[256,4096]{1,0:T(8,128)(2,1)} %refs_4_.1) | copy-start | bytes 6291460
  40.5 4.0 %collective-permute-start.6 = (bf16[64,256]{1,0:T(8,128)(2,1)S(1)}, bf16[64,256]{1,0:T(8,128)(2,1)S(1)}, u32[]{:S(2)}, u32[]{:S(2)}) collective-permute-start(bf16[64,256]{1,0:T(8,128)(2,1)S(1)} %get-tuple-element.59), channel_id=1, source_target_pairs={{0,2},{2,0},{4,6},{6,4},{8,10},{10,8},{12,14},{14,12},{16,18},{18,... | collective-permute-start | bytes 98312 | tf_op jit(solution)/shard_map/ppermute | solution.py:378
  44.4 10.9 %collective-permute-start.12 = (bf16[2,2,256,512]{3,2,1,0:T(8,128)(2,1)S(1)}, bf16[2,2,256,512]{3,2,1,0:T(8,128)(2,1)S(1)}, u32[]{:S(2)}, u32[]{:S(2)}) collective-permute-start(bf16[2,2,256,512]{3,2,1,0:T(8,128)(2,1)S(1)} %get-tuple-element.71), channel_id=1, source_target_pairs={{0,2},{2,0},{4,6},{6,4},{8,10},{10,8},{12,14},{14,12},{16,18},{18,... | collective-permute-start | bytes 3145736 | tf_op jit(solution)/shard_map/ppermute | solution.py:378
  44.8 7.0 %collective-permute-start.7 = (bf16[48,256]{1,0:T(8,128)(2,1)S(1)}, bf16[48,256]{1,0:T(8,128)(2,1)S(1)}, u32[]{:S(2)}, u32[]{:S(2)}) collective-permute-start(bf16[48,256]{1,0:T(8,128)(2,1)S(1)} %get-tuple-element.63), channel_id=1, source_target_pairs={{0,1},{1,0},{2,3},{3,2},{4,5},{5,4},{6,7},{7,6},{8,9},{9,8},{10,11... | collective-permute-start | bytes 73736 | tf_op jit(solution)/shard_map/ppermute | solution.py:378
  45.4 4.6 %collective-permute-start.9 = (bf16[32,256]{1,0:T(8,128)(2,1)S(1)}, bf16[32,256]{1,0:T(8,128)(2,1)S(1)}, u32[]{:S(2)}, u32[]{:S(2)}) collective-permute-start(bf16[32,256]{1,0:T(8,128)(2,1)S(1)} %get-tuple-element.64), channel_id=1, source_target_pairs={{0,29},{1,28},{2,31},{3,30},{4,1},{5,0},{6,3},{7,2},{8,5},{9,4},{1... | collective-permute-start | bytes 49160 | tf_op jit(solution)/shard_map/ppermute | solution.py:494
  48.1 3.7 %collective-permute-start.8 = (bf16[32,256]{1,0:T(8,128)(2,1)S(1)}, bf16[32,256]{1,0:T(8,128)(2,1)S(1)}, u32[]{:S(2)}, u32[]{:S(2)}) collective-permute-start(bf16[32,256]{1,0:T(8,128)(2,1)S(1)} %get-tuple-element.64), channel_id=1, source_target_pairs={{0,28},{2,30},{4,0},{6,2},{8,4},{10,6},{12,8},{14,10},{16,12},{18,... | collective-permute-start | bytes 49160 | tf_op jit(solution)/shard_map/ppermute | solution.py:383
  52.3 22.1 %copy-start.5 = (bf16[3,16,4096]{2,1,0:T(8,128)(2,1)S(1)}, bf16[3,16,4096]{2,1,0:T(8,128)(2,1)}, u32[]{:S(2)}) copy-start(bf16[3,16,4096]{2,1,0:T(8,128)(2,1)} %param.17) | copy-start | bytes 1179652
  52.4 1.6 %collective-permute-start.10 = (bf16[68,2048]{1,0:T(8,128)(2,1)S(1)}, bf16[68,2048]{1,0:T(8,128)(2,1)S(1)}, u32[]{:S(2)}, u32[]{:S(2)}) collective-permute-start(bf16[68,2048]{1,0:T(8,128)(2,1)S(1)} %get-tuple-element.67), channel_id=1, source_target_pairs={{0,2},{2,0},{4,6},{6,4},{8,10},{10,8},{12,14},{14,12},{16,18},{18,... | collective-permute-start | bytes 835592 | tf_op jit(solution)/shard_map/ppermute | solution.py:378
  54.1 6.0 %collective-permute-start.11 = (bf16[68,1024]{1,0:T(8,128)(2,1)S(1)}, bf16[68,1024]{1,0:T(8,128)(2,1)S(1)}, u32[]{:S(2)}, u32[]{:S(2)}) collective-permute-start(bf16[68,1024]{1,0:T(8,128)(2,1)S(1)} %get-tuple-element.69), channel_id=1, source_target_pairs={{0,4},{2,6},{4,0},{6,2},{8,12},{10,14},{12,8},{14,10},{16,20},{18,... | collective-permute-start | bytes 417800 | tf_op jit(solution)/shard_map/ppermute | solution.py:378
  60.2 8.6 %collective-permute-start.13 = (bf16[68,256]{1,0:T(8,128)(2,1)S(1)}, bf16[68,256]{1,0:T(8,128)(2,1)S(1)}, u32[]{:S(2)}, u32[]{:S(2)}) collective-permute-start(bf16[68,256]{1,0:T(8,128)(2,1)S(1)} %get-tuple-element.75), channel_id=1, source_target_pairs={{0,8},{2,10},{4,12},{6,14},{8,0},{10,2},{12,4},{14,6},{16,24},{18,... | collective-permute-start | bytes 104456 | tf_op jit(solution)/shard_map/ppermute | solution.py:378
  60.2 8.5 %collective-permute-start.14 = (bf16[68,256]{1,0:T(8,128)(2,1)S(1)}, bf16[68,256]{1,0:T(8,128)(2,1)S(1)}, u32[]{:S(2)}, u32[]{:S(2)}) collective-permute-start(bf16[68,256]{1,0:T(8,128)(2,1)S(1)} %get-tuple-element.76), channel_id=1, source_target_pairs={{0,16},{2,18},{4,20},{6,22},{8,24},{10,26},{12,28},{14,30},{16,0},... | collective-permute-start | bytes 104456 | tf_op jit(solution)/shard_map/ppermute | solution.py:378
  63.7 6.2 %collective-permute-start.15 = (bf16[68,256]{1,0:T(8,128)(2,1)S(1)}, bf16[68,256]{1,0:T(8,128)(2,1)S(1)}, u32[]{:S(2)}, u32[]{:S(2)}) collective-permute-start(bf16[68,256]{1,0:T(8,128)(2,1)S(1)} %get-tuple-element.77), channel_id=1, source_target_pairs={{0,24},{2,26},{4,28},{6,30},{8,16},{10,18},{12,20},{14,22},{16,8},... | collective-permute-start | bytes 104456 | tf_op jit(solution)/shard_map/ppermute | solution.py:378
  64.6 17.6 %collective-permute-start.19 = (bf16[2,256,512]{2,1,0:T(8,128)(2,1)S(1)}, bf16[2,256,512]{2,1,0:T(8,128)(2,1)S(1)}, u32[]{:S(2)}, u32[]{:S(2)}) collective-permute-start(bf16[2,256,512]{2,1,0:T(8,128)(2,1)S(1)} %fusion.3), channel_id=1, source_target_pairs={{0,28},{2,30},{4,0},{6,2},{8,4},{10,6},{12,8},{14,10},{16,12},{18,... | collective-permute-start | bytes 1572872 | tf_op jit(solution)/shard_map/ppermute | solution.py:383
  70.0 10.9 %collective-permute-start.18 = (bf16[68,256]{1,0:T(8,128)(2,1)S(1)}, bf16[68,256]{1,0:T(8,128)(2,1)S(1)}, u32[]{:S(2)}, u32[]{:S(2)}) collective-permute-start(bf16[68,256]{1,0:T(8,128)(2,1)S(1)} %add_convert_fusion.refs_0_), channel_id=1, source_target_pairs={{0,24},{2,26},{4,28},{6,30},{8,16},{10,18},{12,20},{14,22},{16,8},... | collective-permute-start | bytes 104456 | tf_op jit(solution)/shard_map/ppermute | solution.py:378
  70.5 11.7 %collective-permute-start.17 = (bf16[68,256]{1,0:T(8,128)(2,1)S(1)}, bf16[68,256]{1,0:T(8,128)(2,1)S(1)}, u32[]{:S(2)}, u32[]{:S(2)}) collective-permute-start(bf16[68,256]{1,0:T(8,128)(2,1)S(1)} %add_convert_fusion.refs_0_), channel_id=1, source_target_pairs={{0,16},{2,18},{4,20},{6,22},{8,24},{10,26},{12,28},{14,30},{16,0},... | collective-permute-start | bytes 104456 | tf_op jit(solution)/shard_map/ppermute | solution.py:378
  70.5 11.7 %collective-permute-start.16 = (bf16[68,256]{1,0:T(8,128)(2,1)S(1)}, bf16[68,256]{1,0:T(8,128)(2,1)S(1)}, u32[]{:S(2)}, u32[]{:S(2)}) collective-permute-start(bf16[68,256]{1,0:T(8,128)(2,1)S(1)} %add_convert_fusion.refs_0_), channel_id=1, source_target_pairs={{0,8},{2,10},{4,12},{6,14},{8,0},{10,2},{12,4},{14,6},{16,24},{18,... | collective-permute-start | bytes 104456 | tf_op jit(solution)/shard_map/ppermute | solution.py:378
  82.2 5.2 %collective-permute-start.20 = (bf16[68,1024]{1,0:T(8,128)(2,1)S(1)}, bf16[68,1024]{1,0:T(8,128)(2,1)S(1)}, u32[]{:S(2)}, u32[]{:S(2)}) collective-permute-start(bf16[68,1024]{1,0:T(8,128)(2,1)S(1)} %shard_map.142.refs_0_), channel_id=1, source_target_pairs={{0,4},{2,6},{4,0},{6,2},{8,12},{10,14},{12,8},{14,10},{16,20},{18,... | collective-permute-start | bytes 417800 | tf_op jit(solution)/shard_map/ppermute | solution.py:378
  87.4 1.6 %collective-permute-start.21 = (bf16[68,2048]{1,0:T(8,128)(2,1)S(1)}, bf16[68,2048]{1,0:T(8,128)(2,1)S(1)}, u32[]{:S(2)}, u32[]{:S(2)}) collective-permute-start(bf16[68,2048]{1,0:T(8,128)(2,1)S(1)} %shard_map.143.one), channel_id=1, source_target_pairs={{0,2},{2,0},{4,6},{6,4},{8,10},{10,8},{12,14},{14,12},{16,18},{18,... | collective-permute-start | bytes 835592 | tf_op jit(solution)/shard_map/ppermute | solution.py:378
  (4 other events, 46.9 us)
